TPU v7x, 1024 devices: a whole 8x8x8 slice. The times are simulated.
1024 devices in a mesh: section: 8 (over x_lo, core), expert: 16 (over z, x_hi), dp: 8 (over y).
Axes of the slice: x: 8 (x_hi: 2, x_lo: 4; x = x_hi * 4 + x_lo), y: 8, z: 8, core: 2. Of those that a mesh axis runs over, the one named last changes fastest.
Arguments:
- falling_grad: bfloat16 [8, 1024, 7168], P('section', 'expert', 'dp'), may hold values from -6 to 6
- rising_grad: bfloat16 [8, 1024, 7168], P('section', 'expert', 'dp'), may hold values from -6 to 6
- routes_falling: int32 [8, 1024, 8], P('section', 'expert'), may hold values from 0 to 15, all different within a row; in each aligned block of 64 rows (0 to 63, 64 to 127, ..., all dimensions but the last counted through in order) at most 40 rows name the same one
- routes_rising: int32 [8, 1024, 8], P('section', 'expert'), may hold values from 0 to 15, all different within a row; in each aligned block of 64 rows (0 to 63, 64 to 127, ..., all dimensions but the last counted through in order) at most 40 rows name the same one
- scores_falling: float32 [8, 1024, 8], P('section', 'expert'), may hold values from 0.05 to 0.95
- scores_rising: float32 [8, 1024, 8], P('section', 'expert'), may hold values from 0.05 to 0.95
- down_weight: bfloat16 [8, 16, 1024, 7168], P('section', 'expert', None, 'dp'), may hold values from -0.1875 to 0.1875
- saved_falling: bfloat16 [8, 1024, 16, 640], P('section', 'dp', 'expert'), may hold values from -0.29882812 to 0.29882812
- saved_rising: bfloat16 [8, 1024, 16, 640], P('section', 'dp', 'expert'), may hold values from -0.29882812 to 0.29882812
Outputs:
- hidden_falling: bfloat16 [8, 1024, 16, 640], P('section', 'dp', 'expert')
- hidden_rising: bfloat16 [8, 1024, 16, 640], P('section', 'dp', 'expert')
- logits_falling: float32 [8, 1024, 8], P('section', 'expert')
- logits_rising: float32 [8, 1024, 8], P('section', 'expert')
Inputs may be any that keep to these rules, and one draw needn't show every extreme that they name: `routes_falling`: A token names 8 different experts; in each aligned block of 64 tokens (the tokens of one section and one index of expert) no expert is named by more than 40 tokens, and in some blocks one expert by exactly 40. `routes_rising`: A token names 8 different experts; in each aligned block of 64 tokens (the tokens of one section and one index of expert) no expert is named by more than 40 tokens, and in some blocks one expert by exactly 40.
All inputs are finite; a program needn't handle non-finite values.
Results may differ from a plain program's by a relative error of at most 0.019.
Values may be sent and summed in bfloat16 or wider, within the bound.
No kernel may reach another device: no remote copies, remote signals or barrier semaphores. Data moves between devices by JAX's collectives and lax.ppermute only.
A program may use at most 32 MiB of HBM per device.

v0:
```python
import jax
import jax.numpy as jnp
from jax import lax
from jax.sharding import PartitionSpec as P

route_scale = 2.5


def padded(block, sides, width):
    for axis, dim in sides:
        count = lax.axis_size(axis)
        forward = [(i, i + 1) for i in range(count - 1)]
        forward.append((count - 1, 0))
        backward = [(target, source) for source, target in forward]
        low = lax.ppermute(
            lax.slice_in_dim(block, block.shape[dim] - width, None, axis=dim), axis, forward
        )
        high = lax.ppermute(lax.slice_in_dim(block, 0, width, axis=dim), axis, backward)
        block = jnp.concatenate([low, block, high], axis=dim)
    return block


def placements(routes, experts, capacity):
    route_ids = routes[0]
    token_count, rank_count = route_ids.shape
    flat_ids = route_ids.reshape(token_count * rank_count)
    expert_hot = (flat_ids[:, None] == jnp.arange(experts, dtype=jnp.int32)[None, :]).astype(
        jnp.int32
    )
    earlier = jnp.cumsum(expert_hot, axis=0) - expert_hot
    position = jnp.sum(earlier * expert_hot, axis=1)
    slot_hot = (position[:, None] == jnp.arange(capacity, dtype=jnp.int32)[None, :]).astype(
        jnp.int32
    )
    placed = expert_hot[:, :, None] * slot_hot[:, None, :]
    return placed.reshape(token_count, rank_count, experts * capacity).astype(jnp.float32)


def outgoing(arriving, placed, scores, groups, capacity):
    score_total = jnp.sum(scores[0], axis=1, keepdims=True)
    gate_values = route_scale * scores[0] / score_total
    token_place = jnp.sum(placed, axis=1).astype(jnp.bfloat16)
    slot_rows = jnp.einsum(
        "ts,td->sd", token_place, arriving, preferred_element_type=jnp.float32
    ).astype(jnp.bfloat16)
    slot_gate = jnp.sum(placed * gate_values[:, :, None], axis=(0, 1)).astype(jnp.bfloat16)
    feature_count = arriving.shape[1]
    return (
        slot_rows.reshape(groups, -1, capacity, feature_count),
        slot_gate.reshape(groups, -1, capacity),
        score_total,
    )


def expert_side(hidden_terms, gates_in, saved_acts):
    groups, local_count, capacity = gates_in.shape
    gate_cols = (
        jnp.transpose(gates_in, (1, 0, 2))
        .reshape(local_count, groups * capacity)
        .astype(jnp.float32)
    )
    hidden = (gate_cols[None] * hidden_terms).astype(jnp.bfloat16)
    slot_part = jnp.sum(hidden_terms * saved_acts[0].astype(jnp.float32), axis=0)
    return (hidden[None], slot_part)


def homeward(slot_grad, groups, capacity):
    local_count = slot_grad.shape[0]
    return jnp.transpose(slot_grad.reshape(local_count, groups, capacity), (1, 0, 2))


def logit_grads(returned, placed, scores, score_total):
    route_grad = jnp.sum(placed * returned.reshape(1, 1, -1), axis=2)
    chosen = scores[0]
    weighted_mean = jnp.sum(route_grad * chosen, axis=1, keepdims=True) / score_total
    return (route_scale / score_total * (route_grad - weighted_mean) * chosen * (1.0 - chosen))[
        None
    ]


def shards(
    falling_grad,
    rising_grad,
    routes_falling,
    routes_rising,
    scores_falling,
    scores_rising,
    down_weight,
    saved_falling,
    saved_rising,
):
    groups = lax.axis_size("expert")
    local_count = down_weight.shape[1]
    experts = local_count * groups
    capacity = saved_falling.shape[3] // groups
    ff_shard = saved_falling.shape[1]
    weight = down_weight[0]
    stacked_grads = jnp.concatenate([falling_grad, rising_grad], axis=0)
    bordered = padded(stacked_grads, (("section", 0),), 1)
    placed_falling = placements(routes_falling, experts, capacity)
    placed_rising = placements(routes_rising, experts, capacity)
    rows_falling, gate_falling, total_falling = outgoing(
        bordered[3], placed_falling, scores_falling, groups, capacity
    )
    rows_rising, gate_rising, total_rising = outgoing(
        bordered[0], placed_rising, scores_rising, groups, capacity
    )

    def single_pass(slot_rows, slot_gate, saved_acts):
        rows_in, gates_in = (
            lax.all_to_all(slot_rows, "expert", split_axis=0, concat_axis=0, tiled=True),
            lax.all_to_all(slot_gate, "expert", split_axis=0, concat_axis=0, tiled=True),
        )
        product = jnp.einsum("jecd,efd->fejc", rows_in, weight, preferred_element_type=jnp.float32)
        hidden_terms = lax.psum_scatter(
            product.reshape(ff_shard * lax.axis_size("dp"), local_count, groups * capacity).astype(
                jnp.bfloat16
            ),
            "dp",
            scatter_dimension=0,
            tiled=True,
        ).astype(jnp.float32)
        hidden, slot_part = expert_side(hidden_terms, gates_in, saved_acts)
        summed = lax.psum(slot_part, "dp")
        returned = lax.all_to_all(
            homeward(summed, groups, capacity), "expert", split_axis=0, concat_axis=0, tiled=True
        )
        return (hidden, returned)

    hidden_falling, returned_falling = single_pass(rows_falling, gate_falling, saved_falling)
    hidden_rising, returned_rising = single_pass(rows_rising, gate_rising, saved_rising)
    logits_falling = logit_grads(returned_falling, placed_falling, scores_falling, total_falling)
    logits_rising = logit_grads(returned_rising, placed_rising, scores_rising, total_rising)
    return (hidden_falling, hidden_rising, logits_falling, logits_rising)


def solution(mesh):
    in_specs = (
        P("section", "expert", "dp"),
        P("section", "expert", "dp"),
        P("section", "expert", None),
        P("section", "expert", None),
        P("section", "expert", None),
        P("section", "expert", None),
        P("section", "expert", None, "dp"),
        P("section", "dp", "expert", None),
        P("section", "dp", "expert", None),
    )
    out_specs = (
        P("section", "dp", "expert", None),
        P("section", "dp", "expert", None),
        P("section", "expert", None),
        P("section", "expert", None),
    )
    return jax.shard_map(shards, mesh=mesh, in_specs=in_specs, out_specs=out_specs, check_vma=False)
```

profile of v0, /device:TPU:2, one launch (start us, length us, event | category | flops | bytes accessed | tf_op | source)
XLA Modules:
  0.0 308.8 jit_solution(11888221590359710933)
XLA Ops:
  7.2 2.1 collective-permute-start.1
  12.7 4.5 %multiply_convert_fusion = f32[512,16,40]{2,1,0:T(8,128)} fusion(s32[512,40]{1,0:T(8,128)S(1)} %fusion.21, s32[512,16]{1,0:T(8,128)S(1)} %copy.103), kind=kLoop, calls=%fused_computation.3 | loop fusion | flops 655360 | bytes 1425408 | tf_op jit(solution)/shard_map/convert_element_type | solution.py:36
  17.2 3.8 %convert_element_type.196 = f32[64,8,640]{2,1,0:T(8,128)S(1)} reshape(f32[512,16,40]{2,1,0:T(8,128)} %multiply_convert_fusion) | data formatting | bytes 2621440 | tf_op jit(solution)/shard_map/convert_element_type | solution.py:36
  21.4 2.4 convolution_convert_fusion
  23.8 20.9 %all-to-all-start.3 = ((bf16[16,1,40,896]{3,2,1,0:T(8,128)(2,1)}), bf16[16,1,40,896]{3,2,1,0:T(8,128)(2,1)}, u32[]{:S(2)}, u32[]{:S(2)}) async-start(bf16[16,1,40,896]{3,2,1,0:T(8,128)(2,1)} %bitcast.14), calls=%async_computation.3 | async-start | bytes 2293760 | tf_op jit(solution)/shard_map/all_to_all | solution.py:111
  44.7 3.4 %collective-permute-start = (bf16[1,64,896]{2,1,0:T(8,128)(2,1)}, bf16[1,64,896]{2,1,0:T(8,128)(2,1)}, u32[]{:S(2)}, u32[]{:S(2)}) collective-permute-start(bf16[1,64,896]{2,1,0:T(8,128)(2,1)} %param.9), channel_id=1, source_target_pairs={{128,0},{256,128},{384,256},{512,384},{640,512},{768,640},{896,768... | collective-permute-start | bytes 344072 | tf_op jit(solution)/shard_map/ppermute | solution.py:18
  51.3 4.5 %multiply_convert_fusion.1 = f32[512,16,40]{2,1,0:T(8,128)} fusion(s32[512,40]{1,0:T(8,128)S(1)} %fusion.20, s32[512,16]{1,0:T(8,128)S(1)} %copy.96), kind=kLoop, calls=%fused_computation.5 | loop fusion | flops 655360 | bytes 1425408 | tf_op jit(solution)/shard_map/convert_element_type | solution.py:36
  55.8 3.8 %convert_element_type.180 = f32[64,8,640]{2,1,0:T(8,128)S(1)} reshape(f32[512,16,40]{2,1,0:T(8,128)} %multiply_convert_fusion.1) | data formatting | bytes 2621440 | tf_op jit(solution)/shard_map/convert_element_type | solution.py:36
  60.0 30.1 %all-to-all-done.3 = bf16[16,1,40,896]{3,2,1,0:T(8,128)(2,1)} async-done(((bf16[16,1,40,896]{3,2,1,0:T(8,128)(2,1)}), bf16[16,1,40,896]{3,2,1,0:T(8,128)(2,1)}, u32[]{:S(2)}, u32[]{:S(2)}) %all-to-all-start.3) | async-done | bytes 1146912 | tf_op jit(solution)/shard_map/all_to_all | solution.py:111
  90.1 2.8 fusion.10
  95.9 37.3 %all_to_all.30 = bf16[16,1,40,896]{3,2,1,0:T(8,128)(2,1)S(1)} all-to-all(bf16[16,1,40,896]{3,2,1,0:T(8,128)(2,1)S(1)} %bitcast.115), channel_id=1, replica_groups=mesh['section'=8,'expert'=16,'dp'=8] {'expert'}, dimensions={0} | all-to-all | bytes 2293760 | tf_op jit(solution)/shard_map/all_to_all | solution.py:111
  133.2 1.6 fusion.13
  139.8 43.0 %reduce-scatter.7.cloned.1.call-done = bf16[128,640]{1,0:T(8,128)(2,1)} async-done(((bf16[1024,640]{1,0:T(8,128)(2,1)}), bf16[128,640]{1,0:T(8,128)(2,1)}) %reduce-scatter.7.cloned.1.call-update) | async-done | bytes 163856
  184.2 29.1 %all-reduce = (f32[16,1,40]{2,1,0:T(1,128)}, f32[16,1,40]{2,1,0:T(1,128)}) all-reduce(f32[16,1,40]{2,1,0:T(1,128)S(1)} %transpose_reshape.6, f32[16,1,40]{2,1,0:T(1,128)S(1)} %transpose_reshape.7), channel_id=1, replica_groups=mesh['section'=8,'expert'=16,'dp'=8] {'dp'}, use_global_device_ids=true, to_apply=%region_15.16 | all-reduce | flops 1280 | bytes 10240 | tf_op jit(solution)/shard_map/psum | solution.py:124
  213.3 12.1 %all-to-all-start.5 = ((f32[16,1,40]{2,1,0:T(1,128)}), f32[16,1,40]{2,1,0:T(1,128)S(1)}, u32[]{:S(2)}, u32[]{:S(2)}) async-start(f32[16,1,40]{2,1,0:T(1,128)} %get-tuple-element.29), calls=%async_computation.5 | async-start | bytes 16384 | tf_op jit(solution)/shard_map/all_to_all | solution.py:125
  226.4 11.4 %all-to-all-done.5 = f32[16,1,40]{2,1,0:T(1,128)S(1)} async-done(((f32[16,1,40]{2,1,0:T(1,128)}), f32[16,1,40]{2,1,0:T(1,128)S(1)}, u32[]{:S(2)}, u32[]{:S(2)}) %all-to-all-start.5) | async-done | bytes 2592 | tf_op jit(solution)/shard_map/all_to_all | solution.py:125
  237.8 3.7 %all-to-all-start.4 = ((f32[16,1,40]{2,1,0:T(1,128)}), f32[16,1,40]{2,1,0:T(1,128)S(1)}, u32[]{:S(2)}, u32[]{:S(2)}) async-start(f32[16,1,40]{2,1,0:T(1,128)} %get-tuple-element.28), calls=%async_computation.4 | async-start | bytes 16384 | tf_op jit(solution)/shard_map/all_to_all | solution.py:125
  241.5 9.0 %multiply_reduce_fusion = (f32[512]{0:T(512)S(1)}, bf16[16,40]{1,0:T(8,128)(2,1)S(1)}) fusion(f32[16,40]{1,0:T(8,128)S(1)} %bitcast.117, s32[512,40]{1,0:T(8,128)S(1)} %fusion.21, s32[512,16]{1,0:T(8,128)S(1)} %copy-done.2, f32[512]{0:T(512)S(1)} %div.65), kind=kLoop, calls=%fused_computation | loop fusion | flops 1964928 | bytes 122624 | tf_op jit(solution)/shard_map/reduce_sum | solution.py:73
  250.7 2.8 all-to-all-done.4
  253.6 9.0 %multiply_reduce_fusion.1 = (f32[512]{0:T(512)S(1)}, bf16[16,40]{1,0:T(8,128)(2,1)S(1)}) fusion(f32[16,40]{1,0:T(8,128)S(1)} %bitcast.118, s32[512,40]{1,0:T(8,128)S(1)} %copy-done.6, s32[512,16]{1,0:T(8,128)S(1)} %copy-done.4, f32[512]{0:T(512)S(1)} %div.62), kind=kLoop, calls=%fused_computation.1 | loop fusion | flops 1964928 | bytes 122624 | tf_op jit(solution)/shard_map/reduce_sum | solution.py:73
  263.8 9.0 %all-to-all-start.2 = ((bf16[16,1,40]{2,1,0:T(2,128)(2,1)}), bf16[16,1,40]{2,1,0:T(2,128)(2,1)S(1)}, u32[]{:S(2)}, u32[]{:S(2)}) async-start(bf16[16,1,40]{2,1,0:T(2,128)(2,1)} %copy.107), calls=%async_computation.2 | async-start | bytes 16384 | tf_op jit(solution)/shard_map/all_to_all | solution.py:112
  274.6 10.5 %all-to-all-done.2 = bf16[16,1,40]{2,1,0:T(2,128)(2,1)S(1)} async-done(((bf16[16,1,40]{2,1,0:T(2,128)(2,1)}), bf16[16,1,40]{2,1,0:T(2,128)(2,1)S(1)}, u32[]{:S(2)}, u32[]{:S(2)}) %all-to-all-start.2) | async-done | bytes 1312 | tf_op jit(solution)/shard_map/all_to_all | solution.py:112
  285.1 3.5 %all-to-all-start = ((bf16[16,1,40]{2,1,0:T(2,128)(2,1)}), bf16[16,1,40]{2,1,0:T(2,128)(2,1)S(1)}, u32[]{:S(2)}, u32[]{:S(2)}) async-start(bf16[16,1,40]{2,1,0:T(2,128)(2,1)} %copy.100), calls=%async_computation | async-start | bytes 16384 | tf_op jit(solution)/shard_map/all_to_all | solution.py:112
  289.7 11.2 %all-to-all-done = bf16[16,1,40]{2,1,0:T(2,128)(2,1)S(1)} async-done(((bf16[16,1,40]{2,1,0:T(2,128)(2,1)}), bf16[16,1,40]{2,1,0:T(2,128)(2,1)S(1)}, u32[]{:S(2)}, u32[]{:S(2)}) %all-to-all-start) | async-done | bytes 1312 | tf_op jit(solution)/shard_map/all_to_all | solution.py:112
  (99 shorter events, 22.8 us)
Async XLA Ops:
  7.2 82.9 %copy-start = (bf16[1,1,1024,896]{3,2,1,0:T(8,128)(2,1)S(1)}, bf16[1,1,1024,896]{3,2,1,0:T(8,128)(2,1)}, u32[]{:S(2)}) copy-start(bf16[1,1,1024,896]{3,2,1,0:T(8,128)(2,1)} %param.15) | copy-start | bytes 5505028
  7.2 14.2 %collective-permute-start.1 = (bf16[1,64,896]{2,1,0:T(8,128)(2,1)}, bf16[1,64,896]{2,1,0:T(8,128)(2,1)}, u32[]{:S(2)}, u32[]{:S(2)}) collective-permute-start(bf16[1,64,896]{2,1,0:T(8,128)(2,1)} %param.10), channel_id=1, source_target_pairs={{0,128},{128,256},{256,384},{384,512},{512,640},{640,768},{768,896... | collective-permute-start | bytes 344072 | tf_op jit(solution)/shard_map/ppermute | solution.py:15
  12.0 0.7 copy-start.1
  21.1 27.0 %copy-start.9 = (s32[1,64,8]{1,2,0:T(8,128)S(1)}, s32[1,64,8]{1,2,0:T(8,128)}, u32[]{:S(2)}) copy-start(s32[1,64,8]{1,2,0:T(8,128)} %param.11) | copy-start | bytes 6148
  23.8 66.3 %all-to-all-start.3 = ((bf16[16,1,40,896]{3,2,1,0:T(8,128)(2,1)}), bf16[16,1,40,896]{3,2,1,0:T(8,128)(2,1)}, u32[]{:S(2)}, u32[]{:S(2)}) async-start(bf16[16,1,40,896]{3,2,1,0:T(8,128)(2,1)} %bitcast.14), calls=%async_computation.3 | async-start | bytes 2293760 | tf_op jit(solution)/shard_map/all_to_all | solution.py:111
  44.7 93.8 %reduce-scatter.9.cloned.1.call-start = ((), (), s32[]{:S(2)}) async-start(), calls=%async_computation.9 | async-start | bytes 1474560
  44.7 49.7 %collective-permute-start = (bf16[1,64,896]{2,1,0:T(8,128)(2,1)}, bf16[1,64,896]{2,1,0:T(8,128)(2,1)}, u32[]{:S(2)}, u32[]{:S(2)}) collective-permute-start(bf16[1,64,896]{2,1,0:T(8,128)(2,1)} %param.9), channel_id=1, source_target_pairs={{128,0},{256,128},{384,256},{512,384},{640,512},{768,640},{896,768... | collective-permute-start | bytes 344072 | tf_op jit(solution)/shard_map/ppermute | solution.py:18
  49.9 0.7 copy-start.3
  50.6 0.7 copy-start.5
  94.4 88.5 %reduce-scatter.7.cloned.1.call-start = ((), (), s32[]{:S(2)}) async-start(), calls=%async_computation.8 | async-start | bytes 1474560
  136.2 89.3 %copy-start.7 = (f32[1,64,8]{1,2,0:T(8,128)S(1)}, f32[1,64,8]{1,2,0:T(8,128)}, u32[]{:S(2)}) copy-start(f32[1,64,8]{1,2,0:T(8,128)} %param.14) | copy-start | bytes 6148
  136.2 89.3 %copy-start.8 = (f32[1,64,8]{1,2,0:T(8,128)S(1)}, f32[1,64,8]{1,2,0:T(8,128)}, u32[]{:S(2)}) copy-start(f32[1,64,8]{1,2,0:T(8,128)} %param.13) | copy-start | bytes 6148
  136.2 105.3 %copy-start.2 = (s32[512,16]{1,0:T(8,128)S(1)}, s32[512,16]{1,0:T(8,128)}, u32[]{:S(2)}) copy-start(s32[512,16]{1,0:T(8,128)} %copy-done.1) | copy-start | bytes 98308
  136.2 117.4 %copy-start.4 = (s32[512,16]{1,0:T(8,128)S(1)}, s32[512,16]{1,0:T(8,128)}, u32[]{:S(2)}) copy-start(s32[512,16]{1,0:T(8,128)} %copy-done.3) | copy-start | bytes 98308
  136.2 117.4 %copy-start.6 = (s32[512,40]{1,0:T(8,128)S(1)}, s32[512,40]{1,0:T(8,128)}, u32[]{:S(2)}) copy-start(s32[512,40]{1,0:T(8,128)} %copy-done.5) | copy-start | bytes 245764
  213.3 24.5 %all-to-all-start.5 = ((f32[16,1,40]{2,1,0:T(1,128)}), f32[16,1,40]{2,1,0:T(1,128)S(1)}, u32[]{:S(2)}, u32[]{:S(2)}) async-start(f32[16,1,40]{2,1,0:T(1,128)} %get-tuple-element.29), calls=%async_computation.5 | async-start | bytes 16384 | tf_op jit(solution)/shard_map/all_to_all | solution.py:125
  237.8 15.7 %all-to-all-start.4 = ((f32[16,1,40]{2,1,0:T(1,128)}), f32[16,1,40]{2,1,0:T(1,128)S(1)}, u32[]{:S(2)}, u32[]{:S(2)}) async-start(f32[16,1,40]{2,1,0:T(1,128)} %get-tuple-element.28), calls=%async_computation.4 | async-start | bytes 16384 | tf_op jit(solution)/shard_map/all_to_all | solution.py:125
  263.8 21.3 %all-to-all-start.2 = ((bf16[16,1,40]{2,1,0:T(2,128)(2,1)}), bf16[16,1,40]{2,1,0:T(2,128)(2,1)S(1)}, u32[]{:S(2)}, u32[]{:S(2)}) async-start(bf16[16,1,40]{2,1,0:T(2,128)(2,1)} %copy.107), calls=%async_computation.2 | async-start | bytes 16384 | tf_op jit(solution)/shard_map/all_to_all | solution.py:112
  285.1 15.7 %all-to-all-start = ((bf16[16,1,40]{2,1,0:T(2,128)(2,1)}), bf16[16,1,40]{2,1,0:T(2,128)(2,1)S(1)}, u32[]{:S(2)}, u32[]{:S(2)}) async-start(bf16[16,1,40]{2,1,0:T(2,128)(2,1)} %copy.100), calls=%async_computation | async-start | bytes 16384 | tf_op jit(solution)/shard_map/all_to_all | solution.py:112
Sparse Core Ops, SparseCore 0:
  94.5 40.9 reduce-scatter.8
  138.9 43.8 reduce-scatter.6
where the time goes:
time: 310 us; the launch traced here: 309 us
  waiting for transfers between devices  109 us (35%)
  blocking collectives  66.4 us (21%)
  starting transfers between devices  54.6 us (18%)
  other arithmetic  32.8 us (11%)
  local copies, waits for them, and re-layouts  23.3 us (8%)
  between operations  14.5 us (5%)
  matrix products  8.15 us (3%)
    unnamed x4, waiting for transfers between devices  43.1 us
    all_to_all x1, blocking collectives, single_pass(): lax.all_to_all(slot_rows, 'expert', split_axis=0, concat_axis=0, tiled=True)  37.3 us
    all_to_all x1, waiting for transfers between devices, single_pass(): lax.all_to_all(slot_rows, 'expert', split_axis=0, concat_axis=0, tiled=True)  30.1 us
    psum x1, blocking collectives, single_pass(): summed = lax.psum(slot_part, 'dp')  29.1 us
    all_to_all x2, waiting for transfers between devices, single_pass(): lax.all_to_all(slot_gate, 'expert', split_axis=0, concat_axis=0, tiled=True)  21.7 us
    all_to_all x1, starting transfers between devices, single_pass(): lax.all_to_all(slot_rows, 'expert', split_axis=0, concat_axis=0, tiled=True)  20.9 us
    reduce_sum x2, other arithmetic, logit_grads(): route_grad = jnp.sum(placed * returned.reshape(1, 1, -1), axis=2)  18 us
    all_to_all x2, starting transfers between devices, single_pass(): lax.all_to_all(homeward(summed, groups, capacity), 'expert', split_axis=0...  15.8 us
  transfers between devices with their start and end apart: 9, of which 6 were waited for; matrix products, arithmetic and copies ran while one was open for 15% of the time, Pallas kernels for 0%

commit v1 on v0

v1 whole, which is shorter than its diff:
```python
import functools

import jax
import jax.numpy as jnp
from jax import lax
from jax.experimental import pallas as pl
from jax.experimental.pallas import tpu as pltpu
from jax.sharding import PartitionSpec as P

route_scale = 2.5
META = 8
NT = (((1,), (1,)), ((), ()))
f32 = jnp.float32
bf16 = jnp.bfloat16


def pack_kernel(rf, sf, rr, sr, out, buf):
    top, tok = rf.shape
    buf[...] = jnp.zeros_like(buf)
    for m, (routes, scores) in enumerate(((rf, sf), (rr, sr))):
        ids = routes[...].astype(f32)
        s = scores[...]
        gate = route_scale * s / jnp.sum(s, axis=0, keepdims=True)
        for k in range(top):
            buf[2 * m : 2 * m + 1, k * tok : (k + 1) * tok] = ids[k : k + 1]
            buf[2 * m + 1 : 2 * m + 2, k * tok : (k + 1) * tok] = gate[k : k + 1]
    out[...] = buf[...].astype(out.dtype)


def expert_kernel(blocks, tok, top, cap, info, *refs):
    msgs = refs[:blocks]
    w_ref, saved_ref, part_ref, slot_ref, gate_ref = refs[blocks : blocks + 5]
    rows, rows16, gcol, meta = refs[blocks + 5 :]
    slots = blocks * cap
    lanes = 2 * tok

    @pl.when(pl.program_id(0) == 0)
    def _():
        slot_ref[...] = jnp.zeros_like(slot_ref)
        for b in range(blocks):
            meta[b * META : (b + 1) * META, :] = msgs[b][lanes : lanes + META, : top * tok].astype(f32)
        vals = meta[...]
        mine = (vals == info[0].astype(f32)).astype(f32)
        t_in = lax.rem(lax.broadcasted_iota(jnp.int32, (top * tok, lanes), 0), tok)
        t_out = lax.rem(lax.broadcasted_iota(jnp.int32, (top * tok, lanes), 1), tok)
        same = (t_in == t_out).astype(f32).astype(bf16)
        before = (t_in < t_out).astype(f32).astype(bf16)
        hot = mine.astype(bf16)
        named = jnp.dot(hot, same, preferred_element_type=f32)
        place = jnp.dot(hot, before, preferred_element_type=f32)
        picked = (pltpu.roll(mine, 1, 0) * vals).astype(bf16)
        gates = jnp.dot(picked, same, preferred_element_type=f32)
        rising = lax.broadcasted_iota(jnp.int32, (1, lanes), 1) >= tok
        shift = jnp.where(rising, float(cap), 0.0)
        slot_id = lax.broadcasted_iota(jnp.int32, (2 * cap, lanes), 0).astype(f32)
        for b in range(blocks):
            r = b * META
            name = jnp.where(rising, named[r + 2 : r + 3], named[r : r + 1])
            pos = jnp.where(rising, place[r + 2 : r + 3], place[r : r + 1])
            gate = jnp.where(rising, gates[r + 3 : r + 4], gates[r + 1 : r + 2])
            target = jnp.where(name > 0.5, pos + shift, -1.0)
            put = (slot_id == target).astype(f32)
            got = jnp.dot(put.astype(bf16), msgs[b][:lanes, :], preferred_element_type=f32)
            col = jnp.broadcast_to(jnp.sum(put * gate, axis=1, keepdims=True), (2 * cap, gcol.shape[2]))
            at = pl.ds(pl.multiple_of(info[1 + b] * cap, 8), cap)
            for m in range(2):
                rows[m, at, :] = got[m * cap : (m + 1) * cap]
                gcol[m, at, :] = col[m * cap : (m + 1) * cap]
        first = (lax.broadcasted_iota(jnp.int32, (8, gcol.shape[2]), 1) == 0).astype(f32).astype(bf16)
        for m in range(2):
            rows16[m] = rows[m].astype(bf16)
            gate_ref[:, m * slots : (m + 1) * slots] = lax.dot_general(
                first, gcol[m].astype(bf16), NT, preferred_element_type=f32
            )

    w = w_ref[...]
    for m in range(2):
        cols = slice(m * slots, (m + 1) * slots)
        part = lax.dot_general(w, rows16[m], NT, preferred_element_type=f32).astype(bf16)
        part_ref[:, cols] = part
        prod = part.astype(f32) * saved_ref[:, cols].astype(f32)
        slot_ref[:, cols] += jnp.sum(prod.reshape(-1, 8, slots), axis=0)


def logits_kernel(cap, rf, sf, rr, sr, back, out_f, out_r, grad):
    top, tok = rf.shape
    experts = back.shape[0]
    ids = lax.broadcasted_iota(jnp.int32, (experts, tok), 0)
    t0 = lax.broadcasted_iota(jnp.int32, (tok, tok), 0)
    t1 = lax.broadcasted_iota(jnp.int32, (tok, tok), 1)
    before = (t0 < t1).astype(f32).astype(bf16)
    for m, (routes, scores, out) in enumerate(((rf, sf, out_f), (rr, sr, out_r))):
        named = jnp.zeros((experts, tok), f32)
        for k in range(top):
            named += (routes[k : k + 1, :] == ids).astype(f32)
        place = jnp.dot(named.astype(bf16), before, preferred_element_type=f32)
        vals = jnp.zeros((experts, tok), f32)
        for c in range(cap):
            vals += jnp.where(place == float(c), back[:, m * cap + c : m * cap + c + 1], 0.0)
        for k in range(top):
            chosen = jnp.where(routes[k : k + 1, :] == ids, vals, 0.0)
            grad[k : k + 1, :] = jnp.sum(chosen, axis=0, keepdims=True)
        s = scores[...]
        total = jnp.sum(s, axis=0, keepdims=True)
        mean = jnp.sum(grad[...] * s, axis=0, keepdims=True) / total
        out[...] = route_scale / total * (grad[...] - mean) * s * (1.0 - s)


def shards(
    falling_grad,
    rising_grad,
    routes_falling,
    routes_rising,
    scores_falling,
    scores_rising,
    down_weight,
    saved_falling,
    saved_rising,
):
    blocks = lax.axis_size("expert")
    sections = lax.axis_size("section")
    dp = lax.axis_size("dp")
    tok, width = falling_grad.shape[1:]
    top = routes_falling.shape[2]
    ff_shard, slots = saved_falling.shape[1], saved_falling.shape[3]
    cap = slots // blocks
    ff = ff_shard * dp
    depth = blocks // 2
    lanes = 2 * tok

    side = (
        routes_falling[0].T,
        scores_falling[0].T,
        routes_rising[0].T,
        scores_rising[0].T,
    )
    saved = jnp.concatenate(
        [saved_falling.reshape(ff_shard, slots), saved_rising.reshape(ff_shard, slots)], axis=1
    )
    saved_all = lax.all_gather(saved, "dp", tiled=True)

    def hop(array, by, flip):
        pairs = [
            (s * blocks + e, (s + by) % sections * blocks + (e ^ flip))
            for s in range(sections)
            for e in range(blocks)
        ]
        return lax.ppermute(array, ("section", "expert"), pairs)

    own_f, own_r = hop(falling_grad[0], -1, 0), hop(rising_grad[0], 1, 0)
    far_f, far_r = hop(falling_grad[0], -1, 1), hop(rising_grad[0], 1, 1)
    meta = pl.pallas_call(
        pack_kernel,
        out_shape=jax.ShapeDtypeStruct((META, width), bf16),
        scratch_shapes=[pltpu.VMEM((META, width), f32)],
    )(*side)
    far_meta = hop(meta, 0, 1)
    own = jnp.concatenate([own_f, own_r, meta], axis=0)
    far = jnp.concatenate([far_f, far_r, far_meta], axis=0)

    up = [(i, (i + 2) % blocks) for i in range(blocks)]
    down = [(i, (i - 2) % blocks) for i in range(blocks)]
    me = lax.axis_index("expert")
    level, column = me // 2, me % 2
    msgs, index = [own, far], [me, level * 2 + 1 - column]
    own_up = own_down = own
    far_up = far_down = far
    for t in range(1, depth // 2 + 1):
        own_up = lax.ppermute(own_up, "expert", up)
        msgs.append(own_up)
        index.append((level - t) % depth * 2 + column)
        if t < depth // 2:
            own_down = lax.ppermute(own_down, "expert", down)
            msgs.append(own_down)
            index.append((level + t) % depth * 2 + column)
            far_up = lax.ppermute(far_up, "expert", up)
            msgs.append(far_up)
            index.append((level - t) % depth * 2 + 1 - column)
        far_down = lax.ppermute(far_down, "expert", down)
        msgs.append(far_down)
        index.append((level + t) % depth * 2 + 1 - column)
    info = jnp.stack([me] + index).astype(jnp.int32)

    tile = min(256, ff)
    whole = pl.BlockSpec((lanes + META, width), lambda i: (0, 0))
    partial, slot_part, gates = pl.pallas_call(
        functools.partial(expert_kernel, blocks, tok, top, cap),
        grid=(ff // tile,),
        in_specs=[pl.BlockSpec(memory_space=pltpu.SMEM)]
        + [whole] * blocks
        + [
            pl.BlockSpec((tile, width), lambda i: (i, 0)),
            pl.BlockSpec((tile, 2 * slots), lambda i: (i, 0)),
        ],
        out_specs=[
            pl.BlockSpec((tile, 2 * slots), lambda i: (i, 0)),
            pl.BlockSpec((8, 2 * slots), lambda i: (0, 0)),
            pl.BlockSpec((8, 2 * slots), lambda i: (0, 0)),
        ],
        out_shape=[
            jax.ShapeDtypeStruct((ff, 2 * slots), bf16),
            jax.ShapeDtypeStruct((8, 2 * slots), f32),
            jax.ShapeDtypeStruct((8, 2 * slots), f32),
        ],
        scratch_shapes=[
            pltpu.VMEM((2, slots, width), f32),
            pltpu.VMEM((2, slots, width), bf16),
            pltpu.VMEM((2, slots, 128), f32),
            pltpu.VMEM((blocks * META, top * tok), f32),
        ],
        compiler_params=pltpu.CompilerParams(vmem_limit_bytes=40 * 1024 * 1024),
        cost_estimate=pl.CostEstimate(
            flops=4 * ff * width * slots, bytes_accessed=16 * 1024 * 1024, transcendentals=0
        ),
    )(info, *msgs, down_weight.reshape(ff, width), saved_all)

    terms = lax.psum_scatter(partial, "dp", scatter_dimension=0, tiled=True)
    slot_grad = lax.psum(jnp.sum(slot_part, axis=0), "dp")
    home = jnp.transpose(slot_grad.reshape(2, blocks, cap), (1, 0, 2)).reshape(blocks, 2 * cap)
    back = lax.all_to_all(home, "expert", split_axis=0, concat_axis=0, tiled=True)
    logits = pl.pallas_call(
        functools.partial(logits_kernel, cap),
        out_shape=[jax.ShapeDtypeStruct((top, tok), f32)] * 2,
        scratch_shapes=[pltpu.VMEM((top, tok), f32)],
    )(*side, back)
    scaled = (gates[:1] * terms.astype(f32)).astype(bf16)
    hidden = [scaled[:, m * slots : (m + 1) * slots].reshape(1, ff_shard, 1, slots) for m in range(2)]
    return (*hidden, *(g.T[None] for g in logits))


def solution(mesh):
    in_specs = (
        P("section", "expert", "dp"),
        P("section", "expert", "dp"),
        P("section", "expert", None),
        P("section", "expert", None),
        P("section", "expert", None),
        P("section", "expert", None),
        P("section", "expert", None, "dp"),
        P("section", "dp", "expert", None),
        P("section", "dp", "expert", None),
    )
    out_specs = (
        P("section", "dp", "expert", None),
        P("section", "dp", "expert", None),
        P("section", "expert", None),
        P("section", "expert", None),
    )
    return jax.shard_map(shards, mesh=mesh, in_specs=in_specs, out_specs=out_specs, check_vma=False)
```

time: 310 us -> 167 us (0.54)
  the two profiles are of different devices: /device:TPU:2 before, /device:TPU:4 now
where the time goes in v1:
time: 167 us; the launch traced here: 166 us
  starting transfers between devices  82.5 us (49%)
  waiting for transfers between devices  30.4 us (18%)
  blocking collectives  19.4 us (12%)
  between operations  14.5 us (9%)
  Pallas kernels  10.7 us (6%)
  local copies, waits for them, and re-layouts  4.91 us (3%)
  other arithmetic  3.54 us (2%)
    ppermute x4, starting transfers between devices, shards(): far_down = lax.ppermute(far_down, 'expert', down)  27.2 us
    ppermute x5, starting transfers between devices, hop(): return lax.ppermute(array, ('section', 'expert'), pairs)  19.6 us
    psum x1, blocking collectives, shards(): slot_grad = lax.psum(jnp.sum(slot_part, axis=0), 'dp')  19.4 us
    ppermute x3, starting transfers between devices, shards(): own_down = lax.ppermute(own_down, 'expert', down)  15.4 us
    all_to_all x1, waiting for transfers between devices, shards(): lax.all_to_all(home, 'expert', split_axis=0, concat_axis=0, tiled=True)  12.3 us
    ppermute x4, starting transfers between devices, shards(): own_up = lax.ppermute(own_up, 'expert', up)  9.84 us
    pallas_call x1, Pallas kernels, shards(): pl.pallas_call(functools.partial(expert_kernel, blocks, tok, top, cap), g...  7.49 us
    reduce_scatter x1, waiting for transfers between devices, shards(): terms = lax.psum_scatter(partial, 'dp', scatter_dimension=0, tiled=True)  6.62 us
  transfers between devices with their start and end apart: 22, of which 6 were waited for; matrix products, arithmetic and copies ran while one was open for 1% of the time, Pallas kernels for 2%

profile of v1, /device:TPU:4, one launch (start us, length us, event | category | flops | bytes accessed | tf_op | source)
XLA Modules:
  0.0 165.9 jit_solution(14734099595158439180)
XLA Ops:
  9.0 5.0 %collective-permute-start.2 = (bf16[64,896]{1,0:T(8,128)(2,1)}, bf16[64,896]{1,0:T(8,128)(2,1)S(1)}, u32[]{:S(2)}, u32[]{:S(2)}) collective-permute-start(bf16[64,896]{1,0:T(8,128)(2,1)} %bitcast.59), channel_id=1, source_target_pairs={{0,904},{8,896},{16,920},{24,912},{32,936},{40,928},{48,952},{56,9... | collective-permute-start | bytes 344072 | tf_op jit(solution)/shard_map/ppermute | solution.py:148
  14.1 3.7 %collective-permute-start = (bf16[64,896]{1,0:T(8,128)(2,1)}, bf16[64,896]{1,0:T(8,128)(2,1)S(1)}, u32[]{:S(2)}, u32[]{:S(2)}) collective-permute-start(bf16[64,896]{1,0:T(8,128)(2,1)} %bitcast.60), channel_id=1, source_target_pairs={{0,896},{8,904},{16,912},{24,920},{32,928},{40,936},{48,944},{56,9... | collective-permute-start | bytes 344072 | tf_op jit(solution)/shard_map/ppermute | solution.py:148
  17.7 2.7 %collective-permute-start.3 = (bf16[64,896]{1,0:T(8,128)(2,1)}, bf16[64,896]{1,0:T(8,128)(2,1)S(1)}, u32[]{:S(2)}, u32[]{:S(2)}) collective-permute-start(bf16[64,896]{1,0:T(8,128)(2,1)} %bitcast.61), channel_id=1, source_target_pairs={{0,136},{8,128},{16,152},{24,144},{32,168},{40,160},{48,184},{56,1... | collective-permute-start | bytes 344072 | tf_op jit(solution)/shard_map/ppermute | solution.py:148
  20.5 2.6 %collective-permute-start.1 = (bf16[64,896]{1,0:T(8,128)(2,1)}, bf16[64,896]{1,0:T(8,128)(2,1)S(1)}, u32[]{:S(2)}, u32[]{:S(2)}) collective-permute-start(bf16[64,896]{1,0:T(8,128)(2,1)} %bitcast.62), channel_id=1, source_target_pairs={{0,128},{8,136},{16,144},{24,152},{32,160},{40,168},{48,176},{56,1... | collective-permute-start | bytes 344072 | tf_op jit(solution)/shard_map/ppermute | solution.py:148
  24.5 5.6 %collective-permute-start.4 = (bf16[8,896]{1,0:T(8,128)(2,1)}, bf16[8,896]{1,0:T(8,128)(2,1)S(1)}, u32[]{:S(2)}, u32[]{:S(2)}) collective-permute-start(bf16[8,896]{1,0:T(8,128)(2,1)} %shard_map.120), channel_id=1, source_target_pairs={{0,8},{8,0},{16,24},{24,16},{32,40},{40,32},{48,56},{56,48},{64,72... | collective-permute-start | bytes 43016 | tf_op jit(solution)/shard_map/ppermute | solution.py:148
  30.1 4.2 %collective-permute-done.4 = bf16[8,896]{1,0:T(8,128)(2,1)S(1)} collective-permute-done((bf16[8,896]{1,0:T(8,128)(2,1)}, bf16[8,896]{1,0:T(8,128)(2,1)S(1)}, u32[]{:S(2)}, u32[]{:S(2)}) %collective-permute-start.4) | collective-permute-done | bytes 14368 | tf_op jit(solution)/shard_map/ppermute | solution.py:148
  34.3 17.6 %collective-permute-start.8 = (bf16[136,896]{1,0:T(8,128)(2,1)S(1)}, bf16[136,896]{1,0:T(8,128)(2,1)S(1)}, u32[]{:S(2)}, u32[]{:S(2)}) collective-permute-start(bf16[136,896]{1,0:T(8,128)(2,1)S(1)} %constant_dynamic-update-slice_fusion.refs_1_), channel_id=1, source_target_pairs={{0,112},{8,120},{16,0},{24,8},{32,16},{40,24},{48,32},{56,40},{64,... | collective-permute-start | bytes 731144 | tf_op jit(solution)/shard_map/ppermute | solution.py:179
  52.7 1.9 %collective-permute-start.5 = (bf16[136,896]{1,0:T(8,128)(2,1)S(1)}, bf16[136,896]{1,0:T(8,128)(2,1)S(1)}, u32[]{:S(2)}, u32[]{:S(2)}) collective-permute-start(bf16[136,896]{1,0:T(8,128)(2,1)S(1)} %pad_maximum_fusion.1.refs_0_), channel_id=1, source_target_pairs={{0,16},{8,24},{16,32},{24,40},{32,48},{40,56},{48,64},{56,72},{64,... | collective-permute-start | bytes 731144 | tf_op jit(solution)/shard_map/ppermute | solution.py:169
  54.6 1.9 %collective-permute-start.7 = (bf16[136,896]{1,0:T(8,128)(2,1)S(1)}, bf16[136,896]{1,0:T(8,128)(2,1)S(1)}, u32[]{:S(2)}, u32[]{:S(2)}) collective-permute-start(bf16[136,896]{1,0:T(8,128)(2,1)S(1)} %constant_dynamic-update-slice_fusion.refs_1_), channel_id=1, source_target_pairs={{0,16},{8,24},{16,32},{24,40},{32,48},{40,56},{48,64},{56,72},{64,... | collective-permute-start | bytes 731144 | tf_op jit(solution)/shard_map/ppermute | solution.py:176
  56.5 5.1 %collective-permute-start.6 = (bf16[136,896]{1,0:T(8,128)(2,1)S(1)}, bf16[136,896]{1,0:T(8,128)(2,1)S(1)}, u32[]{:S(2)}, u32[]{:S(2)}) collective-permute-start(bf16[136,896]{1,0:T(8,128)(2,1)S(1)} %pad_maximum_fusion.1.refs_0_), channel_id=1, source_target_pairs={{0,112},{8,120},{16,0},{24,8},{32,16},{40,24},{48,32},{56,40},{64,... | collective-permute-start | bytes 731144 | tf_op jit(solution)/shard_map/ppermute | solution.py:173
  61.7 3.9 %collective-permute-start.12 = (bf16[136,896]{1,0:T(8,128)(2,1)S(1)}, bf16[136,896]{1,0:T(8,128)(2,1)S(1)}, u32[]{:S(2)}, u32[]{:S(2)}) collective-permute-start(bf16[136,896]{1,0:T(8,128)(2,1)S(1)} %collective-permute-done.8.refs_5_), channel_id=1, source_target_pairs={{0,112},{8,120},{16,0},{24,8},{32,16},{40,24},{48,32},{56,40},{64,... | collective-permute-start | bytes 731144 | tf_op jit(solution)/shard_map/ppermute | solution.py:179
  70.6 5.1 %collective-permute-start.10 = (bf16[136,896]{1,0:T(8,128)(2,1)S(1)}, bf16[136,896]{1,0:T(8,128)(2,1)S(1)}, u32[]{:S(2)}, u32[]{:S(2)}) collective-permute-start(bf16[136,896]{1,0:T(8,128)(2,1)S(1)} %collective-permute-done.6.refs_3_), channel_id=1, source_target_pairs={{0,112},{8,120},{16,0},{24,8},{32,16},{40,24},{48,32},{56,40},{64,... | collective-permute-start | bytes 731144 | tf_op jit(solution)/shard_map/ppermute | solution.py:173
  75.7 2.8 %collective-permute-start.16 = (bf16[136,896]{1,0:T(8,128)(2,1)S(1)}, bf16[136,896]{1,0:T(8,128)(2,1)S(1)}, u32[]{:S(2)}, u32[]{:S(2)}) collective-permute-start(bf16[136,896]{1,0:T(8,128)(2,1)S(1)} %collective-permute-done.12.refs_9_), channel_id=1, source_target_pairs={{0,112},{8,120},{16,0},{24,8},{32,16},{40,24},{48,32},{56,40},{64,... | collective-permute-start | bytes 731144 | tf_op jit(solution)/shard_map/ppermute | solution.py:179
  78.6 3.0 %collective-permute-start.13 = (bf16[136,896]{1,0:T(8,128)(2,1)S(1)}, bf16[136,896]{1,0:T(8,128)(2,1)S(1)}, u32[]{:S(2)}, u32[]{:S(2)}) collective-permute-start(bf16[136,896]{1,0:T(8,128)(2,1)S(1)} %collective-permute-done.9.refs_6_), channel_id=1, source_target_pairs={{0,16},{8,24},{16,32},{24,40},{32,48},{40,56},{48,64},{56,72},{64,... | collective-permute-start | bytes 731144 | tf_op jit(solution)/shard_map/ppermute | solution.py:169
  83.6 5.1 %collective-permute-start.14 = (bf16[136,896]{1,0:T(8,128)(2,1)S(1)}, bf16[136,896]{1,0:T(8,128)(2,1)S(1)}, u32[]{:S(2)}, u32[]{:S(2)}) collective-permute-start(bf16[136,896]{1,0:T(8,128)(2,1)S(1)} %collective-permute-done.10.refs_7_), channel_id=1, source_target_pairs={{0,112},{8,120},{16,0},{24,8},{32,16},{40,24},{48,32},{56,40},{64,... | collective-permute-start | bytes 731144 | tf_op jit(solution)/shard_map/ppermute | solution.py:173
  88.7 2.8 %collective-permute-start.18 = (bf16[136,896]{1,0:T(8,128)(2,1)S(1)}, bf16[136,896]{1,0:T(8,128)(2,1)}, u32[]{:S(2)}, u32[]{:S(2)}) collective-permute-start(bf16[136,896]{1,0:T(8,128)(2,1)S(1)} %collective-permute-done.16.refs_13_), channel_id=1, source_target_pairs={{0,112},{8,120},{16,0},{24,8},{32,16},{40,24},{48,32},{56,40},{64,... | collective-permute-start | bytes 731144 | tf_op jit(solution)/shard_map/ppermute | solution.py:179
  91.6 3.0 %collective-permute-start.17 = (bf16[136,896]{1,0:T(8,128)(2,1)S(1)}, bf16[136,896]{1,0:T(8,128)(2,1)}, u32[]{:S(2)}, u32[]{:S(2)}) collective-permute-start(bf16[136,896]{1,0:T(8,128)(2,1)S(1)} %collective-permute-done.13.refs_10_), channel_id=1, source_target_pairs={{0,16},{8,24},{16,32},{24,40},{32,48},{40,56},{48,64},{56,72},{64,... | collective-permute-start | bytes 731144 | tf_op jit(solution)/shard_map/ppermute | solution.py:169
  94.9 2.1 %collective-permute-done.18.refs_15_ = bf16[136,896]{1,0:T(8,128)(2,1)} collective-permute-done((bf16[136,896]{1,0:T(8,128)(2,1)S(1)}, bf16[136,896]{1,0:T(8,128)(2,1)}, u32[]{:S(2)}, u32[]{:S(2)}) %collective-permute-start.18) | collective-permute-done | bytes 243744 | tf_op jit(solution)/shard_map/ppermute | solution.py:179
  97.0 4.0 %collective-permute-done.17.refs_14_ = bf16[136,896]{1,0:T(8,128)(2,1)} collective-permute-done((bf16[136,896]{1,0:T(8,128)(2,1)S(1)}, bf16[136,896]{1,0:T(8,128)(2,1)}, u32[]{:S(2)}, u32[]{:S(2)}) %collective-permute-start.17) | collective-permute-done | bytes 243744 | tf_op jit(solution)/shard_map/ppermute | solution.py:169
  104.2 7.5 %shard_map.121 = (bf16[1024,1280]{1,0:T(8,128)(2,1)}, f32[8,1280]{1,0:T(8,128)S(1)}, f32[8,1280]{1,0:T(8,128)S(1)}) custom-call(s32[17]{0:T(128)S(1)} %stack.68.info, bf16[136,896]{1,0:T(8,128)(2,1)S(1)} %pad_maximum_fusion.1.refs_0_, bf16[136,896]{1,0:T(8,128)(2,1)S(1)} %constant_dynamic-update-slice_fusion.refs_1_, ...), custom_call_target="tpu_custom_call" | custom-call | flops 2348810240 | bytes 16777216 | tf_op jit(solution)/shard_map/pallas_call | solution.py:186
  111.9 19.4 %psum.7 = f32[16,1,80]{2,0,1:T(8,128)} all-reduce(f32[16,1,80]{2,0,1:T(8,128)S(1)} %all_to_all.7), channel_id=1, replica_groups=mesh['section'=8,'expert'=16,'dp'=8] {'dp'}, use_global_device_ids=true, to_apply=%region_2.3 | all-reduce | flops 1280 | bytes 10240 | tf_op jit(solution)/shard_map/psum | solution.py:218
  131.3 4.7 %all-to-all-start = ((f32[16,1,80]{2,1,0:T(1,128)}), f32[16,1,80]{2,1,0:T(1,128)S(1)}, u32[]{:S(2)}, u32[]{:S(2)}) async-start(f32[16,1,80]{2,1,0:T(1,128)} %bitcast.36), calls=%async_computation.1 | async-start | bytes 16384 | tf_op jit(solution)/shard_map/all_to_all | solution.py:220
  136.0 12.3 %all-to-all-done = f32[16,1,80]{2,1,0:T(1,128)S(1)} async-done(((f32[16,1,80]{2,1,0:T(1,128)}), f32[16,1,80]{2,1,0:T(1,128)S(1)}, u32[]{:S(2)}, u32[]{:S(2)}) %all-to-all-start) | async-done | bytes 5152 | tf_op jit(solution)/shard_map/all_to_all | solution.py:220
  150.6 6.6 %reduce-scatter.2.cloned.1.call-done = bf16[128,1280]{1,0:T(8,128)(2,1)} async-done(((bf16[1024,1280]{1,0:T(8,128)(2,1)}), bf16[128,1280]{1,0:T(8,128)(2,1)}) %reduce-scatter.2.cloned.1.call-update) | async-done | bytes 327696 | tf_op jit(solution)/shard_map/reduce_scatter | solution.py:217
  (45 shorter events, 18.6 us)
Async XLA Ops:
  7.2 93.8 %all-gather.2.cloned.1.call-start = ((), (), s32[]{:S(2)}) async-start(), calls=%async_computation.2 | async-start | bytes 2949120 | tf_op jit(solution)/shard_map/all_gather | solution.py:140
  9.0 148.3 %reduce-scatter.2.cloned.1.call-start = ((), (), s32[]{:S(2)}) async-start(), calls=%async_computation.3 | async-start | bytes 2949120 | tf_op jit(solution)/shard_map/reduce_scatter | solution.py:217
  9.0 21.0 %collective-permute-start.2 = (bf16[64,896]{1,0:T(8,128)(2,1)}, bf16[64,896]{1,0:T(8,128)(2,1)S(1)}, u32[]{:S(2)}, u32[]{:S(2)}) collective-permute-start(bf16[64,896]{1,0:T(8,128)(2,1)} %bitcast.59), channel_id=1, source_target_pairs={{0,904},{8,896},{16,920},{24,912},{32,936},{40,928},{48,952},{56,9... | collective-permute-start | bytes 344072 | tf_op jit(solution)/shard_map/ppermute | solution.py:148
  14.1 37.9 %collective-permute-start = (bf16[64,896]{1,0:T(8,128)(2,1)}, bf16[64,896]{1,0:T(8,128)(2,1)S(1)}, u32[]{:S(2)}, u32[]{:S(2)}) collective-permute-start(bf16[64,896]{1,0:T(8,128)(2,1)} %bitcast.60), channel_id=1, source_target_pairs={{0,896},{8,904},{16,912},{24,920},{32,928},{40,936},{48,944},{56,9... | collective-permute-start | bytes 344072 | tf_op jit(solution)/shard_map/ppermute | solution.py:148
  17.7 12.4 %collective-permute-start.3 = (bf16[64,896]{1,0:T(8,128)(2,1)}, bf16[64,896]{1,0:T(8,128)(2,1)S(1)}, u32[]{:S(2)}, u32[]{:S(2)}) collective-permute-start(bf16[64,896]{1,0:T(8,128)(2,1)} %bitcast.61), channel_id=1, source_target_pairs={{0,136},{8,128},{16,152},{24,144},{32,168},{40,160},{48,184},{56,1... | collective-permute-start | bytes 344072 | tf_op jit(solution)/shard_map/ppermute | solution.py:148
  20.5 31.5 %collective-permute-start.1 = (bf16[64,896]{1,0:T(8,128)(2,1)}, bf16[64,896]{1,0:T(8,128)(2,1)S(1)}, u32[]{:S(2)}, u32[]{:S(2)}) collective-permute-start(bf16[64,896]{1,0:T(8,128)(2,1)} %bitcast.62), channel_id=1, source_target_pairs={{0,128},{8,136},{16,144},{24,152},{32,160},{40,168},{48,176},{56,1... | collective-permute-start | bytes 344072 | tf_op jit(solution)/shard_map/ppermute | solution.py:148
  24.5 9.8 %collective-permute-start.4 = (bf16[8,896]{1,0:T(8,128)(2,1)}, bf16[8,896]{1,0:T(8,128)(2,1)S(1)}, u32[]{:S(2)}, u32[]{:S(2)}) collective-permute-start(bf16[8,896]{1,0:T(8,128)(2,1)} %shard_map.120), channel_id=1, source_target_pairs={{0,8},{8,0},{16,24},{24,16},{32,40},{40,32},{48,56},{56,48},{64,72... | collective-permute-start | bytes 43016 | tf_op jit(solution)/shard_map/ppermute | solution.py:148
  34.3 27.3 %collective-permute-start.8 = (bf16[136,896]{1,0:T(8,128)(2,1)S(1)}, bf16[136,896]{1,0:T(8,128)(2,1)S(1)}, u32[]{:S(2)}, u32[]{:S(2)}) collective-permute-start(bf16[136,896]{1,0:T(8,128)(2,1)S(1)} %constant_dynamic-update-slice_fusion.refs_1_), channel_id=1, source_target_pairs={{0,112},{8,120},{16,0},{24,8},{32,16},{40,24},{48,32},{56,40},{64,... | collective-permute-start | bytes 731144 | tf_op jit(solution)/shard_map/ppermute | solution.py:179
  52.7 12.9 %collective-permute-start.5 = (bf16[136,896]{1,0:T(8,128)(2,1)S(1)}, bf16[136,896]{1,0:T(8,128)(2,1)S(1)}, u32[]{:S(2)}, u32[]{:S(2)}) collective-permute-start(bf16[136,896]{1,0:T(8,128)(2,1)S(1)} %pad_maximum_fusion.1.refs_0_), channel_id=1, source_target_pairs={{0,16},{8,24},{16,32},{24,40},{32,48},{40,56},{48,64},{56,72},{64,... | collective-permute-start | bytes 731144 | tf_op jit(solution)/shard_map/ppermute | solution.py:169
  54.6 14.1 %collective-permute-start.7 = (bf16[136,896]{1,0:T(8,128)(2,1)S(1)}, bf16[136,896]{1,0:T(8,128)(2,1)S(1)}, u32[]{:S(2)}, u32[]{:S(2)}) collective-permute-start(bf16[136,896]{1,0:T(8,128)(2,1)S(1)} %constant_dynamic-update-slice_fusion.refs_1_), channel_id=1, source_target_pairs={{0,16},{8,24},{16,32},{24,40},{32,48},{40,56},{48,64},{56,72},{64,... | collective-permute-start | bytes 731144 | tf_op jit(solution)/shard_map/ppermute | solution.py:176
  56.5 14.0 %collective-permute-start.6 = (bf16[136,896]{1,0:T(8,128)(2,1)S(1)}, bf16[136,896]{1,0:T(8,128)(2,1)S(1)}, u32[]{:S(2)}, u32[]{:S(2)}) collective-permute-start(bf16[136,896]{1,0:T(8,128)(2,1)S(1)} %pad_maximum_fusion.1.refs_0_), channel_id=1, source_target_pairs={{0,112},{8,120},{16,0},{24,8},{32,16},{40,24},{48,32},{56,40},{64,... | collective-permute-start | bytes 731144 | tf_op jit(solution)/shard_map/ppermute | solution.py:173
  61.7 14.0 %collective-permute-start.12 = (bf16[136,896]{1,0:T(8,128)(2,1)S(1)}, bf16[136,896]{1,0:T(8,128)(2,1)S(1)}, u32[]{:S(2)}, u32[]{:S(2)}) collective-permute-start(bf16[136,896]{1,0:T(8,128)(2,1)S(1)} %collective-permute-done.8.refs_5_), channel_id=1, source_target_pairs={{0,112},{8,120},{16,0},{24,8},{32,16},{40,24},{48,32},{56,40},{64,... | collective-permute-start | bytes 731144 | tf_op jit(solution)/shard_map/ppermute | solution.py:179
  65.6 13.0 %collective-permute-start.9 = (bf16[136,896]{1,0:T(8,128)(2,1)S(1)}, bf16[136,896]{1,0:T(8,128)(2,1)S(1)}, u32[]{:S(2)}, u32[]{:S(2)}) collective-permute-start(bf16[136,896]{1,0:T(8,128)(2,1)S(1)} %collective-permute-done.5.refs_2_), channel_id=1, source_target_pairs={{0,16},{8,24},{16,32},{24,40},{32,48},{40,56},{48,64},{56,72},{64,... | collective-permute-start | bytes 731144 | tf_op jit(solution)/shard_map/ppermute | solution.py:169
  68.7 12.9 %collective-permute-start.11 = (bf16[136,896]{1,0:T(8,128)(2,1)S(1)}, bf16[136,896]{1,0:T(8,128)(2,1)S(1)}, u32[]{:S(2)}, u32[]{:S(2)}) collective-permute-start(bf16[136,896]{1,0:T(8,128)(2,1)S(1)} %collective-permute-done.7.refs_4_), channel_id=1, source_target_pairs={{0,16},{8,24},{16,32},{24,40},{32,48},{40,56},{48,64},{56,72},{64,... | collective-permute-start | bytes 731144 | tf_op jit(solution)/shard_map/ppermute | solution.py:176
  70.6 13.0 %collective-permute-start.10 = (bf16[136,896]{1,0:T(8,128)(2,1)S(1)}, bf16[136,896]{1,0:T(8,128)(2,1)S(1)}, u32[]{:S(2)}, u32[]{:S(2)}) collective-permute-start(bf16[136,896]{1,0:T(8,128)(2,1)S(1)} %collective-permute-done.6.refs_3_), channel_id=1, source_target_pairs={{0,112},{8,120},{16,0},{24,8},{32,16},{40,24},{48,32},{56,40},{64,... | collective-permute-start | bytes 731144 | tf_op jit(solution)/shard_map/ppermute | solution.py:173
  75.7 13.0 %collective-permute-start.16 = (bf16[136,896]{1,0:T(8,128)(2,1)S(1)}, bf16[136,896]{1,0:T(8,128)(2,1)S(1)}, u32[]{:S(2)}, u32[]{:S(2)}) collective-permute-start(bf16[136,896]{1,0:T(8,128)(2,1)S(1)} %collective-permute-done.12.refs_9_), channel_id=1, source_target_pairs={{0,112},{8,120},{16,0},{24,8},{32,16},{40,24},{48,32},{56,40},{64,... | collective-permute-start | bytes 731144 | tf_op jit(solution)/shard_map/ppermute | solution.py:179
  78.6 13.0 %collective-permute-start.13 = (bf16[136,896]{1,0:T(8,128)(2,1)S(1)}, bf16[136,896]{1,0:T(8,128)(2,1)S(1)}, u32[]{:S(2)}, u32[]{:S(2)}) collective-permute-start(bf16[136,896]{1,0:T(8,128)(2,1)S(1)} %collective-permute-done.9.refs_6_), channel_id=1, source_target_pairs={{0,16},{8,24},{16,32},{24,40},{32,48},{40,56},{48,64},{56,72},{64,... | collective-permute-start | bytes 731144 | tf_op jit(solution)/shard_map/ppermute | solution.py:169
  81.6 13.2 %collective-permute-start.15 = (bf16[136,896]{1,0:T(8,128)(2,1)S(1)}, bf16[136,896]{1,0:T(8,128)(2,1)S(1)}, u32[]{:S(2)}, u32[]{:S(2)}) collective-permute-start(bf16[136,896]{1,0:T(8,128)(2,1)S(1)} %collective-permute-done.11.refs_8_), channel_id=1, source_target_pairs={{0,16},{8,24},{16,32},{24,40},{32,48},{40,56},{48,64},{56,72},{64,... | collective-permute-start | bytes 731144 | tf_op jit(solution)/shard_map/ppermute | solution.py:176
  83.6 11.3 %collective-permute-start.14 = (bf16[136,896]{1,0:T(8,128)(2,1)S(1)}, bf16[136,896]{1,0:T(8,128)(2,1)S(1)}, u32[]{:S(2)}, u32[]{:S(2)}) collective-permute-start(bf16[136,896]{1,0:T(8,128)(2,1)S(1)} %collective-permute-done.10.refs_7_), channel_id=1, source_target_pairs={{0,112},{8,120},{16,0},{24,8},{32,16},{40,24},{48,32},{56,40},{64,... | collective-permute-start | bytes 731144 | tf_op jit(solution)/shard_map/ppermute | solution.py:173
  88.7 8.2 %collective-permute-start.18 = (bf16[136,896]{1,0:T(8,128)(2,1)S(1)}, bf16[136,896]{1,0:T(8,128)(2,1)}, u32[]{:S(2)}, u32[]{:S(2)}) collective-permute-start(bf16[136,896]{1,0:T(8,128)(2,1)S(1)} %collective-permute-done.16.refs_13_), channel_id=1, source_target_pairs={{0,112},{8,120},{16,0},{24,8},{32,16},{40,24},{48,32},{56,40},{64,... | collective-permute-start | bytes 731144 | tf_op jit(solution)/shard_map/ppermute | solution.py:179
  91.6 9.4 %collective-permute-start.17 = (bf16[136,896]{1,0:T(8,128)(2,1)S(1)}, bf16[136,896]{1,0:T(8,128)(2,1)}, u32[]{:S(2)}, u32[]{:S(2)}) collective-permute-start(bf16[136,896]{1,0:T(8,128)(2,1)S(1)} %collective-permute-done.13.refs_10_), channel_id=1, source_target_pairs={{0,16},{8,24},{16,32},{24,40},{32,48},{40,56},{48,64},{56,72},{64,... | collective-permute-start | bytes 731144 | tf_op jit(solution)/shard_map/ppermute | solution.py:169
  101.0 1.7 %copy-start = (bf16[1024,1280]{1,0:T(8,128)(2,1)S(1)}, bf16[1024,1280]{1,0:T(8,128)(2,1)}, u32[]{:S(2)}) copy-start(bf16[1024,1280]{1,0:T(8,128)(2,1)} %all-gather.2.cloned.1.call-done.refs_17_) | copy-start | bytes 7864324
  102.7 1.5 copy-start.1
  131.3 17.0 %all-to-all-start = ((f32[16,1,80]{2,1,0:T(1,128)}), f32[16,1,80]{2,1,0:T(1,128)S(1)}, u32[]{:S(2)}, u32[]{:S(2)}) async-start(f32[16,1,80]{2,1,0:T(1,128)} %bitcast.36), calls=%async_computation.1 | async-start | bytes 16384 | tf_op jit(solution)/shard_map/all_to_all | solution.py:220
  (1 other events, 0.6 us)
Sparse Core Ops, SparseCore 0:
  10.7 58.7 all-gather.1
  111.8 45.3 reduce-scatter.1

commit v2 on v1

v2 whole, which is shorter than its diff:
```python
import functools

import jax
import jax.numpy as jnp
from jax import lax
from jax.experimental import pallas as pl
from jax.experimental.pallas import tpu as pltpu
from jax.sharding import PartitionSpec as P

route_scale = 2.5
META = 8
NT = (((1,), (1,)), ((), ()))
f32 = jnp.float32
bf16 = jnp.bfloat16


def pack_kernel(rf, sf, rr, sr, out, buf):
    top, tok = rf.shape
    buf[...] = jnp.zeros_like(buf)
    for m, (routes, scores) in enumerate(((rf, sf), (rr, sr))):
        ids = routes[...].astype(f32)
        s = scores[...]
        gate = route_scale * s / jnp.sum(s, axis=0, keepdims=True)
        for k in range(top):
            buf[2 * m : 2 * m + 1, k * tok : (k + 1) * tok] = ids[k : k + 1]
            buf[2 * m + 1 : 2 * m + 2, k * tok : (k + 1) * tok] = gate[k : k + 1]
    out[...] = buf[...].astype(out.dtype)


def expert_kernel(blocks, tok, top, cap, info, *refs):
    msgs = refs[:blocks]
    w_hbm, saved_hbm, part_hbm, slot_ref, gate_ref = refs[blocks : blocks + 5]
    rows, rows16, gcol, meta, w_ref, saved_ref, part_ref, w_sem, saved_sem, part_sem = refs[blocks + 5 :]
    slots = blocks * cap
    lanes = 2 * tok
    tiles = w_sem.shape[0]
    tile = w_ref.shape[0] // tiles
    parts = [pl.ds(i * tile, tile) for i in range(tiles)]
    fetched = []
    for i, at in enumerate(parts):
        pair = (
            pltpu.make_async_copy(w_hbm.at[at], w_ref.at[at], w_sem.at[i]),
            pltpu.make_async_copy(saved_hbm.at[at], saved_ref.at[at], saved_sem.at[i]),
        )
        for copy in pair:
            copy.start()
        fetched.append(pair)

    for b in range(blocks):
        meta[b * META : (b + 1) * META, :] = msgs[b][lanes : lanes + META, : top * tok].astype(f32)
    vals = meta[...]
    mine = (vals == info[0].astype(f32)).astype(f32)
    t_in = lax.rem(lax.broadcasted_iota(jnp.int32, (top * tok, lanes), 0), tok)
    t_out = lax.rem(lax.broadcasted_iota(jnp.int32, (top * tok, lanes), 1), tok)
    same = (t_in == t_out).astype(f32).astype(bf16)
    before = (t_in < t_out).astype(f32).astype(bf16)
    hot = mine.astype(bf16)
    named = jnp.dot(hot, same, preferred_element_type=f32)
    place = jnp.dot(hot, before, preferred_element_type=f32)
    picked = (pltpu.roll(mine, 1, 0) * vals).astype(bf16)
    gates = jnp.dot(picked, same, preferred_element_type=f32)
    rising = lax.broadcasted_iota(jnp.int32, (1, lanes), 1) >= tok
    shift = jnp.where(rising, float(cap), 0.0)
    slot_id = lax.broadcasted_iota(jnp.int32, (2 * cap, lanes), 0).astype(f32)
    for b in range(blocks):
        r = b * META
        name = jnp.where(rising, named[r + 2 : r + 3], named[r : r + 1])
        pos = jnp.where(rising, place[r + 2 : r + 3], place[r : r + 1])
        gate = jnp.where(rising, gates[r + 3 : r + 4], gates[r + 1 : r + 2])
        target = jnp.where(name > 0.5, pos + shift, -1.0)
        put = (slot_id == target).astype(f32)
        got = jnp.dot(put.astype(bf16), msgs[b][:lanes, :], preferred_element_type=f32)
        col = jnp.broadcast_to(jnp.sum(put * gate, axis=1, keepdims=True), (2 * cap, gcol.shape[2]))
        at = pl.ds(pl.multiple_of(info[1 + b] * cap, 8), cap)
        for m in range(2):
            rows[m, at, :] = got[m * cap : (m + 1) * cap]
            gcol[m, at, :] = col[m * cap : (m + 1) * cap]
    first = (lax.broadcasted_iota(jnp.int32, (8, gcol.shape[2]), 1) == 0).astype(f32).astype(bf16)
    for m in range(2):
        rows16[m] = rows[m].astype(bf16)
        gate_ref[:, m * slots : (m + 1) * slots] = lax.dot_general(
            first, gcol[m].astype(bf16), NT, preferred_element_type=f32
        )

    sent = []
    for i, at in enumerate(parts):
        for copy in fetched[i]:
            copy.wait()
        w = w_ref[at, :]
        for m in range(2):
            cols = slice(m * slots, (m + 1) * slots)
            part = lax.dot_general(w, rows16[m], NT, preferred_element_type=f32).astype(bf16)
            part_ref[at, cols] = part
            prod = part.astype(f32) * saved_ref[at, cols].astype(f32)
            total = jnp.sum(prod.reshape(-1, 8, slots), axis=0)
            slot_ref[:, cols] = total if i == 0 else slot_ref[:, cols] + total
        copy = pltpu.make_async_copy(part_ref.at[at], part_hbm.at[at], part_sem.at[i])
        copy.start()
        sent.append(copy)
    for copy in sent:
        copy.wait()


def logits_kernel(cap, rf, sf, rr, sr, back, out_f, out_r, grad):
    top, tok = rf.shape
    experts = back.shape[0]
    ids = lax.broadcasted_iota(jnp.int32, (experts, tok), 0)
    t0 = lax.broadcasted_iota(jnp.int32, (tok, tok), 0)
    t1 = lax.broadcasted_iota(jnp.int32, (tok, tok), 1)
    before = (t0 < t1).astype(f32).astype(bf16)
    for m, (routes, scores, out) in enumerate(((rf, sf, out_f), (rr, sr, out_r))):
        named = jnp.zeros((experts, tok), f32)
        for k in range(top):
            named += (routes[k : k + 1, :] == ids).astype(f32)
        place = jnp.dot(named.astype(bf16), before, preferred_element_type=f32)
        vals = jnp.zeros((experts, tok), f32)
        for c in range(cap):
            vals += jnp.where(place == float(c), back[:, m * cap + c : m * cap + c + 1], 0.0)
        for k in range(top):
            chosen = jnp.where(routes[k : k + 1, :] == ids, vals, 0.0)
            grad[k : k + 1, :] = jnp.sum(chosen, axis=0, keepdims=True)
        s = scores[...]
        total = jnp.sum(s, axis=0, keepdims=True)
        mean = jnp.sum(grad[...] * s, axis=0, keepdims=True) / total
        out[...] = route_scale / total * (grad[...] - mean) * s * (1.0 - s)


def shards(
    falling_grad,
    rising_grad,
    routes_falling,
    routes_rising,
    scores_falling,
    scores_rising,
    down_weight,
    saved_falling,
    saved_rising,
):
    blocks = lax.axis_size("expert")
    sections = lax.axis_size("section")
    dp = lax.axis_size("dp")
    tok, width = falling_grad.shape[1:]
    top = routes_falling.shape[2]
    ff_shard, slots = saved_falling.shape[1], saved_falling.shape[3]
    cap = slots // blocks
    ff = ff_shard * dp
    depth = blocks // 2
    lanes = 2 * tok

    side = (
        routes_falling[0].T,
        scores_falling[0].T,
        routes_rising[0].T,
        scores_rising[0].T,
    )
    def hop(array, by, flip):
        pairs = [
            (s * blocks + e, (s + by) % sections * blocks + (e ^ flip))
            for s in range(sections)
            for e in range(blocks)
        ]
        return lax.ppermute(array, ("section", "expert"), pairs)

    own_f, own_r = hop(falling_grad[0], -1, 0), hop(rising_grad[0], 1, 0)
    meta = pl.pallas_call(
        pack_kernel,
        out_shape=jax.ShapeDtypeStruct((META, width), bf16),
        scratch_shapes=[pltpu.VMEM((META, width), f32)],
    )(*side)
    own = jnp.concatenate([own_f, own_r, meta], axis=0)
    far = hop(own, 0, 1)

    saved = jnp.concatenate(
        [saved_falling.reshape(ff_shard, slots), saved_rising.reshape(ff_shard, slots)], axis=1
    )
    own_ring, saved = lax.optimization_barrier((own, saved))
    saved_all = lax.all_gather(saved, "dp", tiled=True)

    up = [(i, (i + 2) % blocks) for i in range(blocks)]
    down = [(i, (i - 2) % blocks) for i in range(blocks)]
    me = lax.axis_index("expert")
    level, column = me // 2, me % 2
    msgs, index = [own, far], [me, level * 2 + 1 - column]

    def step(rise, fall, side, t):
        if rise is not None:
            rise = lax.ppermute(rise, "expert", up)
            msgs.append(rise)
            index.append((level - t) % depth * 2 + side)
        if fall is not None:
            fall = lax.ppermute(fall, "expert", down)
            msgs.append(fall)
            index.append((level + t) % depth * 2 + side)
        return rise, fall

    half = depth // 2
    own_rise = own_fall = own_ring
    for t in range(1, half):
        own_rise, own_fall = step(own_rise, own_fall, column, t)
        if t == 1:
            own_rise, own_fall, far = lax.optimization_barrier((own_rise, own_fall, far))
            msgs[1:] = far, own_rise, own_fall
    step(own_rise, None, column, half)
    far_rise = far_fall = far
    for t in range(1, half):
        far_rise, far_fall = step(far_rise, far_fall, 1 - column, t)
    step(None, far_fall, 1 - column, half)
    info = jnp.stack([me] + index).astype(jnp.int32)

    tiles = max(1, ff // 256)
    vmem, hbm = pl.BlockSpec(memory_space=pltpu.VMEM), pl.BlockSpec(memory_space=pltpu.HBM)
    partial, slot_part, gates = pl.pallas_call(
        functools.partial(expert_kernel, blocks, tok, top, cap),
        in_specs=[pl.BlockSpec(memory_space=pltpu.SMEM)] + [vmem] * blocks + [hbm, hbm],
        out_specs=[hbm, vmem, vmem],
        out_shape=[
            jax.ShapeDtypeStruct((ff, 2 * slots), bf16),
            jax.ShapeDtypeStruct((8, 2 * slots), f32),
            jax.ShapeDtypeStruct((8, 2 * slots), f32),
        ],
        scratch_shapes=[
            pltpu.VMEM((2, slots, width), f32),
            pltpu.VMEM((2, slots, width), bf16),
            pltpu.VMEM((2, slots, 128), f32),
            pltpu.VMEM((blocks * META, top * tok), f32),
            pltpu.VMEM((ff, width), bf16),
            pltpu.VMEM((ff, 2 * slots), bf16),
            pltpu.VMEM((ff, 2 * slots), bf16),
            pltpu.SemaphoreType.DMA((tiles,)),
            pltpu.SemaphoreType.DMA((tiles,)),
            pltpu.SemaphoreType.DMA((tiles,)),
        ],
        compiler_params=pltpu.CompilerParams(vmem_limit_bytes=50 * 1024 * 1024),
        cost_estimate=pl.CostEstimate(
            flops=4 * ff * width * slots, bytes_accessed=16 * 1024 * 1024, transcendentals=0
        ),
    )(info, *msgs, down_weight.reshape(ff, width), saved_all)

    terms = lax.psum_scatter(partial, "dp", scatter_dimension=0, tiled=True)
    slot_grad = lax.psum(jnp.sum(slot_part, axis=0), "dp")
    home = jnp.transpose(slot_grad.reshape(2, blocks, cap), (1, 0, 2)).reshape(blocks, 2 * cap)
    back = lax.all_to_all(home, "expert", split_axis=0, concat_axis=0, tiled=True)
    logits = pl.pallas_call(
        functools.partial(logits_kernel, cap),
        out_shape=[jax.ShapeDtypeStruct((top, tok), f32)] * 2,
        scratch_shapes=[pltpu.VMEM((top, tok), f32)],
    )(*side, back)
    hidden = []
    for m in range(2):
        cols = slice(m * slots, (m + 1) * slots)
        scaled = (gates[:1, cols] * terms[:, cols].astype(f32)).astype(bf16)
        hidden.append(scaled.reshape(1, ff_shard, 1, slots))
    return (*hidden, *(g.T[None] for g in logits))


def solution(mesh):
    in_specs = (
        P("section", "expert", "dp"),
        P("section", "expert", "dp"),
        P("section", "expert", None),
        P("section", "expert", None),
        P("section", "expert", None),
        P("section", "expert", None),
        P("section", "expert", None, "dp"),
        P("section", "dp", "expert", None),
        P("section", "dp", "expert", None),
    )
    out_specs = (
        P("section", "dp", "expert", None),
        P("section", "dp", "expert", None),
        P("section", "expert", None),
        P("section", "expert", None),
    )
    return jax.shard_map(shards, mesh=mesh, in_specs=in_specs, out_specs=out_specs, check_vma=False)
```

time: 167 us -> 160 us (0.958)
  the two profiles are of different devices: /device:TPU:4 before, /device:TPU:6 now
where the time goes in v2:
time: 160 us; the launch traced here: 159 us
  starting transfers between devices  74.2 us (46%)
  waiting for transfers between devices  34.5 us (22%)
  blocking collectives  19.3 us (12%)
  between operations  14.5 us (9%)
  Pallas kernels  11.7 us (7%)
  other arithmetic  4.3 us (3%)
    ppermute x7, starting transfers between devices, step(): fall = lax.ppermute(fall, 'expert', down)  40.7 us
    psum x1, blocking collectives, shards(): slot_grad = lax.psum(jnp.sum(slot_part, axis=0), 'dp')  19.3 us
    ppermute x7, starting transfers between devices, step(): rise = lax.ppermute(rise, 'expert', up)  17.2 us
    all_to_all x1, waiting for transfers between devices, shards(): lax.all_to_all(home, 'expert', split_axis=0, concat_axis=0, tiled=True)  12.3 us
    ppermute x3, starting transfers between devices, hop(): return lax.ppermute(array, ('section', 'expert'), pairs)  10.1 us
    ppermute x7, waiting for transfers between devices, step(): rise = lax.ppermute(rise, 'expert', up)  9 us
    pallas_call x1, Pallas kernels, shards(): pl.pallas_call(functools.partial(expert_kernel, blocks, tok, top, cap), i...  8.58 us
    reduce_scatter x1, waiting for transfers between devices, shards(): terms = lax.psum_scatter(partial, 'dp', scatter_dimension=0, tiled=True)  6.49 us
  transfers between devices with their start and end apart: 20, of which 8 were waited for; matrix products, arithmetic and copies ran while one was open for 1% of the time, Pallas kernels for 2%

profile of v2, /device:TPU:6, one launch (start us, length us, event | category | flops | bytes accessed | tf_op | source)
XLA Modules:
  0.0 159.4 jit_solution(17436062506548956141)
XLA Ops:
  9.1 2.4 %collective-permute-start.1 = (bf16[64,896]{1,0:T(8,128)(2,1)}, bf16[64,896]{1,0:T(8,128)(2,1)S(1)}, u32[]{:S(2)}, u32[]{:S(2)}) collective-permute-start(bf16[64,896]{1,0:T(8,128)(2,1)} %bitcast.60), channel_id=1, source_target_pairs={{0,128},{8,136},{16,144},{24,152},{32,160},{40,168},{48,176},{56,1... | collective-permute-start | bytes 344072 | tf_op jit(solution)/shard_map/ppermute | solution.py:162
  16.3 5.8 %collective-permute-start.4 = (bf16[136,896]{1,0:T(8,128)(2,1)S(1)}, bf16[136,896]{1,0:T(8,128)(2,1)S(1)}, u32[]{:S(2)}, u32[]{:S(2)}) collective-permute-start(bf16[136,896]{1,0:T(8,128)(2,1)S(1)} %pad_maximum_fusion.1.refs_0_), channel_id=1, source_target_pairs={{0,8},{8,0},{16,24},{24,16},{32,40},{40,32},{48,56},{56,48},{64,72... | collective-permute-start | bytes 731144 | tf_op jit(solution)/shard_map/ppermute | solution.py:162
  22.1 17.3 %collective-permute-start.3 = (bf16[136,896]{1,0:T(8,128)(2,1)S(1)}, bf16[136,896]{1,0:T(8,128)(2,1)S(1)}, u32[]{:S(2)}, u32[]{:S(2)}) collective-permute-start(bf16[136,896]{1,0:T(8,128)(2,1)S(1)} %pad_maximum_fusion.1.refs_0_), channel_id=1, source_target_pairs={{0,112},{8,120},{16,0},{24,8},{32,16},{40,24},{48,32},{56,40},{64,... | collective-permute-start | bytes 731144 | tf_op jit(solution)/shard_map/ppermute | solution.py:191
  39.4 1.9 %collective-permute-start.2 = (bf16[136,896]{1,0:T(8,128)(2,1)S(1)}, bf16[136,896]{1,0:T(8,128)(2,1)S(1)}, u32[]{:S(2)}, u32[]{:S(2)}) collective-permute-start(bf16[136,896]{1,0:T(8,128)(2,1)S(1)} %pad_maximum_fusion.1.refs_0_), channel_id=1, source_target_pairs={{0,16},{8,24},{16,32},{24,40},{32,48},{40,56},{48,64},{56,72},{64,... | collective-permute-start | bytes 731144 | tf_op jit(solution)/shard_map/ppermute | solution.py:187
  41.3 4.2 %collective-permute-done.3.refs_3_ = bf16[136,896]{1,0:T(8,128)(2,1)S(1)} collective-permute-done((bf16[136,896]{1,0:T(8,128)(2,1)S(1)}, bf16[136,896]{1,0:T(8,128)(2,1)S(1)}, u32[]{:S(2)}, u32[]{:S(2)}) %collective-permute-start.3) | collective-permute-done | bytes 243744 | tf_op jit(solution)/shard_map/ppermute | solution.py:191
  45.5 5.3 %collective-permute-done.2.refs_2_ = bf16[136,896]{1,0:T(8,128)(2,1)S(1)} collective-permute-done((bf16[136,896]{1,0:T(8,128)(2,1)S(1)}, bf16[136,896]{1,0:T(8,128)(2,1)S(1)}, u32[]{:S(2)}, u32[]{:S(2)}) %collective-permute-start.2) | collective-permute-done | bytes 243744 | tf_op jit(solution)/shard_map/ppermute | solution.py:187
  50.8 3.6 %collective-permute-start.11 = (bf16[136,896]{1,0:T(8,128)(2,1)S(1)}, bf16[136,896]{1,0:T(8,128)(2,1)S(1)}, u32[]{:S(2)}, u32[]{:S(2)}) collective-permute-start(bf16[136,896]{1,0:T(8,128)(2,1)S(1)} %collective-permute-done.4.refs_1_), channel_id=1, source_target_pairs={{0,112},{8,120},{16,0},{24,8},{32,16},{40,24},{48,32},{56,40},{64,... | collective-permute-start | bytes 731144 | tf_op jit(solution)/shard_map/ppermute | solution.py:191
  54.5 2.2 %collective-permute-start.5 = (bf16[136,896]{1,0:T(8,128)(2,1)S(1)}, bf16[136,896]{1,0:T(8,128)(2,1)S(1)}, u32[]{:S(2)}, u32[]{:S(2)}) collective-permute-start(bf16[136,896]{1,0:T(8,128)(2,1)S(1)} %collective-permute-done.2.refs_2_), channel_id=1, source_target_pairs={{0,16},{8,24},{16,32},{24,40},{32,48},{40,56},{48,64},{56,72},{64,... | collective-permute-start | bytes 731144 | tf_op jit(solution)/shard_map/ppermute | solution.py:187
  56.7 1.9 %collective-permute-start.10 = (bf16[136,896]{1,0:T(8,128)(2,1)S(1)}, bf16[136,896]{1,0:T(8,128)(2,1)S(1)}, u32[]{:S(2)}, u32[]{:S(2)}) collective-permute-start(bf16[136,896]{1,0:T(8,128)(2,1)S(1)} %collective-permute-done.4.refs_1_), channel_id=1, source_target_pairs={{0,16},{8,24},{16,32},{24,40},{32,48},{40,56},{48,64},{56,72},{64,... | collective-permute-start | bytes 731144 | tf_op jit(solution)/shard_map/ppermute | solution.py:187
  60.4 5.1 %collective-permute-start.13 = (bf16[136,896]{1,0:T(8,128)(2,1)S(1)}, bf16[136,896]{1,0:T(8,128)(2,1)S(1)}, u32[]{:S(2)}, u32[]{:S(2)}) collective-permute-start(bf16[136,896]{1,0:T(8,128)(2,1)S(1)} %collective-permute-done.11.refs_10_), channel_id=1, source_target_pairs={{0,112},{8,120},{16,0},{24,8},{32,16},{40,24},{48,32},{56,40},{64,... | collective-permute-start | bytes 731144 | tf_op jit(solution)/shard_map/ppermute | solution.py:191
  65.5 1.9 %collective-permute-start.6 = (bf16[136,896]{1,0:T(8,128)(2,1)S(1)}, bf16[136,896]{1,0:T(8,128)(2,1)S(1)}, u32[]{:S(2)}, u32[]{:S(2)}) collective-permute-start(bf16[136,896]{1,0:T(8,128)(2,1)S(1)} %collective-permute-done.3.refs_3_), channel_id=1, source_target_pairs={{0,112},{8,120},{16,0},{24,8},{32,16},{40,24},{48,32},{56,40},{64,... | collective-permute-start | bytes 731144 | tf_op jit(solution)/shard_map/ppermute | solution.py:191
  67.4 3.9 %collective-permute-start.7 = (bf16[136,896]{1,0:T(8,128)(2,1)S(1)}, bf16[136,896]{1,0:T(8,128)(2,1)S(1)}, u32[]{:S(2)}, u32[]{:S(2)}) collective-permute-start(bf16[136,896]{1,0:T(8,128)(2,1)S(1)} %collective-permute-done.5.refs_4_), channel_id=1, source_target_pairs={{0,16},{8,24},{16,32},{24,40},{32,48},{40,56},{48,64},{56,72},{64,... | collective-permute-start | bytes 731144 | tf_op jit(solution)/shard_map/ppermute | solution.py:187
  71.4 1.9 %collective-permute-start.12 = (bf16[136,896]{1,0:T(8,128)(2,1)S(1)}, bf16[136,896]{1,0:T(8,128)(2,1)S(1)}, u32[]{:S(2)}, u32[]{:S(2)}) collective-permute-start(bf16[136,896]{1,0:T(8,128)(2,1)S(1)} %collective-permute-done.10.refs_9_), channel_id=1, source_target_pairs={{0,16},{8,24},{16,32},{24,40},{32,48},{40,56},{48,64},{56,72},{64,... | collective-permute-start | bytes 731144 | tf_op jit(solution)/shard_map/ppermute | solution.py:187
  73.3 5.1 %collective-permute-start.15 = (bf16[136,896]{1,0:T(8,128)(2,1)S(1)}, bf16[136,896]{1,0:T(8,128)(2,1)S(1)}, u32[]{:S(2)}, u32[]{:S(2)}) collective-permute-start(bf16[136,896]{1,0:T(8,128)(2,1)S(1)} %collective-permute-done.13.refs_12_), channel_id=1, source_target_pairs={{0,112},{8,120},{16,0},{24,8},{32,16},{40,24},{48,32},{56,40},{64,... | collective-permute-start | bytes 731144 | tf_op jit(solution)/shard_map/ppermute | solution.py:191
  78.5 2.4 %collective-permute-start.8 = (bf16[136,896]{1,0:T(8,128)(2,1)S(1)}, bf16[136,896]{1,0:T(8,128)(2,1)S(1)}, u32[]{:S(2)}, u32[]{:S(2)}) collective-permute-start(bf16[136,896]{1,0:T(8,128)(2,1)S(1)} %collective-permute-done.6.refs_5_), channel_id=1, source_target_pairs={{0,112},{8,120},{16,0},{24,8},{32,16},{40,24},{48,32},{56,40},{64,... | collective-permute-start | bytes 731144 | tf_op jit(solution)/shard_map/ppermute | solution.py:191
  80.9 3.4 %collective-permute-start.9 = (bf16[136,896]{1,0:T(8,128)(2,1)S(1)}, bf16[136,896]{1,0:T(8,128)(2,1)S(1)}, u32[]{:S(2)}, u32[]{:S(2)}) collective-permute-start(bf16[136,896]{1,0:T(8,128)(2,1)S(1)} %collective-permute-done.7.refs_6_), channel_id=1, source_target_pairs={{0,16},{8,24},{16,32},{24,40},{32,48},{40,56},{48,64},{56,72},{64,... | collective-permute-start | bytes 731144 | tf_op jit(solution)/shard_map/ppermute | solution.py:187
  84.3 1.9 %collective-permute-start.14 = (bf16[136,896]{1,0:T(8,128)(2,1)S(1)}, bf16[136,896]{1,0:T(8,128)(2,1)}, u32[]{:S(2)}, u32[]{:S(2)}) collective-permute-start(bf16[136,896]{1,0:T(8,128)(2,1)S(1)} %collective-permute-done.12.refs_11_), channel_id=1, source_target_pairs={{0,16},{8,24},{16,32},{24,40},{32,48},{40,56},{48,64},{56,72},{64,... | collective-permute-start | bytes 731144 | tf_op jit(solution)/shard_map/ppermute | solution.py:187
  86.3 5.1 %collective-permute-start.16 = (bf16[136,896]{1,0:T(8,128)(2,1)S(1)}, bf16[136,896]{1,0:T(8,128)(2,1)}, u32[]{:S(2)}, u32[]{:S(2)}) collective-permute-start(bf16[136,896]{1,0:T(8,128)(2,1)S(1)} %collective-permute-done.15.refs_14_), channel_id=1, source_target_pairs={{0,112},{8,120},{16,0},{24,8},{32,16},{40,24},{48,32},{56,40},{64,... | collective-permute-start | bytes 731144 | tf_op jit(solution)/shard_map/ppermute | solution.py:191
  92.6 2.7 %collective-permute-done.14.refs_13_ = bf16[136,896]{1,0:T(8,128)(2,1)} collective-permute-done((bf16[136,896]{1,0:T(8,128)(2,1)S(1)}, bf16[136,896]{1,0:T(8,128)(2,1)}, u32[]{:S(2)}, u32[]{:S(2)}) %collective-permute-start.14) | collective-permute-done | bytes 243744 | tf_op jit(solution)/shard_map/ppermute | solution.py:187
  95.4 8.6 %shard_map.121 = (bf16[1024,1280]{1,0:T(8,128)(2,1)}, f32[8,1280]{1,0:T(8,128)S(1)}, f32[8,1280]{1,0:T(8,128)S(1)}) custom-call(s32[17]{0:T(128)S(1)} %stack.68.info, bf16[136,896]{1,0:T(8,128)(2,1)S(1)} %pad_maximum_fusion.1.refs_0_, bf16[136,896]{1,0:T(8,128)(2,1)S(1)} %collective-permute-done.4.refs_1_, ...), custom_call_target="tpu_custom_call" | custom-call | flops 2348810240 | bytes 16777216 | tf_op jit(solution)/shard_map/pallas_call | solution.py:212
  104.2 19.3 %psum.7 = f32[16,1,80]{2,0,1:T(8,128)} all-reduce(f32[16,1,80]{2,0,1:T(8,128)S(1)} %all_to_all.7), channel_id=1, replica_groups=mesh['section'=8,'expert'=16,'dp'=8] {'dp'}, use_global_device_ids=true, to_apply=%region_2.3 | all-reduce | flops 1280 | bytes 10240 | tf_op jit(solution)/shard_map/psum | solution.py:240
  123.5 6.1 %all-to-all-start = ((f32[16,1,80]{2,1,0:T(1,128)}), f32[16,1,80]{2,1,0:T(1,128)S(1)}, u32[]{:S(2)}, u32[]{:S(2)}) async-start(f32[16,1,80]{2,1,0:T(1,128)} %bitcast.36), calls=%async_computation.1 | async-start | bytes 16384 | tf_op jit(solution)/shard_map/all_to_all | solution.py:242
  129.7 12.3 %all-to-all-done = f32[16,1,80]{2,1,0:T(1,128)S(1)} async-done(((f32[16,1,80]{2,1,0:T(1,128)}), f32[16,1,80]{2,1,0:T(1,128)S(1)}, u32[]{:S(2)}, u32[]{:S(2)}) %all-to-all-start) | async-done | bytes 5152 | tf_op jit(solution)/shard_map/all_to_all | solution.py:242
  144.3 6.5 %reduce-scatter.2.cloned.1.call-done = bf16[128,1280]{1,0:T(8,128)(2,1)} async-done(((bf16[1024,1280]{1,0:T(8,128)(2,1)}), bf16[128,1280]{1,0:T(8,128)(2,1)}) %reduce-scatter.2.cloned.1.call-update) | async-done | bytes 327696 | tf_op jit(solution)/shard_map/reduce_scatter | solution.py:239
  (33 shorter events, 13.8 us)
Async XLA Ops:
  7.2 88.2 %all-gather.2.cloned.1.call-start = ((), (), s32[]{:S(2)}) async-start(), calls=%async_computation.2 | async-start | bytes 2949120 | tf_op jit(solution)/shard_map/all_gather | solution.py:177
  7.2 7.6 %collective-permute-start = (bf16[64,896]{1,0:T(8,128)(2,1)}, bf16[64,896]{1,0:T(8,128)(2,1)S(1)}, u32[]{:S(2)}, u32[]{:S(2)}) collective-permute-start(bf16[64,896]{1,0:T(8,128)(2,1)} %bitcast.59), channel_id=1, source_target_pairs={{0,896},{8,904},{16,912},{24,920},{32,928},{40,936},{48,944},{56,9... | collective-permute-start | bytes 344072 | tf_op jit(solution)/shard_map/ppermute | solution.py:162
  9.1 6.3 %collective-permute-start.1 = (bf16[64,896]{1,0:T(8,128)(2,1)}, bf16[64,896]{1,0:T(8,128)(2,1)S(1)}, u32[]{:S(2)}, u32[]{:S(2)}) collective-permute-start(bf16[64,896]{1,0:T(8,128)(2,1)} %bitcast.60), channel_id=1, source_target_pairs={{0,128},{8,136},{16,144},{24,152},{32,160},{40,168},{48,176},{56,1... | collective-permute-start | bytes 344072 | tf_op jit(solution)/shard_map/ppermute | solution.py:162
  16.2 134.6 %reduce-scatter.2.cloned.1.call-start = ((), (), s32[]{:S(2)}) async-start(), calls=%async_computation.3 | async-start | bytes 2949120 | tf_op jit(solution)/shard_map/reduce_scatter | solution.py:239
  16.3 25.1 %collective-permute-start.4 = (bf16[136,896]{1,0:T(8,128)(2,1)S(1)}, bf16[136,896]{1,0:T(8,128)(2,1)S(1)}, u32[]{:S(2)}, u32[]{:S(2)}) collective-permute-start(bf16[136,896]{1,0:T(8,128)(2,1)S(1)} %pad_maximum_fusion.1.refs_0_), channel_id=1, source_target_pairs={{0,8},{8,0},{16,24},{24,16},{32,40},{40,32},{48,56},{56,48},{64,72... | collective-permute-start | bytes 731144 | tf_op jit(solution)/shard_map/ppermute | solution.py:162
  22.1 23.4 %collective-permute-start.3 = (bf16[136,896]{1,0:T(8,128)(2,1)S(1)}, bf16[136,896]{1,0:T(8,128)(2,1)S(1)}, u32[]{:S(2)}, u32[]{:S(2)}) collective-permute-start(bf16[136,896]{1,0:T(8,128)(2,1)S(1)} %pad_maximum_fusion.1.refs_0_), channel_id=1, source_target_pairs={{0,112},{8,120},{16,0},{24,8},{32,16},{40,24},{48,32},{56,40},{64,... | collective-permute-start | bytes 731144 | tf_op jit(solution)/shard_map/ppermute | solution.py:191
  39.4 11.4 %collective-permute-start.2 = (bf16[136,896]{1,0:T(8,128)(2,1)S(1)}, bf16[136,896]{1,0:T(8,128)(2,1)S(1)}, u32[]{:S(2)}, u32[]{:S(2)}) collective-permute-start(bf16[136,896]{1,0:T(8,128)(2,1)S(1)} %pad_maximum_fusion.1.refs_0_), channel_id=1, source_target_pairs={{0,16},{8,24},{16,32},{24,40},{32,48},{40,56},{48,64},{56,72},{64,... | collective-permute-start | bytes 731144 | tf_op jit(solution)/shard_map/ppermute | solution.py:187
  50.8 9.5 %collective-permute-start.11 = (bf16[136,896]{1,0:T(8,128)(2,1)S(1)}, bf16[136,896]{1,0:T(8,128)(2,1)S(1)}, u32[]{:S(2)}, u32[]{:S(2)}) collective-permute-start(bf16[136,896]{1,0:T(8,128)(2,1)S(1)} %collective-permute-done.4.refs_1_), channel_id=1, source_target_pairs={{0,112},{8,120},{16,0},{24,8},{32,16},{40,24},{48,32},{56,40},{64,... | collective-permute-start | bytes 731144 | tf_op jit(solution)/shard_map/ppermute | solution.py:191
  54.5 13.0 %collective-permute-start.5 = (bf16[136,896]{1,0:T(8,128)(2,1)S(1)}, bf16[136,896]{1,0:T(8,128)(2,1)S(1)}, u32[]{:S(2)}, u32[]{:S(2)}) collective-permute-start(bf16[136,896]{1,0:T(8,128)(2,1)S(1)} %collective-permute-done.2.refs_2_), channel_id=1, source_target_pairs={{0,16},{8,24},{16,32},{24,40},{32,48},{40,56},{48,64},{56,72},{64,... | collective-permute-start | bytes 731144 | tf_op jit(solution)/shard_map/ppermute | solution.py:187
  56.7 14.7 %collective-permute-start.10 = (bf16[136,896]{1,0:T(8,128)(2,1)S(1)}, bf16[136,896]{1,0:T(8,128)(2,1)S(1)}, u32[]{:S(2)}, u32[]{:S(2)}) collective-permute-start(bf16[136,896]{1,0:T(8,128)(2,1)S(1)} %collective-permute-done.4.refs_1_), channel_id=1, source_target_pairs={{0,16},{8,24},{16,32},{24,40},{32,48},{40,56},{48,64},{56,72},{64,... | collective-permute-start | bytes 731144 | tf_op jit(solution)/shard_map/ppermute | solution.py:187
  60.4 12.9 %collective-permute-start.13 = (bf16[136,896]{1,0:T(8,128)(2,1)S(1)}, bf16[136,896]{1,0:T(8,128)(2,1)S(1)}, u32[]{:S(2)}, u32[]{:S(2)}) collective-permute-start(bf16[136,896]{1,0:T(8,128)(2,1)S(1)} %collective-permute-done.11.refs_10_), channel_id=1, source_target_pairs={{0,112},{8,120},{16,0},{24,8},{32,16},{40,24},{48,32},{56,40},{64,... | collective-permute-start | bytes 731144 | tf_op jit(solution)/shard_map/ppermute | solution.py:191
  65.5 13.0 %collective-permute-start.6 = (bf16[136,896]{1,0:T(8,128)(2,1)S(1)}, bf16[136,896]{1,0:T(8,128)(2,1)S(1)}, u32[]{:S(2)}, u32[]{:S(2)}) collective-permute-start(bf16[136,896]{1,0:T(8,128)(2,1)S(1)} %collective-permute-done.3.refs_3_), channel_id=1, source_target_pairs={{0,112},{8,120},{16,0},{24,8},{32,16},{40,24},{48,32},{56,40},{64,... | collective-permute-start | bytes 731144 | tf_op jit(solution)/shard_map/ppermute | solution.py:191
  67.4 13.5 %collective-permute-start.7 = (bf16[136,896]{1,0:T(8,128)(2,1)S(1)}, bf16[136,896]{1,0:T(8,128)(2,1)S(1)}, u32[]{:S(2)}, u32[]{:S(2)}) collective-permute-start(bf16[136,896]{1,0:T(8,128)(2,1)S(1)} %collective-permute-done.5.refs_4_), channel_id=1, source_target_pairs={{0,16},{8,24},{16,32},{24,40},{32,48},{40,56},{48,64},{56,72},{64,... | collective-permute-start | bytes 731144 | tf_op jit(solution)/shard_map/ppermute | solution.py:187
  71.4 13.0 %collective-permute-start.12 = (bf16[136,896]{1,0:T(8,128)(2,1)S(1)}, bf16[136,896]{1,0:T(8,128)(2,1)S(1)}, u32[]{:S(2)}, u32[]{:S(2)}) collective-permute-start(bf16[136,896]{1,0:T(8,128)(2,1)S(1)} %collective-permute-done.10.refs_9_), channel_id=1, source_target_pairs={{0,16},{8,24},{16,32},{24,40},{32,48},{40,56},{48,64},{56,72},{64,... | collective-permute-start | bytes 731144 | tf_op jit(solution)/shard_map/ppermute | solution.py:187
  73.3 13.0 %collective-permute-start.15 = (bf16[136,896]{1,0:T(8,128)(2,1)S(1)}, bf16[136,896]{1,0:T(8,128)(2,1)S(1)}, u32[]{:S(2)}, u32[]{:S(2)}) collective-permute-start(bf16[136,896]{1,0:T(8,128)(2,1)S(1)} %collective-permute-done.13.refs_12_), channel_id=1, source_target_pairs={{0,112},{8,120},{16,0},{24,8},{32,16},{40,24},{48,32},{56,40},{64,... | collective-permute-start | bytes 731144 | tf_op jit(solution)/shard_map/ppermute | solution.py:191
  78.5 13.2 %collective-permute-start.8 = (bf16[136,896]{1,0:T(8,128)(2,1)S(1)}, bf16[136,896]{1,0:T(8,128)(2,1)S(1)}, u32[]{:S(2)}, u32[]{:S(2)}) collective-permute-start(bf16[136,896]{1,0:T(8,128)(2,1)S(1)} %collective-permute-done.6.refs_5_), channel_id=1, source_target_pairs={{0,112},{8,120},{16,0},{24,8},{32,16},{40,24},{48,32},{56,40},{64,... | collective-permute-start | bytes 731144 | tf_op jit(solution)/shard_map/ppermute | solution.py:191
  80.9 11.7 %collective-permute-start.9 = (bf16[136,896]{1,0:T(8,128)(2,1)S(1)}, bf16[136,896]{1,0:T(8,128)(2,1)S(1)}, u32[]{:S(2)}, u32[]{:S(2)}) collective-permute-start(bf16[136,896]{1,0:T(8,128)(2,1)S(1)} %collective-permute-done.7.refs_6_), channel_id=1, source_target_pairs={{0,16},{8,24},{16,32},{24,40},{32,48},{40,56},{48,64},{56,72},{64,... | collective-permute-start | bytes 731144 | tf_op jit(solution)/shard_map/ppermute | solution.py:187
  84.3 11.0 %collective-permute-start.14 = (bf16[136,896]{1,0:T(8,128)(2,1)S(1)}, bf16[136,896]{1,0:T(8,128)(2,1)}, u32[]{:S(2)}, u32[]{:S(2)}) collective-permute-start(bf16[136,896]{1,0:T(8,128)(2,1)S(1)} %collective-permute-done.12.refs_11_), channel_id=1, source_target_pairs={{0,16},{8,24},{16,32},{24,40},{32,48},{40,56},{48,64},{56,72},{64,... | collective-permute-start | bytes 731144 | tf_op jit(solution)/shard_map/ppermute | solution.py:187
  86.3 9.1 %collective-permute-start.16 = (bf16[136,896]{1,0:T(8,128)(2,1)S(1)}, bf16[136,896]{1,0:T(8,128)(2,1)}, u32[]{:S(2)}, u32[]{:S(2)}) collective-permute-start(bf16[136,896]{1,0:T(8,128)(2,1)S(1)} %collective-permute-done.15.refs_14_), channel_id=1, source_target_pairs={{0,112},{8,120},{16,0},{24,8},{32,16},{40,24},{48,32},{56,40},{64,... | collective-permute-start | bytes 731144 | tf_op jit(solution)/shard_map/ppermute | solution.py:191
  123.5 18.4 %all-to-all-start = ((f32[16,1,80]{2,1,0:T(1,128)}), f32[16,1,80]{2,1,0:T(1,128)S(1)}, u32[]{:S(2)}, u32[]{:S(2)}) async-start(f32[16,1,80]{2,1,0:T(1,128)} %bitcast.36), calls=%async_computation.1 | async-start | bytes 16384 | tf_op jit(solution)/shard_map/all_to_all | solution.py:242
  142.0 0.6 copy-start
Sparse Core Ops, SparseCore 0:
  16.3 60.6 all-gather.1
  104.1 46.6 reduce-scatter.1

commit v3 on v2

v3 whole, which is shorter than its diff:
```python
import functools

import jax
import jax.numpy as jnp
from jax import lax
from jax.experimental import pallas as pl
from jax.experimental.pallas import tpu as pltpu
from jax.sharding import PartitionSpec as P

route_scale = 2.5
META = 8
NT = (((1,), (1,)), ((), ()))
f32 = jnp.float32
bf16 = jnp.bfloat16


def pack_kernel(rf, sf, rr, sr, out, buf):
    top, tok = rf.shape
    buf[...] = jnp.zeros_like(buf)
    for m, (routes, scores) in enumerate(((rf, sf), (rr, sr))):
        ids = routes[...].astype(f32)
        s = scores[...]
        gate = route_scale * s / jnp.sum(s, axis=0, keepdims=True)
        for k in range(top):
            buf[2 * m : 2 * m + 1, k * tok : (k + 1) * tok] = ids[k : k + 1]
            buf[2 * m + 1 : 2 * m + 2, k * tok : (k + 1) * tok] = gate[k : k + 1]
    out[...] = buf[...].astype(out.dtype)


def saved_kernel(half, info, first, second, out):
    for m, ref in enumerate((first, second)):
        turned = pltpu.roll(ref[...].astype(f32), info[3], 1).astype(out.dtype)
        for h in range(2):
            at = (2 * h + m) * half
            out[:, at : at + half] = turned[:, h * half : (h + 1) * half]


def hidden_kernel(half, info, terms, gate_0, gate_1, first, second):
    for m, out in enumerate((first, second)):
        low, high = slice(m * half, (m + 1) * half), slice((2 + m) * half, (3 + m) * half)
        x = jnp.concatenate([terms[:, low], terms[:, high]], axis=1).astype(f32)
        gate = jnp.concatenate([gate_0[0:1, low], gate_1[0:1, low]], axis=1)
        out[...] = pltpu.roll(x * gate, info[2], 1).astype(out.dtype)


def expert_kernel(blocks, tok, top, cap, half, info, *refs):
    msgs = refs[:blocks]
    refs = refs[blocks:]
    w_hbm, saved_hbm = refs[:2]
    part_hbm, slot_ref, gate_ref, rows16, gcol, meta, w_ref, saved_ref, part_ref, w_sem, saved_sem, part_sem = refs[-12:]
    slots = blocks * cap
    lanes = 2 * tok
    tiles = w_sem.shape[0]
    tile = w_ref.shape[0] // tiles
    columns = pl.ds(half * 2 * slots, 2 * slots)
    parts = [pl.ds(i * tile, tile) for i in range(tiles)]
    fetched = []
    for i, at in enumerate(parts):
        pair = (
            pltpu.make_async_copy(w_hbm.at[at], w_ref.at[at], w_sem.at[i]),
            pltpu.make_async_copy(saved_hbm.at[at, columns], saved_ref.at[at], saved_sem.at[i]),
        )
        for copy in pair:
            copy.start()
        fetched.append(pair)

    for b in range(blocks):
        meta[b * META : (b + 1) * META, :] = msgs[b][lanes : lanes + META, : top * tok].astype(f32)
    vals = meta[...]
    mine = (vals == info[0].astype(f32)).astype(f32)
    t_in = lax.rem(lax.broadcasted_iota(jnp.int32, (top * tok, lanes), 0), tok)
    t_out = lax.rem(lax.broadcasted_iota(jnp.int32, (top * tok, lanes), 1), tok)
    same = (t_in == t_out).astype(f32).astype(bf16)
    before = (t_in < t_out).astype(f32).astype(bf16)
    hot = mine.astype(bf16)
    named = jnp.dot(hot, same, preferred_element_type=f32)
    place = jnp.dot(hot, before, preferred_element_type=f32)
    picked = (pltpu.roll(mine, 1, 0) * vals).astype(bf16)
    gates = jnp.dot(picked, same, preferred_element_type=f32)
    rising = lax.broadcasted_iota(jnp.int32, (1, lanes), 1) >= tok
    shift = jnp.where(rising, float(cap), 0.0)
    slot_id = lax.broadcasted_iota(jnp.int32, (2 * cap, lanes), 0).astype(f32)
    swapped = info[1] == 1
    for p in range(blocks // 2):
        got, col = [], []
        for b in (2 * p, 2 * p + 1):
            r = b * META
            name = jnp.where(rising, named[r + 2 : r + 3], named[r : r + 1])
            pos = jnp.where(rising, place[r + 2 : r + 3], place[r : r + 1])
            gate = jnp.where(rising, gates[r + 3 : r + 4], gates[r + 1 : r + 2])
            target = jnp.where(name > 0.5, pos + shift, -1.0)
            put = (slot_id == target).astype(f32)
            got.append(jnp.dot(put.astype(bf16), msgs[b][:lanes, :], preferred_element_type=f32))
            col.append(jnp.broadcast_to(jnp.sum(put * gate, axis=1, keepdims=True), (2 * cap, gcol.shape[1])))
        for array, ref in ((got, rows16), (col, gcol)):
            low = jnp.where(swapped, array[1], array[0])
            high = jnp.where(swapped, array[0], array[1])
            for m in range(2):
                at, take = m * slots + 2 * p * cap, slice(m * cap, (m + 1) * cap)
                ref[at : at + 2 * cap, :] = jnp.concatenate([low[take], high[take]], axis=0).astype(bf16)
    first = (lax.broadcasted_iota(jnp.int32, (8, gcol.shape[1]), 1) == 0).astype(f32).astype(bf16)
    gate_ref[...] = lax.dot_general(first, gcol[...], NT, preferred_element_type=f32)

    sent = []
    for i, at in enumerate(parts):
        for copy in fetched[i]:
            copy.wait()
        part = lax.dot_general(w_ref[at, :], rows16[...], NT, preferred_element_type=f32).astype(bf16)
        part_ref[at, :] = part
        prod = part.astype(f32) * saved_ref[at, :].astype(f32)
        total = jnp.sum(prod.reshape(-1, 8, 2 * slots), axis=0)
        slot_ref[...] = total if i == 0 else slot_ref[...] + total
        copy = pltpu.make_async_copy(part_ref.at[at], part_hbm.at[at, columns], part_sem.at[i])
        copy.start()
        sent.append(copy)
    for copy in sent:
        copy.wait()


def logits_kernel(cap, rf, sf, rr, sr, back, out_f, out_r, grad):
    top, tok = rf.shape
    experts = back.shape[0]
    ids = lax.broadcasted_iota(jnp.int32, (experts, tok), 0)
    t0 = lax.broadcasted_iota(jnp.int32, (tok, tok), 0)
    t1 = lax.broadcasted_iota(jnp.int32, (tok, tok), 1)
    before = (t0 < t1).astype(f32).astype(bf16)
    for m, (routes, scores, out) in enumerate(((rf, sf, out_f), (rr, sr, out_r))):
        named = jnp.zeros((experts, tok), f32)
        for k in range(top):
            named += (routes[k : k + 1, :] == ids).astype(f32)
        place = jnp.dot(named.astype(bf16), before, preferred_element_type=f32)
        vals = jnp.zeros((experts, tok), f32)
        for c in range(cap):
            vals += jnp.where(place == float(c), back[:, m * cap + c : m * cap + c + 1], 0.0)
        for k in range(top):
            chosen = jnp.where(routes[k : k + 1, :] == ids, vals, 0.0)
            grad[k : k + 1, :] = jnp.sum(chosen, axis=0, keepdims=True)
        s = scores[...]
        total = jnp.sum(s, axis=0, keepdims=True)
        mean = jnp.sum(grad[...] * s, axis=0, keepdims=True) / total
        out[...] = route_scale / total * (grad[...] - mean) * s * (1.0 - s)


def shards(
    falling_grad,
    rising_grad,
    routes_falling,
    routes_rising,
    scores_falling,
    scores_rising,
    down_weight,
    saved_falling,
    saved_rising,
):
    blocks = lax.axis_size("expert")
    sections = lax.axis_size("section")
    dp = lax.axis_size("dp")
    tok, width = falling_grad.shape[1:]
    top = routes_falling.shape[2]
    ff_shard, slots = saved_falling.shape[1], saved_falling.shape[3]
    cap = slots // blocks
    ff = ff_shard * dp
    depth = blocks // 2
    lanes = 2 * tok

    side = (
        routes_falling[0].T,
        scores_falling[0].T,
        routes_rising[0].T,
        scores_rising[0].T,
    )
    me = lax.axis_index("expert")
    level, column = me // 2, me % 2
    turn = (level + depth - 1) % depth
    group = slots // 2
    info = jnp.stack(
        [me, column, turn * 2 * cap, (depth - turn) % depth * 2 * cap]
    ).astype(jnp.int32)
    smem = pl.BlockSpec(memory_space=pltpu.SMEM)
    vmem = pl.BlockSpec(memory_space=pltpu.VMEM)
    hbm = pl.BlockSpec(memory_space=pltpu.HBM)

    def hop(array, by, flip):
        pairs = [
            (s * blocks + e, (s + by) % sections * blocks + (e ^ flip))
            for s in range(sections)
            for e in range(blocks)
        ]
        return lax.ppermute(array, ("section", "expert"), pairs)

    own_f, own_r = hop(falling_grad[0], -1, 0), hop(rising_grad[0], 1, 0)
    meta = pl.pallas_call(
        pack_kernel,
        out_shape=jax.ShapeDtypeStruct((META, width), bf16),
        scratch_shapes=[pltpu.VMEM((META, width), f32)],
    )(*side)
    own = jnp.concatenate([own_f, own_r, meta], axis=0)
    far = hop(own, 0, 1)

    saved = pl.pallas_call(
        functools.partial(saved_kernel, group),
        in_specs=[smem, vmem, vmem],
        out_specs=vmem,
        out_shape=jax.ShapeDtypeStruct((ff_shard, 2 * slots), bf16),
    )(info, saved_falling.reshape(ff_shard, slots), saved_rising.reshape(ff_shard, slots))
    own_ring, saved = lax.optimization_barrier((own, saved))
    saved_all = lax.all_gather(saved, "dp", tiled=True)

    up = [(i, (i + 2) % blocks) for i in range(blocks)]
    down = [(i, (i - 2) % blocks) for i in range(blocks)]
    half = depth // 2
    near, away = {0: own}, {0: far}
    near[-1] = lax.ppermute(own_ring, "expert", up)
    near[1] = lax.ppermute(own_ring, "expert", down)
    near[-1], near[1], away[0] = lax.optimization_barrier((near[-1], near[1], far))
    for t in range(1, half + 1):
        if t > 1:
            near[-t] = lax.ppermute(near[1 - t], "expert", up)
        if 1 < t < half:
            near[t] = lax.ppermute(near[t - 1], "expert", down)
        if t < half:
            away[-t] = lax.ppermute(away[1 - t], "expert", up)
        away[t] = lax.ppermute(away[t - 1], "expert", down)
    near[half] = near[-half]

    tiles = max(1, ff // 256)

    def multiply(part, levels, held):
        msgs = [side[r if r <= half else r - depth] for r in levels for side in (near, away)]
        blocks = len(msgs)
        width_out = 2 * blocks * cap
        return pl.pallas_call(
            functools.partial(expert_kernel, blocks, tok, top, cap, part),
            in_specs=[smem] + [vmem] * blocks + [hbm, hbm] + [hbm] * len(held),
            out_specs=[hbm, vmem, vmem],
            out_shape=[
                jax.ShapeDtypeStruct((ff, 2 * slots), bf16),
                jax.ShapeDtypeStruct((8, width_out), f32),
                jax.ShapeDtypeStruct((8, width_out), f32),
            ],
            input_output_aliases={blocks + 3: 0} if held else {},
            scratch_shapes=[
                pltpu.VMEM((width_out, width), bf16),
                pltpu.VMEM((width_out, 128), bf16),
                pltpu.VMEM((blocks * META, top * tok), f32),
                pltpu.VMEM((ff, width), bf16),
                pltpu.VMEM((ff, width_out), bf16),
                pltpu.VMEM((ff, width_out), bf16),
                pltpu.SemaphoreType.DMA((tiles,)),
                pltpu.SemaphoreType.DMA((tiles,)),
                pltpu.SemaphoreType.DMA((tiles,)),
            ],
            compiler_params=pltpu.CompilerParams(vmem_limit_bytes=50 * 1024 * 1024),
            cost_estimate=pl.CostEstimate(
                flops=2 * ff * width * slots, bytes_accessed=8 * 1024 * 1024, transcendentals=0
            ),
        )(info, *msgs, down_weight.reshape(ff, width), saved_all, *held)

    partial, slot_0, gate_0 = multiply(0, (-1, 0, 1, 2), ())
    partial, slot_1, gate_1 = multiply(1, (3, 4, 5, 6), (partial,))

    terms = lax.psum_scatter(partial, "dp", scatter_dimension=0, tiled=True)
    slot_part = jnp.stack([slot_0, slot_1], axis=1).reshape(8, 2, 2, group)
    slot_part = jnp.moveaxis(jnp.sum(slot_part, axis=0), 0, 1).reshape(2, slots)
    slot_grad = lax.psum(slot_part, "dp")
    slot_grad = jnp.roll(slot_grad, info[2], axis=1)
    home = jnp.transpose(slot_grad.reshape(2, blocks, cap), (1, 0, 2)).reshape(blocks, 2 * cap)
    back = lax.all_to_all(home, "expert", split_axis=0, concat_axis=0, tiled=True)
    logits = pl.pallas_call(
        functools.partial(logits_kernel, cap),
        out_shape=[jax.ShapeDtypeStruct((top, tok), f32)] * 2,
        scratch_shapes=[pltpu.VMEM((top, tok), f32)],
    )(*side, back)
    hidden = pl.pallas_call(
        functools.partial(hidden_kernel, group),
        in_specs=[smem, vmem, vmem, vmem],
        out_specs=[vmem, vmem],
        out_shape=[jax.ShapeDtypeStruct((ff_shard, slots), bf16)] * 2,
    )(info, terms, gate_0, gate_1)
    hidden = [h.reshape(1, ff_shard, 1, slots) for h in hidden]
    return (*hidden, *(g.T[None] for g in logits))


def solution(mesh):
    in_specs = (
        P("section", "expert", "dp"),
        P("section", "expert", "dp"),
        P("section", "expert", None),
        P("section", "expert", None),
        P("section", "expert", None),
        P("section", "expert", None),
        P("section", "expert", None, "dp"),
        P("section", "dp", "expert", None),
        P("section", "dp", "expert", None),
    )
    out_specs = (
        P("section", "dp", "expert", None),
        P("section", "dp", "expert", None),
        P("section", "expert", None),
        P("section", "expert", None),
    )
    return jax.shard_map(shards, mesh=mesh, in_specs=in_specs, out_specs=out_specs, check_vma=False)
```

time: 160 us -> 162 us (1.012)
  the two profiles are of different devices: /device:TPU:6 before, /device:TPU:8 now
where the time goes in v3:
time: 162 us; the launch traced here: 161 us
  starting transfers between devices  67.1 us (41%)
  blocking collectives  32.7 us (20%)
  waiting for transfers between devices  21.4 us (13%)
  Pallas kernels  19.9 us (12%)
  between operations  14.4 us (9%)
  local copies, waits for them, and re-layouts  3.73 us (2%)
    ppermute x3, starting transfers between devices, hop(): return lax.ppermute(array, ('section', 'expert'), pairs)  21.5 us
    psum x1, blocking collectives, shards(): slot_grad = lax.psum(slot_part, 'dp')  18.6 us
    ppermute x4, starting transfers between devices, shards(): away[t] = lax.ppermute(away[t - 1], 'expert', down)  17 us
    all_to_all x1, blocking collectives, shards(): lax.all_to_all(home, 'expert', split_axis=0, concat_axis=0, tiled=True)  14.1 us
    pallas_call x2, Pallas kernels, multiply(): pl.pallas_call(functools.partial(expert_kernel, blocks, tok, top, cap, pa...  12.5 us
    reduce_scatter x1, waiting for transfers between devices, shards(): terms = lax.psum_scatter(partial, 'dp', scatter_dimension=0, tiled=True)  12.1 us
    ppermute x3, starting transfers between devices, shards(): near[-t] = lax.ppermute(near[1 - t], 'expert', up)  11.8 us
    ppermute x3, starting transfers between devices, shards(): away[-t] = lax.ppermute(away[1 - t], 'expert', up)  5.76 us
  transfers between devices with their start and end apart: 19, of which 5 were waited for; matrix products, arithmetic and copies ran while one was open for 1% of the time, Pallas kernels for 7%

profile of v3, /device:TPU:8, one launch (start us, length us, event | category | flops | bytes accessed | tf_op | source)
XLA Modules:
  0.0 160.7 jit_solution(1104114275190480365)
XLA Ops:
  7.2 2.0 %collective-permute-start = (bf16[64,896]{1,0:T(8,128)(2,1)}, bf16[64,896]{1,0:T(8,128)(2,1)S(1)}, u32[]{:S(2)}, u32[]{:S(2)}) collective-permute-start(bf16[64,896]{1,0:T(8,128)(2,1)} %bitcast.51), channel_id=1, source_target_pairs={{0,896},{8,904},{16,912},{24,920},{32,928},{40,936},{48,944},{56,9... | collective-permute-start | bytes 344072 | tf_op jit(solution)/shard_map/ppermute | solution.py:189
  9.2 2.3 %collective-permute-start.1 = (bf16[64,896]{1,0:T(8,128)(2,1)}, bf16[64,896]{1,0:T(8,128)(2,1)S(1)}, u32[]{:S(2)}, u32[]{:S(2)}) collective-permute-start(bf16[64,896]{1,0:T(8,128)(2,1)} %bitcast.52), channel_id=1, source_target_pairs={{0,128},{8,136},{16,144},{24,152},{32,160},{40,168},{48,176},{56,1... | collective-permute-start | bytes 344072 | tf_op jit(solution)/shard_map/ppermute | solution.py:189
  12.2 2.1 %shard_map.121 = bf16[128,1280]{1,0:T(8,128)(2,1)} custom-call(s32[4]{0:T(128)} %pad_add_fusion.info, bf16[128,640]{1,0:T(8,128)(2,1)} %bitcast.35, bf16[128,640]{1,0:T(8,128)(2,1)} %bitcast.36), custom_call_target="tpu_custom_call" | custom-call | tf_op jit(solution)/shard_map/pallas_call | solution.py:200
  18.1 17.2 %collective-permute-start.4 = (bf16[136,896]{1,0:T(8,128)(2,1)S(1)}, bf16[136,896]{1,0:T(8,128)(2,1)S(1)}, u32[]{:S(2)}, u32[]{:S(2)}) collective-permute-start(bf16[136,896]{1,0:T(8,128)(2,1)S(1)} %pad_maximum_fusion.refs_2_), channel_id=1, source_target_pairs={{0,8},{8,0},{16,24},{24,16},{32,40},{40,32},{48,56},{56,48},{64,72... | collective-permute-start | bytes 731144 | tf_op jit(solution)/shard_map/ppermute | solution.py:189
  35.3 5.2 %collective-permute-start.3 = (bf16[136,896]{1,0:T(8,128)(2,1)S(1)}, bf16[136,896]{1,0:T(8,128)(2,1)S(1)}, u32[]{:S(2)}, u32[]{:S(2)}) collective-permute-start(bf16[136,896]{1,0:T(8,128)(2,1)S(1)} %pad_maximum_fusion.refs_2_), channel_id=1, source_target_pairs={{0,112},{8,120},{16,0},{24,8},{32,16},{40,24},{48,32},{56,40},{64,... | collective-permute-start | bytes 731144 | tf_op jit(solution)/shard_map/ppermute | solution.py:214
  40.5 1.9 %collective-permute-start.2 = (bf16[136,896]{1,0:T(8,128)(2,1)S(1)}, bf16[136,896]{1,0:T(8,128)(2,1)S(1)}, u32[]{:S(2)}, u32[]{:S(2)}) collective-permute-start(bf16[136,896]{1,0:T(8,128)(2,1)S(1)} %pad_maximum_fusion.refs_2_), channel_id=1, source_target_pairs={{0,16},{8,24},{16,32},{24,40},{32,48},{40,56},{48,64},{56,72},{64,... | collective-permute-start | bytes 731144 | tf_op jit(solution)/shard_map/ppermute | solution.py:213
  44.2 5.6 %collective-permute-done.2.refs_0_ = bf16[136,896]{1,0:T(8,128)(2,1)S(1)} collective-permute-done((bf16[136,896]{1,0:T(8,128)(2,1)S(1)}, bf16[136,896]{1,0:T(8,128)(2,1)S(1)}, u32[]{:S(2)}, u32[]{:S(2)}) %collective-permute-start.2) | collective-permute-done | bytes 243744 | tf_op jit(solution)/shard_map/ppermute | solution.py:213
  51.7 3.9 %collective-permute-start.10 = (bf16[136,896]{1,0:T(8,128)(2,1)S(1)}, bf16[136,896]{1,0:T(8,128)(2,1)S(1)}, u32[]{:S(2)}, u32[]{:S(2)}) collective-permute-start(bf16[136,896]{1,0:T(8,128)(2,1)S(1)} %collective-permute-done.2.refs_0_), channel_id=1, source_target_pairs={{0,16},{8,24},{16,32},{24,40},{32,48},{40,56},{48,64},{56,72},{64,... | collective-permute-start | bytes 731144 | tf_op jit(solution)/shard_map/ppermute | solution.py:218
  55.7 1.9 %collective-permute-start.14 = (bf16[136,896]{1,0:T(8,128)(2,1)S(1)}, bf16[136,896]{1,0:T(8,128)(2,1)S(1)}, u32[]{:S(2)}, u32[]{:S(2)}) collective-permute-start(bf16[136,896]{1,0:T(8,128)(2,1)S(1)} %collective-permute-done.4.refs_3_), channel_id=1, source_target_pairs={{0,16},{8,24},{16,32},{24,40},{32,48},{40,56},{48,64},{56,72},{64,... | collective-permute-start | bytes 731144 | tf_op jit(solution)/shard_map/ppermute | solution.py:222
  57.9 4.9 %collective-permute-start.8 = (bf16[136,896]{1,0:T(8,128)(2,1)S(1)}, bf16[136,896]{1,0:T(8,128)(2,1)S(1)}, u32[]{:S(2)}, u32[]{:S(2)}) collective-permute-start(bf16[136,896]{1,0:T(8,128)(2,1)S(1)} %collective-permute-done.7.refs_5_), channel_id=1, source_target_pairs={{0,112},{8,120},{16,0},{24,8},{32,16},{40,24},{48,32},{56,40},{64,... | collective-permute-start | bytes 731144 | tf_op jit(solution)/shard_map/ppermute | solution.py:223
  62.7 1.9 %collective-permute-start.5 = (bf16[136,896]{1,0:T(8,128)(2,1)S(1)}, bf16[136,896]{1,0:T(8,128)(2,1)S(1)}, u32[]{:S(2)}, u32[]{:S(2)}) collective-permute-start(bf16[136,896]{1,0:T(8,128)(2,1)S(1)} %collective-permute-done.3.refs_4_), channel_id=1, source_target_pairs={{0,112},{8,120},{16,0},{24,8},{32,16},{40,24},{48,32},{56,40},{64,... | collective-permute-start | bytes 731144 | tf_op jit(solution)/shard_map/ppermute | solution.py:220
  64.7 3.9 %collective-permute-start.11 = (bf16[136,896]{1,0:T(8,128)(2,1)S(1)}, bf16[136,896]{1,0:T(8,128)(2,1)S(1)}, u32[]{:S(2)}, u32[]{:S(2)}) collective-permute-start(bf16[136,896]{1,0:T(8,128)(2,1)S(1)} %collective-permute-done.10.refs_6_), channel_id=1, source_target_pairs={{0,16},{8,24},{16,32},{24,40},{32,48},{40,56},{48,64},{56,72},{64,... | collective-permute-start | bytes 731144 | tf_op jit(solution)/shard_map/ppermute | solution.py:218
  68.6 1.9 %collective-permute-start.15 = (bf16[136,896]{1,0:T(8,128)(2,1)S(1)}, bf16[136,896]{1,0:T(8,128)(2,1)S(1)}, u32[]{:S(2)}, u32[]{:S(2)}) collective-permute-start(bf16[136,896]{1,0:T(8,128)(2,1)S(1)} %collective-permute-done.14.refs_1_), channel_id=1, source_target_pairs={{0,16},{8,24},{16,32},{24,40},{32,48},{40,56},{48,64},{56,72},{64,... | collective-permute-start | bytes 731144 | tf_op jit(solution)/shard_map/ppermute | solution.py:222
  70.6 5.1 %collective-permute-start.9 = (bf16[136,896]{1,0:T(8,128)(2,1)S(1)}, bf16[136,896]{1,0:T(8,128)(2,1)S(1)}, u32[]{:S(2)}, u32[]{:S(2)}) collective-permute-start(bf16[136,896]{1,0:T(8,128)(2,1)S(1)} %collective-permute-done.8.refs_7_), channel_id=1, source_target_pairs={{0,112},{8,120},{16,0},{24,8},{32,16},{40,24},{48,32},{56,40},{64,... | collective-permute-start | bytes 731144 | tf_op jit(solution)/shard_map/ppermute | solution.py:223
  75.7 1.9 %collective-permute-start.6 = (bf16[136,896]{1,0:T(8,128)(2,1)S(1)}, bf16[136,896]{1,0:T(8,128)(2,1)S(1)}, u32[]{:S(2)}, u32[]{:S(2)}) collective-permute-start(bf16[136,896]{1,0:T(8,128)(2,1)S(1)} %collective-permute-done.5.refs_6_), channel_id=1, source_target_pairs={{0,112},{8,120},{16,0},{24,8},{32,16},{40,24},{48,32},{56,40},{64,... | collective-permute-start | bytes 731144 | tf_op jit(solution)/shard_map/ppermute | solution.py:220
  77.6 3.9 %collective-permute-start.12 = (bf16[136,896]{1,0:T(8,128)(2,1)S(1)}, bf16[136,896]{1,0:T(8,128)(2,1)S(1)}, u32[]{:S(2)}, u32[]{:S(2)}) collective-permute-start(bf16[136,896]{1,0:T(8,128)(2,1)S(1)} %collective-permute-done.11.refs_4_), channel_id=1, source_target_pairs={{0,16},{8,24},{16,32},{24,40},{32,48},{40,56},{48,64},{56,72},{64,... | collective-permute-start | bytes 731144 | tf_op jit(solution)/shard_map/ppermute | solution.py:218
  81.6 1.9 %collective-permute-start.16 = (bf16[136,896]{1,0:T(8,128)(2,1)S(1)}, bf16[136,896]{1,0:T(8,128)(2,1)}, u32[]{:S(2)}, u32[]{:S(2)}) collective-permute-start(bf16[136,896]{1,0:T(8,128)(2,1)S(1)} %collective-permute-done.15.refs_7_), channel_id=1, source_target_pairs={{0,16},{8,24},{16,32},{24,40},{32,48},{40,56},{48,64},{56,72},{64,... | collective-permute-start | bytes 731144 | tf_op jit(solution)/shard_map/ppermute | solution.py:222
  83.5 5.1 %collective-permute-start.13 = (bf16[136,896]{1,0:T(8,128)(2,1)S(1)}, bf16[136,896]{1,0:T(8,128)(2,1)}, u32[]{:S(2)}, u32[]{:S(2)}) collective-permute-start(bf16[136,896]{1,0:T(8,128)(2,1)S(1)} %collective-permute-done.9.refs_1_), channel_id=1, source_target_pairs={{0,112},{8,120},{16,0},{24,8},{32,16},{40,24},{48,32},{56,40},{64,... | collective-permute-start | bytes 731144 | tf_op jit(solution)/shard_map/ppermute | solution.py:223
  90.8 6.0 %shard_map.122 = (bf16[1024,1280]{1,0:T(8,128)(2,1)}, f32[8,640]{1,0:T(8,128)S(1)}, f32[8,640]{1,0:T(8,128)S(1)}) custom-call(s32[4]{0:T(128)S(1)} %copy-done.4, bf16[136,896]{1,0:T(8,128)(2,1)S(1)} %collective-permute-done.2.refs_0_, bf16[136,896]{1,0:T(8,128)(2,1)S(1)} %collective-permute-done.14.refs_1_, bf16[136,896]{1,0:T(8,128)(2,1)S(1)} %pad_maximum_fusion.refs_2_, ...), custom_call_target="tpu_custom_call" | custom-call | flops 1174405120 | bytes 8388608 | tf_op jit(solution)/shard_map/pallas_call | solution.py:232
  97.4 6.5 %shard_map.123 = (bf16[1024,1280]{1,0:T(8,128)(2,1)}, f32[8,640]{1,0:T(8,128)S(1)}, f32[8,640]{1,0:T(8,128)S(1)}) custom-call(s32[4]{0:T(128)S(1)} %copy-done.4, bf16[136,896]{1,0:T(8,128)(2,1)S(1)} %collective-permute-done.6.refs_0_, bf16[136,896]{1,0:T(8,128)(2,1)S(1)} %collective-permute-done.9.refs_1_, ...), custom_call_target="tpu_custom_call", output_to_operand_aliasing={{0}: (11, {})} | custom-call | flops 1174405120 | bytes 8388608 | tf_op jit(solution)/shard_map/pallas_call | solution.py:232
  104.9 18.6 %psum.7 = f32[2,640]{1,0:T(2,128)S(1)} all-reduce(f32[2,640]{1,0:T(2,128)S(1)} %reshape.44), channel_id=1, replica_groups=mesh['section'=8,'expert'=16,'dp'=8] {'dp'}, use_global_device_ids=true, to_apply=%region_2.3 | all-reduce | flops 1280 | bytes 10240 | tf_op jit(solution)/shard_map/psum | solution.py:265
  123.9 14.1 %all_to_all.11 = f32[16,1,80]{2,1,0:T(1,128)} all-to-all(f32[16,1,80]{2,1,0:T(1,128)S(1)} %bitcast.39), channel_id=1, replica_groups=mesh['section'=8,'expert'=16,'dp'=8] {'expert'}, dimensions={0} | all-to-all | bytes 10240 | tf_op jit(solution)/shard_map/all_to_all | solution.py:268
  139.7 12.1 %reduce-scatter.2.cloned.1.call-done.terms = bf16[128,1280]{1,0:T(8,128)(2,1)} async-done(((bf16[1024,1280]{1,0:T(8,128)(2,1)}), bf16[128,1280]{1,0:T(8,128)(2,1)}) %reduce-scatter.2.cloned.1.call-update) | async-done | bytes 327696 | tf_op jit(solution)/shard_map/reduce_scatter | solution.py:262
  151.8 2.1 %shard_map.124 = (bf16[128,640]{1,0:T(8,128)(2,1)}, bf16[128,640]{1,0:T(8,128)(2,1)}) custom-call(s32[4]{0:T(128)} %pad_add_fusion.info, bf16[128,1280]{1,0:T(8,128)(2,1)} %reduce-scatter.2.cloned.1.call-done.terms, f32[8,640]{1,0:T(8,128)} %copy-done.2, f32[8,640]{1,0:T(8,128)} %copy-done.3), custom_call_target="tpu_custom_call" | custom-call | tf_op jit(solution)/shard_map/pallas_call | solution.py:274
  (45 shorter events, 14.0 us)
Async XLA Ops:
  7.2 81.5 %all-gather.2.cloned.1.call-start = ((), (), s32[]{:S(2)}) async-start(), calls=%async_computation.2 | async-start | bytes 2949120 | tf_op jit(solution)/shard_map/all_gather | solution.py:207
  7.2 8.6 %collective-permute-start = (bf16[64,896]{1,0:T(8,128)(2,1)}, bf16[64,896]{1,0:T(8,128)(2,1)S(1)}, u32[]{:S(2)}, u32[]{:S(2)}) collective-permute-start(bf16[64,896]{1,0:T(8,128)(2,1)} %bitcast.51), channel_id=1, source_target_pairs={{0,896},{8,904},{16,912},{24,920},{32,928},{40,936},{48,944},{56,9... | collective-permute-start | bytes 344072 | tf_op jit(solution)/shard_map/ppermute | solution.py:189
  9.2 8.1 %collective-permute-start.1 = (bf16[64,896]{1,0:T(8,128)(2,1)}, bf16[64,896]{1,0:T(8,128)(2,1)S(1)}, u32[]{:S(2)}, u32[]{:S(2)}) collective-permute-start(bf16[64,896]{1,0:T(8,128)(2,1)} %bitcast.52), channel_id=1, source_target_pairs={{0,128},{8,136},{16,144},{24,152},{32,160},{40,168},{48,176},{56,1... | collective-permute-start | bytes 344072 | tf_op jit(solution)/shard_map/ppermute | solution.py:189
  18.1 133.7 %reduce-scatter.2.cloned.1.call-start = ((), (), s32[]{:S(2)}) async-start(), calls=%async_computation.3 | async-start | bytes 2949120 | tf_op jit(solution)/shard_map/reduce_scatter | solution.py:262
  18.1 24.3 %collective-permute-start.4 = (bf16[136,896]{1,0:T(8,128)(2,1)S(1)}, bf16[136,896]{1,0:T(8,128)(2,1)S(1)}, u32[]{:S(2)}, u32[]{:S(2)}) collective-permute-start(bf16[136,896]{1,0:T(8,128)(2,1)S(1)} %pad_maximum_fusion.refs_2_), channel_id=1, source_target_pairs={{0,8},{8,0},{16,24},{24,16},{32,40},{40,32},{48,56},{56,48},{64,72... | collective-permute-start | bytes 731144 | tf_op jit(solution)/shard_map/ppermute | solution.py:189
  35.3 8.8 %collective-permute-start.3 = (bf16[136,896]{1,0:T(8,128)(2,1)S(1)}, bf16[136,896]{1,0:T(8,128)(2,1)S(1)}, u32[]{:S(2)}, u32[]{:S(2)}) collective-permute-start(bf16[136,896]{1,0:T(8,128)(2,1)S(1)} %pad_maximum_fusion.refs_2_), channel_id=1, source_target_pairs={{0,112},{8,120},{16,0},{24,8},{32,16},{40,24},{48,32},{56,40},{64,... | collective-permute-start | bytes 731144 | tf_op jit(solution)/shard_map/ppermute | solution.py:214
  40.5 9.3 %collective-permute-start.2 = (bf16[136,896]{1,0:T(8,128)(2,1)S(1)}, bf16[136,896]{1,0:T(8,128)(2,1)S(1)}, u32[]{:S(2)}, u32[]{:S(2)}) collective-permute-start(bf16[136,896]{1,0:T(8,128)(2,1)S(1)} %pad_maximum_fusion.refs_2_), channel_id=1, source_target_pairs={{0,16},{8,24},{16,32},{24,40},{32,48},{40,56},{48,64},{56,72},{64,... | collective-permute-start | bytes 731144 | tf_op jit(solution)/shard_map/ppermute | solution.py:213
  49.8 8.1 %collective-permute-start.7 = (bf16[136,896]{1,0:T(8,128)(2,1)S(1)}, bf16[136,896]{1,0:T(8,128)(2,1)S(1)}, u32[]{:S(2)}, u32[]{:S(2)}) collective-permute-start(bf16[136,896]{1,0:T(8,128)(2,1)S(1)} %collective-permute-done.4.refs_3_), channel_id=1, source_target_pairs={{0,112},{8,120},{16,0},{24,8},{32,16},{40,24},{48,32},{56,40},{64,... | collective-permute-start | bytes 731144 | tf_op jit(solution)/shard_map/ppermute | solution.py:223
  51.7 12.9 %collective-permute-start.10 = (bf16[136,896]{1,0:T(8,128)(2,1)S(1)}, bf16[136,896]{1,0:T(8,128)(2,1)S(1)}, u32[]{:S(2)}, u32[]{:S(2)}) collective-permute-start(bf16[136,896]{1,0:T(8,128)(2,1)S(1)} %collective-permute-done.2.refs_0_), channel_id=1, source_target_pairs={{0,16},{8,24},{16,32},{24,40},{32,48},{40,56},{48,64},{56,72},{64,... | collective-permute-start | bytes 731144 | tf_op jit(solution)/shard_map/ppermute | solution.py:218
  55.7 13.0 %collective-permute-start.14 = (bf16[136,896]{1,0:T(8,128)(2,1)S(1)}, bf16[136,896]{1,0:T(8,128)(2,1)S(1)}, u32[]{:S(2)}, u32[]{:S(2)}) collective-permute-start(bf16[136,896]{1,0:T(8,128)(2,1)S(1)} %collective-permute-done.4.refs_3_), channel_id=1, source_target_pairs={{0,16},{8,24},{16,32},{24,40},{32,48},{40,56},{48,64},{56,72},{64,... | collective-permute-start | bytes 731144 | tf_op jit(solution)/shard_map/ppermute | solution.py:222
  57.9 12.7 %collective-permute-start.8 = (bf16[136,896]{1,0:T(8,128)(2,1)S(1)}, bf16[136,896]{1,0:T(8,128)(2,1)S(1)}, u32[]{:S(2)}, u32[]{:S(2)}) collective-permute-start(bf16[136,896]{1,0:T(8,128)(2,1)S(1)} %collective-permute-done.7.refs_5_), channel_id=1, source_target_pairs={{0,112},{8,120},{16,0},{24,8},{32,16},{40,24},{48,32},{56,40},{64,... | collective-permute-start | bytes 731144 | tf_op jit(solution)/shard_map/ppermute | solution.py:223
  62.7 13.0 %collective-permute-start.5 = (bf16[136,896]{1,0:T(8,128)(2,1)S(1)}, bf16[136,896]{1,0:T(8,128)(2,1)S(1)}, u32[]{:S(2)}, u32[]{:S(2)}) collective-permute-start(bf16[136,896]{1,0:T(8,128)(2,1)S(1)} %collective-permute-done.3.refs_4_), channel_id=1, source_target_pairs={{0,112},{8,120},{16,0},{24,8},{32,16},{40,24},{48,32},{56,40},{64,... | collective-permute-start | bytes 731144 | tf_op jit(solution)/shard_map/ppermute | solution.py:220
  64.7 13.0 %collective-permute-start.11 = (bf16[136,896]{1,0:T(8,128)(2,1)S(1)}, bf16[136,896]{1,0:T(8,128)(2,1)S(1)}, u32[]{:S(2)}, u32[]{:S(2)}) collective-permute-start(bf16[136,896]{1,0:T(8,128)(2,1)S(1)} %collective-permute-done.10.refs_6_), channel_id=1, source_target_pairs={{0,16},{8,24},{16,32},{24,40},{32,48},{40,56},{48,64},{56,72},{64,... | collective-permute-start | bytes 731144 | tf_op jit(solution)/shard_map/ppermute | solution.py:218
  68.6 13.0 %collective-permute-start.15 = (bf16[136,896]{1,0:T(8,128)(2,1)S(1)}, bf16[136,896]{1,0:T(8,128)(2,1)S(1)}, u32[]{:S(2)}, u32[]{:S(2)}) collective-permute-start(bf16[136,896]{1,0:T(8,128)(2,1)S(1)} %collective-permute-done.14.refs_1_), channel_id=1, source_target_pairs={{0,16},{8,24},{16,32},{24,40},{32,48},{40,56},{48,64},{56,72},{64,... | collective-permute-start | bytes 731144 | tf_op jit(solution)/shard_map/ppermute | solution.py:222
  70.6 13.0 %collective-permute-start.9 = (bf16[136,896]{1,0:T(8,128)(2,1)S(1)}, bf16[136,896]{1,0:T(8,128)(2,1)S(1)}, u32[]{:S(2)}, u32[]{:S(2)}) collective-permute-start(bf16[136,896]{1,0:T(8,128)(2,1)S(1)} %collective-permute-done.8.refs_7_), channel_id=1, source_target_pairs={{0,112},{8,120},{16,0},{24,8},{32,16},{40,24},{48,32},{56,40},{64,... | collective-permute-start | bytes 731144 | tf_op jit(solution)/shard_map/ppermute | solution.py:223
  75.7 21.7 %collective-permute-start.6 = (bf16[136,896]{1,0:T(8,128)(2,1)S(1)}, bf16[136,896]{1,0:T(8,128)(2,1)S(1)}, u32[]{:S(2)}, u32[]{:S(2)}) collective-permute-start(bf16[136,896]{1,0:T(8,128)(2,1)S(1)} %collective-permute-done.5.refs_6_), channel_id=1, source_target_pairs={{0,112},{8,120},{16,0},{24,8},{32,16},{40,24},{48,32},{56,40},{64,... | collective-permute-start | bytes 731144 | tf_op jit(solution)/shard_map/ppermute | solution.py:220
  77.6 19.8 %collective-permute-start.12 = (bf16[136,896]{1,0:T(8,128)(2,1)S(1)}, bf16[136,896]{1,0:T(8,128)(2,1)S(1)}, u32[]{:S(2)}, u32[]{:S(2)}) collective-permute-start(bf16[136,896]{1,0:T(8,128)(2,1)S(1)} %collective-permute-done.11.refs_4_), channel_id=1, source_target_pairs={{0,16},{8,24},{16,32},{24,40},{32,48},{40,56},{48,64},{56,72},{64,... | collective-permute-start | bytes 731144 | tf_op jit(solution)/shard_map/ppermute | solution.py:218
  81.6 15.8 %collective-permute-start.16 = (bf16[136,896]{1,0:T(8,128)(2,1)S(1)}, bf16[136,896]{1,0:T(8,128)(2,1)}, u32[]{:S(2)}, u32[]{:S(2)}) collective-permute-start(bf16[136,896]{1,0:T(8,128)(2,1)S(1)} %collective-permute-done.15.refs_7_), channel_id=1, source_target_pairs={{0,16},{8,24},{16,32},{24,40},{32,48},{40,56},{48,64},{56,72},{64,... | collective-permute-start | bytes 731144 | tf_op jit(solution)/shard_map/ppermute | solution.py:222
  83.5 13.9 %collective-permute-start.13 = (bf16[136,896]{1,0:T(8,128)(2,1)S(1)}, bf16[136,896]{1,0:T(8,128)(2,1)}, u32[]{:S(2)}, u32[]{:S(2)}) collective-permute-start(bf16[136,896]{1,0:T(8,128)(2,1)S(1)} %collective-permute-done.9.refs_1_), channel_id=1, source_target_pairs={{0,112},{8,120},{16,0},{24,8},{32,16},{40,24},{48,32},{56,40},{64,... | collective-permute-start | bytes 731144 | tf_op jit(solution)/shard_map/ppermute | solution.py:223
  88.7 1.5 copy-start
  90.2 0.6 copy-start.4
  90.8 6.6 %copy-start.1 = (bf16[1,1,1024,896]{3,2,1,0:T(8,128)(2,1)S(1)}, bf16[1,1,1024,896]{3,2,1,0:T(8,128)(2,1)}, u32[]{:S(2)}) copy-start(bf16[1,1,1024,896]{3,2,1,0:T(8,128)(2,1)} %param.15) | copy-start | bytes 5505028
  96.8 0.6 copy-start.2
  104.0 0.6 copy-start.3
Sparse Core Ops, SparseCore 0:
  18.2 58.7 all-gather.1
  104.7 47.0 reduce-scatter.1

commit v4 on v2

--- a/solution.py
+++ b/solution.py
@@ -27,29 +27,12 @@
     out[...] = buf[...].astype(out.dtype)
 
 
-def expert_kernel(blocks, tok, top, cap, info, *refs):
-    msgs = refs[:blocks]
-    w_hbm, saved_hbm, part_hbm, slot_ref, gate_ref = refs[blocks : blocks + 5]
-    rows, rows16, gcol, meta, w_ref, saved_ref, part_ref, w_sem, saved_sem, part_sem = refs[blocks + 5 :]
-    slots = blocks * cap
-    lanes = 2 * tok
-    tiles = w_sem.shape[0]
-    tile = w_ref.shape[0] // tiles
-    parts = [pl.ds(i * tile, tile) for i in range(tiles)]
-    fetched = []
-    for i, at in enumerate(parts):
-        pair = (
-            pltpu.make_async_copy(w_hbm.at[at], w_ref.at[at], w_sem.at[i]),
-            pltpu.make_async_copy(saved_hbm.at[at], saved_ref.at[at], saved_sem.at[i]),
-        )
-        for copy in pair:
-            copy.start()
-        fetched.append(pair)
-
+def placements(msgs, tok, top, cap, expert, meta):
+    blocks, lanes = len(msgs), 2 * tok
     for b in range(blocks):
         meta[b * META : (b + 1) * META, :] = msgs[b][lanes : lanes + META, : top * tok].astype(f32)
     vals = meta[...]
-    mine = (vals == info[0].astype(f32)).astype(f32)
+    mine = (vals == expert.astype(f32)).astype(f32)
     t_in = lax.rem(lax.broadcasted_iota(jnp.int32, (top * tok, lanes), 0), tok)
     t_out = lax.rem(lax.broadcasted_iota(jnp.int32, (top * tok, lanes), 1), tok)
     same = (t_in == t_out).astype(f32).astype(bf16)
@@ -62,14 +45,47 @@
     rising = lax.broadcasted_iota(jnp.int32, (1, lanes), 1) >= tok
     shift = jnp.where(rising, float(cap), 0.0)
     slot_id = lax.broadcasted_iota(jnp.int32, (2 * cap, lanes), 0).astype(f32)
+    result = []
     for b in range(blocks):
         r = b * META
         name = jnp.where(rising, named[r + 2 : r + 3], named[r : r + 1])
         pos = jnp.where(rising, place[r + 2 : r + 3], place[r : r + 1])
         gate = jnp.where(rising, gates[r + 3 : r + 4], gates[r + 1 : r + 2])
         target = jnp.where(name > 0.5, pos + shift, -1.0)
-        put = (slot_id == target).astype(f32)
-        got = jnp.dot(put.astype(bf16), msgs[b][:lanes, :], preferred_element_type=f32)
+        result.append(((slot_id == target).astype(f32), gate))
+    return result
+
+
+def early_kernel(blocks, tok, top, cap, info, *refs):
+    msgs, (out, meta) = refs[:blocks], refs[blocks:]
+    for b, (put, _) in enumerate(placements(msgs, tok, top, cap, info[0], meta)):
+        got = jnp.dot(put.astype(bf16), msgs[b][: 2 * tok, :], preferred_element_type=f32)
+        out[b * 2 * cap : (b + 1) * 2 * cap, :] = got.astype(bf16)
+
+
+def expert_kernel(blocks, early, tok, top, cap, info, *refs):
+    msgs = refs[:blocks]
+    done_ref, w_hbm, saved_hbm, part_hbm, slot_ref, gate_ref = refs[blocks : blocks + 6]
+    rows, rows16, gcol, meta, w_ref, saved_ref, part_ref, w_sem, saved_sem, part_sem = refs[blocks + 6 :]
+    slots = blocks * cap
+    tiles = saved_sem.shape[0]
+    tile = w_ref.shape[0] // tiles
+    parts = [pl.ds(i * tile, tile) for i in range(tiles)]
+    fetched = []
+    for i, at in enumerate(parts):
+        pair = (
+            pltpu.make_async_copy(w_hbm.at[at], w_ref.at[at], w_sem.at[i]),
+            pltpu.make_async_copy(saved_hbm.at[at], saved_ref.at[at], saved_sem.at[i]),
+        )
+        for copy in pair:
+            copy.start()
+        fetched.append(pair)
+
+    for b, (put, gate) in enumerate(placements(msgs, tok, top, cap, info[0], meta)):
+        if b < early:
+            got = done_ref[b * 2 * cap : (b + 1) * 2 * cap, :].astype(f32)
+        else:
+            got = jnp.dot(put.astype(bf16), msgs[b][: 2 * tok, :], preferred_element_type=f32)
         col = jnp.broadcast_to(jnp.sum(put * gate, axis=1, keepdims=True), (2 * cap, gcol.shape[2]))
         at = pl.ds(pl.multiple_of(info[1 + b] * cap, 8), cap)
         for m in range(2):
@@ -77,26 +93,22 @@
             gcol[m, at, :] = col[m * cap : (m + 1) * cap]
     first = (lax.broadcasted_iota(jnp.int32, (8, gcol.shape[2]), 1) == 0).astype(f32).astype(bf16)
     for m in range(2):
-        rows16[m] = rows[m].astype(bf16)
-        gate_ref[:, m * slots : (m + 1) * slots] = lax.dot_general(
-            first, gcol[m].astype(bf16), NT, preferred_element_type=f32
-        )
+        cols = slice(m * slots, (m + 1) * slots)
+        rows16[cols, :] = rows[m].astype(bf16)
+        gate_ref[:, cols] = lax.dot_general(first, gcol[m].astype(bf16), NT, preferred_element_type=f32)
 
     sent = []
     for i, at in enumerate(parts):
-        for copy in fetched[i]:
-            copy.wait()
-        w = w_ref[at, :]
-        for m in range(2):
-            cols = slice(m * slots, (m + 1) * slots)
-            part = lax.dot_general(w, rows16[m], NT, preferred_element_type=f32).astype(bf16)
-            part_ref[at, cols] = part
-            prod = part.astype(f32) * saved_ref[at, cols].astype(f32)
-            total = jnp.sum(prod.reshape(-1, 8, slots), axis=0)
-            slot_ref[:, cols] = total if i == 0 else slot_ref[:, cols] + total
+        fetched[i][0].wait()
+        part = lax.dot_general(w_ref[at, :], rows16[...], NT, preferred_element_type=f32).astype(bf16)
+        part_ref[at, :] = part
         copy = pltpu.make_async_copy(part_ref.at[at], part_hbm.at[at], part_sem.at[i])
         copy.start()
         sent.append(copy)
+        fetched[i][1].wait()
+        prod = part.astype(f32) * saved_ref[at, :].astype(f32)
+        total = jnp.sum(prod.reshape(-1, 8, 2 * slots), axis=0)
+        slot_ref[...] = total if i == 0 else slot_ref[...] + total
     for copy in sent:
         copy.wait()
 
@@ -205,13 +217,29 @@
     for t in range(1, half):
         far_rise, far_fall = step(far_rise, far_fall, 1 - column, t)
     step(None, far_fall, 1 - column, half)
-    info = jnp.stack([me] + index).astype(jnp.int32)
+    late = (7, 8, 13, 14, 15)
+    order = [i for i in range(blocks) if i not in late] + list(late)
+    early = blocks - len(late)
+    msgs = [msgs[i] for i in order]
+    info = jnp.stack([me] + [index[i] for i in order]).astype(jnp.int32)
 
     tiles = max(1, ff // 256)
-    vmem, hbm = pl.BlockSpec(memory_space=pltpu.VMEM), pl.BlockSpec(memory_space=pltpu.HBM)
+    smem, vmem = pl.BlockSpec(memory_space=pltpu.SMEM), pl.BlockSpec(memory_space=pltpu.VMEM)
+    hbm = pl.BlockSpec(memory_space=pltpu.HBM)
+    done = pl.pallas_call(
+        functools.partial(early_kernel, early, tok, top, cap),
+        in_specs=[smem] + [vmem] * early,
+        out_specs=vmem,
+        out_shape=jax.ShapeDtypeStruct((early * 2 * cap, width), bf16),
+        scratch_shapes=[pltpu.VMEM((early * META, top * tok), f32)],
+        compiler_params=pltpu.CompilerParams(vmem_limit_bytes=32 * 1024 * 1024),
+        cost_estimate=pl.CostEstimate(
+            flops=4 * ff * width * slots, bytes_accessed=8 * 1024 * 1024, transcendentals=0
+        ),
+    )(info, *msgs[:early])
     partial, slot_part, gates = pl.pallas_call(
-        functools.partial(expert_kernel, blocks, tok, top, cap),
-        in_specs=[pl.BlockSpec(memory_space=pltpu.SMEM)] + [vmem] * blocks + [hbm, hbm],
+        functools.partial(expert_kernel, blocks, early, tok, top, cap),
+        in_specs=[smem] + [vmem] * blocks + [vmem, hbm, hbm],
         out_specs=[hbm, vmem, vmem],
         out_shape=[
             jax.ShapeDtypeStruct((ff, 2 * slots), bf16),
@@ -220,7 +248,7 @@
         ],
         scratch_shapes=[
             pltpu.VMEM((2, slots, width), f32),
-            pltpu.VMEM((2, slots, width), bf16),
+            pltpu.VMEM((2 * slots, width), bf16),
             pltpu.VMEM((2, slots, 128), f32),
             pltpu.VMEM((blocks * META, top * tok), f32),
             pltpu.VMEM((ff, width), bf16),
@@ -230,11 +258,11 @@
             pltpu.SemaphoreType.DMA((tiles,)),
             pltpu.SemaphoreType.DMA((tiles,)),
         ],
-        compiler_params=pltpu.CompilerParams(vmem_limit_bytes=50 * 1024 * 1024),
+        compiler_params=pltpu.CompilerParams(vmem_limit_bytes=48 * 1024 * 1024),
         cost_estimate=pl.CostEstimate(
             flops=4 * ff * width * slots, bytes_accessed=16 * 1024 * 1024, transcendentals=0
         ),
-    )(info, *msgs, down_weight.reshape(ff, width), saved_all)
+    )(info, *msgs, done, down_weight.reshape(ff, width), saved_all)
 
     terms = lax.psum_scatter(partial, "dp", scatter_dimension=0, tiled=True)
     slot_grad = lax.psum(jnp.sum(slot_part, axis=0), "dp")

time: 160 us -> 162 us (1.012)
  waiting for transfers between devices: 34.5 us -> 30.9 us
  local copies, waits for them, and re-layouts: 0.88 us -> 3.61 us
  Pallas kernels: 11.7 us -> 14 us
    pallas_call x1 -> x2, Pallas kernels: 8.58 us -> 10.8 us  [the longest x1 8.79 us: shards(): pl.pallas_call(functools.partial(expert_kernel, blocks, early, tok, top,...]
    unnamed x2 -> x8, local copies, waits for them, and re-layouts: 0.6 us -> 2.58 us
    ppermute x7, waiting for transfers between devices: 9 us -> 7.2 us  [step(): rise = lax.ppermute(rise, 'expert', up)]
  transfers between devices with their start and end apart: 20 -> 20, of which waited for: 8 -> 7; matrix products, arithmetic and copies ran while one was open for 1% -> 2% of each run, Pallas kernels for 2% -> 3%
where the time goes in v4:
time: 162 us; the launch traced here: 161 us
  starting transfers between devices  74 us (46%)
  waiting for transfers between devices  30.9 us (19%)
  blocking collectives  19.6 us (12%)
  between operations  14.5 us (9%)
  Pallas kernels  14 us (9%)
  other arithmetic  4.28 us (3%)
  local copies, waits for them, and re-layouts  3.61 us (2%)
    ppermute x7, starting transfers between devices, step(): fall = lax.ppermute(fall, 'expert', down)  40.8 us
    psum x1, blocking collectives, shards(): slot_grad = lax.psum(jnp.sum(slot_part, axis=0), 'dp')  19.6 us
    ppermute x7, starting transfers between devices, step(): rise = lax.ppermute(rise, 'expert', up)  17.1 us
    all_to_all x1, waiting for transfers between devices, shards(): lax.all_to_all(home, 'expert', split_axis=0, concat_axis=0, tiled=True)  11.5 us
    ppermute x3, starting transfers between devices, hop(): return lax.ppermute(array, ('section', 'expert'), pairs)  10.1 us
    pallas_call x1, Pallas kernels, shards(): pl.pallas_call(functools.partial(expert_kernel, blocks, early, tok, top,...  8.79 us
    ppermute x7, waiting for transfers between devices, step(): rise = lax.ppermute(rise, 'expert', up)  7.2 us
    ppermute x7, waiting for transfers between devices, step(): fall = lax.ppermute(fall, 'expert', down)  5.91 us
  transfers between devices with their start and end apart: 20, of which 7 were waited for; matrix products, arithmetic and copies ran while one was open for 2% of the time, Pallas kernels for 3%

profile of v4, /device:TPU:6, one launch (start us, length us, event | category | flops | bytes accessed | tf_op | source)
XLA Modules:
  0.0 160.8 jit_solution(7108081195286546847)
XLA Ops:
  9.1 2.4 %collective-permute-start.1 = (bf16[64,896]{1,0:T(8,128)(2,1)}, bf16[64,896]{1,0:T(8,128)(2,1)S(1)}, u32[]{:S(2)}, u32[]{:S(2)}) collective-permute-start(bf16[64,896]{1,0:T(8,128)(2,1)} %bitcast.60), channel_id=1, source_target_pairs={{0,128},{8,136},{16,144},{24,152},{32,160},{40,168},{48,176},{56,1... | collective-permute-start | bytes 344072 | tf_op jit(solution)/shard_map/ppermute | solution.py:174
  16.3 5.8 %collective-permute-start.4 = (bf16[136,896]{1,0:T(8,128)(2,1)S(1)}, bf16[136,896]{1,0:T(8,128)(2,1)S(1)}, u32[]{:S(2)}, u32[]{:S(2)}) collective-permute-start(bf16[136,896]{1,0:T(8,128)(2,1)S(1)} %pad_maximum_fusion.1.refs_0_), channel_id=1, source_target_pairs={{0,8},{8,0},{16,24},{24,16},{32,40},{40,32},{48,56},{56,48},{64,72... | collective-permute-start | bytes 731144 | tf_op jit(solution)/shard_map/ppermute | solution.py:174
  22.1 17.3 %collective-permute-start.3 = (bf16[136,896]{1,0:T(8,128)(2,1)S(1)}, bf16[136,896]{1,0:T(8,128)(2,1)S(1)}, u32[]{:S(2)}, u32[]{:S(2)}) collective-permute-start(bf16[136,896]{1,0:T(8,128)(2,1)S(1)} %pad_maximum_fusion.1.refs_0_), channel_id=1, source_target_pairs={{0,112},{8,120},{16,0},{24,8},{32,16},{40,24},{48,32},{56,40},{64,... | collective-permute-start | bytes 731144 | tf_op jit(solution)/shard_map/ppermute | solution.py:203
  39.4 1.9 %collective-permute-start.2 = (bf16[136,896]{1,0:T(8,128)(2,1)S(1)}, bf16[136,896]{1,0:T(8,128)(2,1)S(1)}, u32[]{:S(2)}, u32[]{:S(2)}) collective-permute-start(bf16[136,896]{1,0:T(8,128)(2,1)S(1)} %pad_maximum_fusion.1.refs_0_), channel_id=1, source_target_pairs={{0,16},{8,24},{16,32},{24,40},{32,48},{40,56},{48,64},{56,72},{64,... | collective-permute-start | bytes 731144 | tf_op jit(solution)/shard_map/ppermute | solution.py:199
  41.3 4.2 %collective-permute-done.3.refs_3_ = bf16[136,896]{1,0:T(8,128)(2,1)S(1)} collective-permute-done((bf16[136,896]{1,0:T(8,128)(2,1)S(1)}, bf16[136,896]{1,0:T(8,128)(2,1)S(1)}, u32[]{:S(2)}, u32[]{:S(2)}) %collective-permute-start.3) | collective-permute-done | bytes 243744 | tf_op jit(solution)/shard_map/ppermute | solution.py:203
  45.5 5.3 %collective-permute-done.2.refs_2_ = bf16[136,896]{1,0:T(8,128)(2,1)S(1)} collective-permute-done((bf16[136,896]{1,0:T(8,128)(2,1)S(1)}, bf16[136,896]{1,0:T(8,128)(2,1)S(1)}, u32[]{:S(2)}, u32[]{:S(2)}) %collective-permute-start.2) | collective-permute-done | bytes 243744 | tf_op jit(solution)/shard_map/ppermute | solution.py:199
  50.8 3.6 %collective-permute-start.9 = (bf16[136,896]{1,0:T(8,128)(2,1)S(1)}, bf16[136,896]{1,0:T(8,128)(2,1)S(1)}, u32[]{:S(2)}, u32[]{:S(2)}) collective-permute-start(bf16[136,896]{1,0:T(8,128)(2,1)S(1)} %collective-permute-done.4.refs_1_), channel_id=1, source_target_pairs={{0,112},{8,120},{16,0},{24,8},{32,16},{40,24},{48,32},{56,40},{64,... | collective-permute-start | bytes 731144 | tf_op jit(solution)/shard_map/ppermute | solution.py:203
  54.5 2.2 %collective-permute-start.5 = (bf16[136,896]{1,0:T(8,128)(2,1)S(1)}, bf16[136,896]{1,0:T(8,128)(2,1)S(1)}, u32[]{:S(2)}, u32[]{:S(2)}) collective-permute-start(bf16[136,896]{1,0:T(8,128)(2,1)S(1)} %collective-permute-done.2.refs_2_), channel_id=1, source_target_pairs={{0,16},{8,24},{16,32},{24,40},{32,48},{40,56},{48,64},{56,72},{64,... | collective-permute-start | bytes 731144 | tf_op jit(solution)/shard_map/ppermute | solution.py:199
  56.7 1.9 %collective-permute-start.8 = (bf16[136,896]{1,0:T(8,128)(2,1)S(1)}, bf16[136,896]{1,0:T(8,128)(2,1)S(1)}, u32[]{:S(2)}, u32[]{:S(2)}) collective-permute-start(bf16[136,896]{1,0:T(8,128)(2,1)S(1)} %collective-permute-done.4.refs_1_), channel_id=1, source_target_pairs={{0,16},{8,24},{16,32},{24,40},{32,48},{40,56},{48,64},{56,72},{64,... | collective-permute-start | bytes 731144 | tf_op jit(solution)/shard_map/ppermute | solution.py:199
  60.3 5.2 %collective-permute-start.11 = (bf16[136,896]{1,0:T(8,128)(2,1)S(1)}, bf16[136,896]{1,0:T(8,128)(2,1)S(1)}, u32[]{:S(2)}, u32[]{:S(2)}) collective-permute-start(bf16[136,896]{1,0:T(8,128)(2,1)S(1)} %collective-permute-done.9.refs_8_), channel_id=1, source_target_pairs={{0,112},{8,120},{16,0},{24,8},{32,16},{40,24},{48,32},{56,40},{64,... | collective-permute-start | bytes 731144 | tf_op jit(solution)/shard_map/ppermute | solution.py:203
  65.5 1.9 %collective-permute-start.6 = (bf16[136,896]{1,0:T(8,128)(2,1)S(1)}, bf16[136,896]{1,0:T(8,128)(2,1)}, u32[]{:S(2)}, u32[]{:S(2)}) collective-permute-start(bf16[136,896]{1,0:T(8,128)(2,1)S(1)} %collective-permute-done.3.refs_3_), channel_id=1, source_target_pairs={{0,112},{8,120},{16,0},{24,8},{32,16},{40,24},{48,32},{56,40},{64,... | collective-permute-start | bytes 731144 | tf_op jit(solution)/shard_map/ppermute | solution.py:203
  67.4 3.9 %collective-permute-start.7 = (bf16[136,896]{1,0:T(8,128)(2,1)S(1)}, bf16[136,896]{1,0:T(8,128)(2,1)}, u32[]{:S(2)}, u32[]{:S(2)}) collective-permute-start(bf16[136,896]{1,0:T(8,128)(2,1)S(1)} %collective-permute-done.5.refs_4_), channel_id=1, source_target_pairs={{0,16},{8,24},{16,32},{24,40},{32,48},{40,56},{48,64},{56,72},{64,... | collective-permute-start | bytes 731144 | tf_op jit(solution)/shard_map/ppermute | solution.py:199
  71.4 1.9 %collective-permute-start.10 = (bf16[136,896]{1,0:T(8,128)(2,1)S(1)}, bf16[136,896]{1,0:T(8,128)(2,1)}, u32[]{:S(2)}, u32[]{:S(2)}) collective-permute-start(bf16[136,896]{1,0:T(8,128)(2,1)S(1)} %collective-permute-done.8.refs_7_), channel_id=1, source_target_pairs={{0,16},{8,24},{16,32},{24,40},{32,48},{40,56},{48,64},{56,72},{64,... | collective-permute-start | bytes 731144 | tf_op jit(solution)/shard_map/ppermute | solution.py:199
  73.3 5.1 %collective-permute-start.15 = (bf16[136,896]{1,0:T(8,128)(2,1)S(1)}, bf16[136,896]{1,0:T(8,128)(2,1)}, u32[]{:S(2)}, u32[]{:S(2)}) collective-permute-start(bf16[136,896]{1,0:T(8,128)(2,1)S(1)} %collective-permute-done.11.refs_10_), channel_id=1, source_target_pairs={{0,112},{8,120},{16,0},{24,8},{32,16},{40,24},{48,32},{56,40},{64,... | collective-permute-start | bytes 731144 | tf_op jit(solution)/shard_map/ppermute | solution.py:203
  78.5 2.5 %collective-permute-start.12 = (bf16[136,896]{1,0:T(8,128)(2,1)}, bf16[136,896]{1,0:T(8,128)(2,1)}, u32[]{:S(2)}, u32[]{:S(2)}) collective-permute-start(bf16[136,896]{1,0:T(8,128)(2,1)} %collective-permute-done.6.refs_5_), channel_id=1, source_target_pairs={{0,112},{8,120},{16,0},{24,8},{32,16},{40,24},{48,32},{56,40},{64,... | collective-permute-start | bytes 731144 | tf_op jit(solution)/shard_map/ppermute | solution.py:203
  81.0 3.3 %collective-permute-start.13 = (bf16[136,896]{1,0:T(8,128)(2,1)}, bf16[136,896]{1,0:T(8,128)(2,1)}, u32[]{:S(2)}, u32[]{:S(2)}) collective-permute-start(bf16[136,896]{1,0:T(8,128)(2,1)} %collective-permute-done.7.refs_6_), channel_id=1, source_target_pairs={{0,16},{8,24},{16,32},{24,40},{32,48},{40,56},{48,64},{56,72},{64,... | collective-permute-start | bytes 731144 | tf_op jit(solution)/shard_map/ppermute | solution.py:199
  84.4 1.9 %collective-permute-start.14 = (bf16[136,896]{1,0:T(8,128)(2,1)}, bf16[136,896]{1,0:T(8,128)(2,1)}, u32[]{:S(2)}, u32[]{:S(2)}) collective-permute-start(bf16[136,896]{1,0:T(8,128)(2,1)} %collective-permute-done.10.refs_9_), channel_id=1, source_target_pairs={{0,16},{8,24},{16,32},{24,40},{32,48},{40,56},{48,64},{56,72},{64,... | collective-permute-start | bytes 731144 | tf_op jit(solution)/shard_map/ppermute | solution.py:199
  86.3 5.1 %collective-permute-start.16 = (bf16[136,896]{1,0:T(8,128)(2,1)}, bf16[136,896]{1,0:T(8,128)(2,1)}, u32[]{:S(2)}, u32[]{:S(2)}) collective-permute-start(bf16[136,896]{1,0:T(8,128)(2,1)} %collective-permute-done.15.refs_14_), channel_id=1, source_target_pairs={{0,112},{8,120},{16,0},{24,8},{32,16},{40,24},{48,32},{56,40},{64,... | collective-permute-start | bytes 731144 | tf_op jit(solution)/shard_map/ppermute | solution.py:203
  91.7 2.0 %shard_map.121.refs_16_ = bf16[880,896]{1,0:T(8,128)(2,1)S(1)} custom-call(s32[17]{0:T(128)S(1)} %stack.68.info, bf16[136,896]{1,0:T(8,128)(2,1)S(1)} %pad_maximum_fusion.1.refs_0_, bf16[136,896]{1,0:T(8,128)(2,1)S(1)} %collective-permute-done.4.refs_1_, bf16[136,896]{1,0:T(8,128)(2,1)S(1)} %collective-permute-done.2.refs_2_, ...), custom_call_target="tpu_custom_call" | custom-call | flops 2348810240 | bytes 8388608 | tf_op jit(solution)/shard_map/pallas_call | solution.py:229
  95.6 8.8 %shard_map.122 = (bf16[1024,1280]{1,0:T(8,128)(2,1)}, f32[8,1280]{1,0:T(8,128)S(1)}, f32[8,1280]{1,0:T(8,128)S(1)}) custom-call(s32[17]{0:T(128)S(1)} %stack.68.info, bf16[136,896]{1,0:T(8,128)(2,1)S(1)} %pad_maximum_fusion.1.refs_0_, bf16[136,896]{1,0:T(8,128)(2,1)S(1)} %collective-permute-done.4.refs_1_, ...), custom_call_target="tpu_custom_call" | custom-call | flops 2348810240 | bytes 16777216 | tf_op jit(solution)/shard_map/pallas_call | solution.py:240
  106.6 19.6 %psum.7 = f32[16,1,80]{2,0,1:T(8,128)} all-reduce(f32[16,1,80]{2,0,1:T(8,128)S(1)} %all_to_all.7), channel_id=1, replica_groups=mesh['section'=8,'expert'=16,'dp'=8] {'dp'}, use_global_device_ids=true, to_apply=%region_2.3 | all-reduce | flops 1280 | bytes 10240 | tf_op jit(solution)/shard_map/psum | solution.py:268
  126.3 5.8 %all-to-all-start = ((f32[16,1,80]{2,1,0:T(1,128)}), f32[16,1,80]{2,1,0:T(1,128)S(1)}, u32[]{:S(2)}, u32[]{:S(2)}) async-start(f32[16,1,80]{2,1,0:T(1,128)} %bitcast.36), calls=%async_computation.1 | async-start | bytes 16384 | tf_op jit(solution)/shard_map/all_to_all | solution.py:270
  132.8 11.5 %all-to-all-done = f32[16,1,80]{2,1,0:T(1,128)S(1)} async-done(((f32[16,1,80]{2,1,0:T(1,128)}), f32[16,1,80]{2,1,0:T(1,128)S(1)}, u32[]{:S(2)}, u32[]{:S(2)}) %all-to-all-start) | async-done | bytes 5152 | tf_op jit(solution)/shard_map/all_to_all | solution.py:270
  146.7 5.5 %reduce-scatter.2.cloned.1.call-done = bf16[128,1280]{1,0:T(8,128)(2,1)} async-done(((bf16[1024,1280]{1,0:T(8,128)(2,1)}), bf16[128,1280]{1,0:T(8,128)(2,1)}) %reduce-scatter.2.cloned.1.call-update) | async-done | bytes 327696 | tf_op jit(solution)/shard_map/reduce_scatter | solution.py:267
  (40 shorter events, 17.4 us)
Async XLA Ops:
  7.2 88.4 %all-gather.2.cloned.1.call-start = ((), (), s32[]{:S(2)}) async-start(), calls=%async_computation.2 | async-start | bytes 2949120 | tf_op jit(solution)/shard_map/all_gather | solution.py:189
  7.2 7.5 %collective-permute-start = (bf16[64,896]{1,0:T(8,128)(2,1)}, bf16[64,896]{1,0:T(8,128)(2,1)S(1)}, u32[]{:S(2)}, u32[]{:S(2)}) collective-permute-start(bf16[64,896]{1,0:T(8,128)(2,1)} %bitcast.59), channel_id=1, source_target_pairs={{0,896},{8,904},{16,912},{24,920},{32,928},{40,936},{48,944},{56,9... | collective-permute-start | bytes 344072 | tf_op jit(solution)/shard_map/ppermute | solution.py:174
  9.1 6.3 %collective-permute-start.1 = (bf16[64,896]{1,0:T(8,128)(2,1)}, bf16[64,896]{1,0:T(8,128)(2,1)S(1)}, u32[]{:S(2)}, u32[]{:S(2)}) collective-permute-start(bf16[64,896]{1,0:T(8,128)(2,1)} %bitcast.60), channel_id=1, source_target_pairs={{0,128},{8,136},{16,144},{24,152},{32,160},{40,168},{48,176},{56,1... | collective-permute-start | bytes 344072 | tf_op jit(solution)/shard_map/ppermute | solution.py:174
  16.2 136.0 %reduce-scatter.2.cloned.1.call-start = ((), (), s32[]{:S(2)}) async-start(), calls=%async_computation.3 | async-start | bytes 2949120 | tf_op jit(solution)/shard_map/reduce_scatter | solution.py:267
  16.3 25.1 %collective-permute-start.4 = (bf16[136,896]{1,0:T(8,128)(2,1)S(1)}, bf16[136,896]{1,0:T(8,128)(2,1)S(1)}, u32[]{:S(2)}, u32[]{:S(2)}) collective-permute-start(bf16[136,896]{1,0:T(8,128)(2,1)S(1)} %pad_maximum_fusion.1.refs_0_), channel_id=1, source_target_pairs={{0,8},{8,0},{16,24},{24,16},{32,40},{40,32},{48,56},{56,48},{64,72... | collective-permute-start | bytes 731144 | tf_op jit(solution)/shard_map/ppermute | solution.py:174
  22.1 23.4 %collective-permute-start.3 = (bf16[136,896]{1,0:T(8,128)(2,1)S(1)}, bf16[136,896]{1,0:T(8,128)(2,1)S(1)}, u32[]{:S(2)}, u32[]{:S(2)}) collective-permute-start(bf16[136,896]{1,0:T(8,128)(2,1)S(1)} %pad_maximum_fusion.1.refs_0_), channel_id=1, source_target_pairs={{0,112},{8,120},{16,0},{24,8},{32,16},{40,24},{48,32},{56,40},{64,... | collective-permute-start | bytes 731144 | tf_op jit(solution)/shard_map/ppermute | solution.py:203
  39.4 11.4 %collective-permute-start.2 = (bf16[136,896]{1,0:T(8,128)(2,1)S(1)}, bf16[136,896]{1,0:T(8,128)(2,1)S(1)}, u32[]{:S(2)}, u32[]{:S(2)}) collective-permute-start(bf16[136,896]{1,0:T(8,128)(2,1)S(1)} %pad_maximum_fusion.1.refs_0_), channel_id=1, source_target_pairs={{0,16},{8,24},{16,32},{24,40},{32,48},{40,56},{48,64},{56,72},{64,... | collective-permute-start | bytes 731144 | tf_op jit(solution)/shard_map/ppermute | solution.py:199
  50.8 9.5 %collective-permute-start.9 = (bf16[136,896]{1,0:T(8,128)(2,1)S(1)}, bf16[136,896]{1,0:T(8,128)(2,1)S(1)}, u32[]{:S(2)}, u32[]{:S(2)}) collective-permute-start(bf16[136,896]{1,0:T(8,128)(2,1)S(1)} %collective-permute-done.4.refs_1_), channel_id=1, source_target_pairs={{0,112},{8,120},{16,0},{24,8},{32,16},{40,24},{48,32},{56,40},{64,... | collective-permute-start | bytes 731144 | tf_op jit(solution)/shard_map/ppermute | solution.py:203
  54.5 13.0 %collective-permute-start.5 = (bf16[136,896]{1,0:T(8,128)(2,1)S(1)}, bf16[136,896]{1,0:T(8,128)(2,1)S(1)}, u32[]{:S(2)}, u32[]{:S(2)}) collective-permute-start(bf16[136,896]{1,0:T(8,128)(2,1)S(1)} %collective-permute-done.2.refs_2_), channel_id=1, source_target_pairs={{0,16},{8,24},{16,32},{24,40},{32,48},{40,56},{48,64},{56,72},{64,... | collective-permute-start | bytes 731144 | tf_op jit(solution)/shard_map/ppermute | solution.py:199
  56.7 14.7 %collective-permute-start.8 = (bf16[136,896]{1,0:T(8,128)(2,1)S(1)}, bf16[136,896]{1,0:T(8,128)(2,1)S(1)}, u32[]{:S(2)}, u32[]{:S(2)}) collective-permute-start(bf16[136,896]{1,0:T(8,128)(2,1)S(1)} %collective-permute-done.4.refs_1_), channel_id=1, source_target_pairs={{0,16},{8,24},{16,32},{24,40},{32,48},{40,56},{48,64},{56,72},{64,... | collective-permute-start | bytes 731144 | tf_op jit(solution)/shard_map/ppermute | solution.py:199
  60.3 13.0 %collective-permute-start.11 = (bf16[136,896]{1,0:T(8,128)(2,1)S(1)}, bf16[136,896]{1,0:T(8,128)(2,1)S(1)}, u32[]{:S(2)}, u32[]{:S(2)}) collective-permute-start(bf16[136,896]{1,0:T(8,128)(2,1)S(1)} %collective-permute-done.9.refs_8_), channel_id=1, source_target_pairs={{0,112},{8,120},{16,0},{24,8},{32,16},{40,24},{48,32},{56,40},{64,... | collective-permute-start | bytes 731144 | tf_op jit(solution)/shard_map/ppermute | solution.py:203
  65.5 13.0 %collective-permute-start.6 = (bf16[136,896]{1,0:T(8,128)(2,1)S(1)}, bf16[136,896]{1,0:T(8,128)(2,1)}, u32[]{:S(2)}, u32[]{:S(2)}) collective-permute-start(bf16[136,896]{1,0:T(8,128)(2,1)S(1)} %collective-permute-done.3.refs_3_), channel_id=1, source_target_pairs={{0,112},{8,120},{16,0},{24,8},{32,16},{40,24},{48,32},{56,40},{64,... | collective-permute-start | bytes 731144 | tf_op jit(solution)/shard_map/ppermute | solution.py:203
  67.4 13.6 %collective-permute-start.7 = (bf16[136,896]{1,0:T(8,128)(2,1)S(1)}, bf16[136,896]{1,0:T(8,128)(2,1)}, u32[]{:S(2)}, u32[]{:S(2)}) collective-permute-start(bf16[136,896]{1,0:T(8,128)(2,1)S(1)} %collective-permute-done.5.refs_4_), channel_id=1, source_target_pairs={{0,16},{8,24},{16,32},{24,40},{32,48},{40,56},{48,64},{56,72},{64,... | collective-permute-start | bytes 731144 | tf_op jit(solution)/shard_map/ppermute | solution.py:199
  71.4 13.0 %collective-permute-start.10 = (bf16[136,896]{1,0:T(8,128)(2,1)S(1)}, bf16[136,896]{1,0:T(8,128)(2,1)}, u32[]{:S(2)}, u32[]{:S(2)}) collective-permute-start(bf16[136,896]{1,0:T(8,128)(2,1)S(1)} %collective-permute-done.8.refs_7_), channel_id=1, source_target_pairs={{0,16},{8,24},{16,32},{24,40},{32,48},{40,56},{48,64},{56,72},{64,... | collective-permute-start | bytes 731144 | tf_op jit(solution)/shard_map/ppermute | solution.py:199
  73.3 13.0 %collective-permute-start.15 = (bf16[136,896]{1,0:T(8,128)(2,1)S(1)}, bf16[136,896]{1,0:T(8,128)(2,1)}, u32[]{:S(2)}, u32[]{:S(2)}) collective-permute-start(bf16[136,896]{1,0:T(8,128)(2,1)S(1)} %collective-permute-done.11.refs_10_), channel_id=1, source_target_pairs={{0,112},{8,120},{16,0},{24,8},{32,16},{40,24},{48,32},{56,40},{64,... | collective-permute-start | bytes 731144 | tf_op jit(solution)/shard_map/ppermute | solution.py:203
  78.5 15.2 %collective-permute-start.12 = (bf16[136,896]{1,0:T(8,128)(2,1)}, bf16[136,896]{1,0:T(8,128)(2,1)}, u32[]{:S(2)}, u32[]{:S(2)}) collective-permute-start(bf16[136,896]{1,0:T(8,128)(2,1)} %collective-permute-done.6.refs_5_), channel_id=1, source_target_pairs={{0,112},{8,120},{16,0},{24,8},{32,16},{40,24},{48,32},{56,40},{64,... | collective-permute-start | bytes 731144 | tf_op jit(solution)/shard_map/ppermute | solution.py:203
  81.0 12.7 %collective-permute-start.13 = (bf16[136,896]{1,0:T(8,128)(2,1)}, bf16[136,896]{1,0:T(8,128)(2,1)}, u32[]{:S(2)}, u32[]{:S(2)}) collective-permute-start(bf16[136,896]{1,0:T(8,128)(2,1)} %collective-permute-done.7.refs_6_), channel_id=1, source_target_pairs={{0,16},{8,24},{16,32},{24,40},{32,48},{40,56},{48,64},{56,72},{64,... | collective-permute-start | bytes 731144 | tf_op jit(solution)/shard_map/ppermute | solution.py:199
  84.4 11.2 %collective-permute-start.14 = (bf16[136,896]{1,0:T(8,128)(2,1)}, bf16[136,896]{1,0:T(8,128)(2,1)}, u32[]{:S(2)}, u32[]{:S(2)}) collective-permute-start(bf16[136,896]{1,0:T(8,128)(2,1)} %collective-permute-done.10.refs_9_), channel_id=1, source_target_pairs={{0,16},{8,24},{16,32},{24,40},{32,48},{40,56},{48,64},{56,72},{64,... | collective-permute-start | bytes 731144 | tf_op jit(solution)/shard_map/ppermute | solution.py:199
  86.3 9.3 %collective-permute-start.16 = (bf16[136,896]{1,0:T(8,128)(2,1)}, bf16[136,896]{1,0:T(8,128)(2,1)}, u32[]{:S(2)}, u32[]{:S(2)}) collective-permute-start(bf16[136,896]{1,0:T(8,128)(2,1)} %collective-permute-done.15.refs_14_), channel_id=1, source_target_pairs={{0,112},{8,120},{16,0},{24,8},{32,16},{40,24},{48,32},{56,40},{64,... | collective-permute-start | bytes 731144 | tf_op jit(solution)/shard_map/ppermute | solution.py:203
  104.4 0.6 copy-start
  105.0 0.6 copy-start.2
  105.6 0.8 copy-start.1
  126.3 18.1 %all-to-all-start = ((f32[16,1,80]{2,1,0:T(1,128)}), f32[16,1,80]{2,1,0:T(1,128)S(1)}, u32[]{:S(2)}, u32[]{:S(2)}) async-start(f32[16,1,80]{2,1,0:T(1,128)} %bitcast.36), calls=%async_computation.1 | async-start | bytes 16384 | tf_op jit(solution)/shard_map/all_to_all | solution.py:270
  144.4 0.6 copy-start.3
Sparse Core Ops, SparseCore 0:
  16.3 60.6 all-gather.1
  105.8 46.3 reduce-scatter.1

commit v5 on v2

--- a/solution.py
+++ b/solution.py
@@ -29,22 +29,9 @@
 
 def expert_kernel(blocks, tok, top, cap, info, *refs):
     msgs = refs[:blocks]
-    w_hbm, saved_hbm, part_hbm, slot_ref, gate_ref = refs[blocks : blocks + 5]
-    rows, rows16, gcol, meta, w_ref, saved_ref, part_ref, w_sem, saved_sem, part_sem = refs[blocks + 5 :]
+    rows16, gate_ref, rows, gcol, meta = refs[blocks:]
     slots = blocks * cap
     lanes = 2 * tok
-    tiles = w_sem.shape[0]
-    tile = w_ref.shape[0] // tiles
-    parts = [pl.ds(i * tile, tile) for i in range(tiles)]
-    fetched = []
-    for i, at in enumerate(parts):
-        pair = (
-            pltpu.make_async_copy(w_hbm.at[at], w_ref.at[at], w_sem.at[i]),
-            pltpu.make_async_copy(saved_hbm.at[at], saved_ref.at[at], saved_sem.at[i]),
-        )
-        for copy in pair:
-            copy.start()
-        fetched.append(pair)
 
     for b in range(blocks):
         meta[b * META : (b + 1) * META, :] = msgs[b][lanes : lanes + META, : top * tok].astype(f32)
@@ -77,28 +64,10 @@
             gcol[m, at, :] = col[m * cap : (m + 1) * cap]
     first = (lax.broadcasted_iota(jnp.int32, (8, gcol.shape[2]), 1) == 0).astype(f32).astype(bf16)
     for m in range(2):
-        rows16[m] = rows[m].astype(bf16)
+        rows16[m * slots : (m + 1) * slots, :] = rows[m].astype(bf16)
         gate_ref[:, m * slots : (m + 1) * slots] = lax.dot_general(
             first, gcol[m].astype(bf16), NT, preferred_element_type=f32
         )
-
-    sent = []
-    for i, at in enumerate(parts):
-        for copy in fetched[i]:
-            copy.wait()
-        w = w_ref[at, :]
-        for m in range(2):
-            cols = slice(m * slots, (m + 1) * slots)
-            part = lax.dot_general(w, rows16[m], NT, preferred_element_type=f32).astype(bf16)
-            part_ref[at, cols] = part
-            prod = part.astype(f32) * saved_ref[at, cols].astype(f32)
-            total = jnp.sum(prod.reshape(-1, 8, slots), axis=0)
-            slot_ref[:, cols] = total if i == 0 else slot_ref[:, cols] + total
-        copy = pltpu.make_async_copy(part_ref.at[at], part_hbm.at[at], part_sem.at[i])
-        copy.start()
-        sent.append(copy)
-    for copy in sent:
-        copy.wait()
 
 
 def logits_kernel(cap, rf, sf, rr, sr, back, out_f, out_r, grad):
@@ -207,37 +176,33 @@
     step(None, far_fall, 1 - column, half)
     info = jnp.stack([me] + index).astype(jnp.int32)
 
-    tiles = max(1, ff // 256)
-    vmem, hbm = pl.BlockSpec(memory_space=pltpu.VMEM), pl.BlockSpec(memory_space=pltpu.HBM)
-    partial, slot_part, gates = pl.pallas_call(
+    vmem = pl.BlockSpec(memory_space=pltpu.VMEM)
+    rows, gates = pl.pallas_call(
         functools.partial(expert_kernel, blocks, tok, top, cap),
-        in_specs=[pl.BlockSpec(memory_space=pltpu.SMEM)] + [vmem] * blocks + [hbm, hbm],
-        out_specs=[hbm, vmem, vmem],
+        in_specs=[pl.BlockSpec(memory_space=pltpu.SMEM)] + [vmem] * blocks,
+        out_specs=[vmem, vmem],
         out_shape=[
-            jax.ShapeDtypeStruct((ff, 2 * slots), bf16),
-            jax.ShapeDtypeStruct((8, 2 * slots), f32),
+            jax.ShapeDtypeStruct((2 * slots, width), bf16),
             jax.ShapeDtypeStruct((8, 2 * slots), f32),
         ],
         scratch_shapes=[
             pltpu.VMEM((2, slots, width), f32),
-            pltpu.VMEM((2, slots, width), bf16),
             pltpu.VMEM((2, slots, 128), f32),
             pltpu.VMEM((blocks * META, top * tok), f32),
-            pltpu.VMEM((ff, width), bf16),
-            pltpu.VMEM((ff, 2 * slots), bf16),
-            pltpu.VMEM((ff, 2 * slots), bf16),
-            pltpu.SemaphoreType.DMA((tiles,)),
-            pltpu.SemaphoreType.DMA((tiles,)),
-            pltpu.SemaphoreType.DMA((tiles,)),
         ],
-        compiler_params=pltpu.CompilerParams(vmem_limit_bytes=50 * 1024 * 1024),
+        compiler_params=pltpu.CompilerParams(vmem_limit_bytes=32 * 1024 * 1024),
         cost_estimate=pl.CostEstimate(
-            flops=4 * ff * width * slots, bytes_accessed=16 * 1024 * 1024, transcendentals=0
+            flops=ff * width * slots, bytes_accessed=8 * 1024 * 1024, transcendentals=0
         ),
-    )(info, *msgs, down_weight.reshape(ff, width), saved_all)
+    )(info, *msgs)
+    partial = lax.dot_general(
+        down_weight.reshape(ff, width), rows, NT, preferred_element_type=f32
+    ).astype(bf16)
 
     terms = lax.psum_scatter(partial, "dp", scatter_dimension=0, tiled=True)
-    slot_grad = lax.psum(jnp.sum(slot_part, axis=0), "dp")
+    slot_grad = lax.psum(
+        jnp.sum(partial.astype(f32) * saved_all.astype(f32), axis=0), "dp"
+    )
     home = jnp.transpose(slot_grad.reshape(2, blocks, cap), (1, 0, 2)).reshape(blocks, 2 * cap)
     back = lax.all_to_all(home, "expert", split_axis=0, concat_axis=0, tiled=True)
     logits = pl.pallas_call(

time: 160 us -> 169 us (1.056)
  Pallas kernels: 11.7 us -> 6.11 us
  local copies, waits for them, and re-layouts: 0.88 us -> 5.07 us
  matrix products: 0 us -> 4.17 us
  other arithmetic: 4.3 us -> 7.54 us
  waiting for transfers between devices: 34.5 us -> 36.7 us
    ppermute x3, waiting for transfers between devices: 0.69 us -> 14.1 us  [hop(): return lax.ppermute(array, ('section', 'expert'), pairs)]
    ppermute x7, waiting for transfers between devices: 9 us -> 2.95 us  [step(): rise = lax.ppermute(rise, 'expert', up)]
    pallas_call x1, Pallas kernels: 8.58 us -> 2.93 us  [shards(): pl.pallas_call(functools.partial(expert_kernel, blocks, tok, top, cap), i...]
    dot_general x0 -> x1, matrix products: none -> 4.17 us  [shards(): lax.dot_general(down_weight.reshape(ff, width), rows, NT, preferred_eleme...]
    ppermute x7, starting transfers between devices: 17.2 us -> 21.4 us  [step(): rise = lax.ppermute(rise, 'expert', up)]
    ppermute x7, starting transfers between devices: 40.7 us -> 37.2 us  [step(): fall = lax.ppermute(fall, 'expert', down)]
    reduce_sum x1, other arithmetic: 0.02 us -> 3.27 us  [shards(): jnp.sum(partial.astype(f32) * saved_all.astype(f32), axis=0)]
    unnamed x2 -> x12, local copies, waits for them, and re-layouts: 0.6 us -> 3.49 us
  transfers between devices with their start and end apart: 20 -> 20, of which waited for: 8 -> 9; matrix products, arithmetic and copies ran while one was open for 1% -> 6% of each run, Pallas kernels for 2% -> 4%
where the time goes in v5:
time: 169 us; the launch traced here: 168 us
  starting transfers between devices  74.3 us (44%)
  waiting for transfers between devices  36.7 us (22%)
  blocking collectives  19.4 us (11%)
  between operations  14.5 us (9%)
  other arithmetic  7.54 us (4%)
  Pallas kernels  6.11 us (4%)
  local copies, waits for them, and re-layouts  5.07 us (3%)
  matrix products  4.17 us (2%)
    ppermute x7, starting transfers between devices, step(): fall = lax.ppermute(fall, 'expert', down)  37.2 us
    ppermute x7, starting transfers between devices, step(): rise = lax.ppermute(rise, 'expert', up)  21.4 us
    psum x1, blocking collectives, shards(): lax.psum(jnp.sum(partial.astype(f32) * saved_all.astype(f32), axis=0), 'dp')  19.4 us
    ppermute x3, waiting for transfers between devices, hop(): return lax.ppermute(array, ('section', 'expert'), pairs)  14.1 us
    all_to_all x1, waiting for transfers between devices, shards(): lax.all_to_all(home, 'expert', split_axis=0, concat_axis=0, tiled=True)  11.5 us
    ppermute x3, starting transfers between devices, hop(): return lax.ppermute(array, ('section', 'expert'), pairs)  9.12 us
    all_to_all x1, starting transfers between devices, shards(): lax.all_to_all(home, 'expert', split_axis=0, concat_axis=0, tiled=True)  6.48 us
    reduce_scatter x1, waiting for transfers between devices, shards(): terms = lax.psum_scatter(partial, 'dp', scatter_dimension=0, tiled=True)  4.46 us
  transfers between devices with their start and end apart: 20, of which 9 were waited for; matrix products, arithmetic and copies ran while one was open for 6% of the time, Pallas kernels for 4%

profile of v5, /device:TPU:6, one launch (start us, length us, event | category | flops | bytes accessed | tf_op | source)
XLA Modules:
  0.0 167.7 jit_solution(17964626015183952004)
XLA Ops:
  7.2 2.1 %collective-permute-start = (bf16[64,896]{1,0:T(8,128)(2,1)}, bf16[64,896]{1,0:T(8,128)(2,1)S(1)}, u32[]{:S(2)}, u32[]{:S(2)}) collective-permute-start(bf16[64,896]{1,0:T(8,128)(2,1)} %bitcast.63), channel_id=1, source_target_pairs={{0,896},{8,904},{16,912},{24,920},{32,928},{40,936},{48,944},{56,9... | collective-permute-start | bytes 344072 | tf_op jit(solution)/shard_map/ppermute | solution.py:131
  9.3 2.4 %collective-permute-start.1 = (bf16[64,896]{1,0:T(8,128)(2,1)}, bf16[64,896]{1,0:T(8,128)(2,1)S(1)}, u32[]{:S(2)}, u32[]{:S(2)}) collective-permute-start(bf16[64,896]{1,0:T(8,128)(2,1)} %bitcast.64), channel_id=1, source_target_pairs={{0,128},{8,136},{16,144},{24,152},{32,160},{40,168},{48,176},{56,1... | collective-permute-start | bytes 344072 | tf_op jit(solution)/shard_map/ppermute | solution.py:131
  16.4 6.3 %collective-permute-start.2 = (bf16[136,896]{1,0:T(8,128)(2,1)S(1)}, bf16[136,896]{1,0:T(8,128)(2,1)S(1)}, u32[]{:S(2)}, u32[]{:S(2)}) collective-permute-start(bf16[136,896]{1,0:T(8,128)(2,1)S(1)} %pad_maximum_fusion.1.refs_0_), channel_id=1, source_target_pairs={{0,16},{8,24},{16,32},{24,40},{32,48},{40,56},{48,64},{56,72},{64,... | collective-permute-start | bytes 731144 | tf_op jit(solution)/shard_map/ppermute | solution.py:156
  22.8 14.0 %collective-permute-start.3 = (bf16[136,896]{1,0:T(8,128)(2,1)S(1)}, bf16[136,896]{1,0:T(8,128)(2,1)S(1)}, u32[]{:S(2)}, u32[]{:S(2)}) collective-permute-start(bf16[136,896]{1,0:T(8,128)(2,1)S(1)} %pad_maximum_fusion.1.refs_0_), channel_id=1, source_target_pairs={{0,112},{8,120},{16,0},{24,8},{32,16},{40,24},{48,32},{56,40},{64,... | collective-permute-start | bytes 731144 | tf_op jit(solution)/shard_map/ppermute | solution.py:160
  36.8 4.7 %collective-permute-start.4 = (bf16[136,896]{1,0:T(8,128)(2,1)S(1)}, bf16[136,896]{1,0:T(8,128)(2,1)S(1)}, u32[]{:S(2)}, u32[]{:S(2)}) collective-permute-start(bf16[136,896]{1,0:T(8,128)(2,1)S(1)} %pad_maximum_fusion.1.refs_0_), channel_id=1, source_target_pairs={{0,8},{8,0},{16,24},{24,16},{32,40},{40,32},{48,56},{56,48},{64,72... | collective-permute-start | bytes 731144 | tf_op jit(solution)/shard_map/ppermute | solution.py:131
  43.0 13.4 %collective-permute-done.4.refs_1_ = bf16[136,896]{1,0:T(8,128)(2,1)S(1)} collective-permute-done((bf16[136,896]{1,0:T(8,128)(2,1)S(1)}, bf16[136,896]{1,0:T(8,128)(2,1)S(1)}, u32[]{:S(2)}, u32[]{:S(2)}) %collective-permute-start.4) | collective-permute-done | bytes 243744 | tf_op jit(solution)/shard_map/ppermute | solution.py:131
  56.4 3.6 %collective-permute-start.11 = (bf16[136,896]{1,0:T(8,128)(2,1)S(1)}, bf16[136,896]{1,0:T(8,128)(2,1)S(1)}, u32[]{:S(2)}, u32[]{:S(2)}) collective-permute-start(bf16[136,896]{1,0:T(8,128)(2,1)S(1)} %collective-permute-done.4.refs_1_), channel_id=1, source_target_pairs={{0,112},{8,120},{16,0},{24,8},{32,16},{40,24},{48,32},{56,40},{64,... | collective-permute-start | bytes 731144 | tf_op jit(solution)/shard_map/ppermute | solution.py:160
  60.0 2.2 %collective-permute-start.10 = (bf16[136,896]{1,0:T(8,128)(2,1)S(1)}, bf16[136,896]{1,0:T(8,128)(2,1)S(1)}, u32[]{:S(2)}, u32[]{:S(2)}) collective-permute-start(bf16[136,896]{1,0:T(8,128)(2,1)S(1)} %collective-permute-done.4.refs_1_), channel_id=1, source_target_pairs={{0,16},{8,24},{16,32},{24,40},{32,48},{40,56},{48,64},{56,72},{64,... | collective-permute-start | bytes 731144 | tf_op jit(solution)/shard_map/ppermute | solution.py:156
  66.0 4.7 %collective-permute-start.13 = (bf16[136,896]{1,0:T(8,128)(2,1)S(1)}, bf16[136,896]{1,0:T(8,128)(2,1)S(1)}, u32[]{:S(2)}, u32[]{:S(2)}) collective-permute-start(bf16[136,896]{1,0:T(8,128)(2,1)S(1)} %collective-permute-done.11.refs_10_), channel_id=1, source_target_pairs={{0,112},{8,120},{16,0},{24,8},{32,16},{40,24},{48,32},{56,40},{64,... | collective-permute-start | bytes 731144 | tf_op jit(solution)/shard_map/ppermute | solution.py:160
  70.7 2.3 %collective-permute-start.6 = (bf16[136,896]{1,0:T(8,128)(2,1)S(1)}, bf16[136,896]{1,0:T(8,128)(2,1)}, u32[]{:S(2)}, u32[]{:S(2)}) collective-permute-start(bf16[136,896]{1,0:T(8,128)(2,1)S(1)} %collective-permute-done.3.refs_3_), channel_id=1, source_target_pairs={{0,112},{8,120},{16,0},{24,8},{32,16},{40,24},{48,32},{56,40},{64,... | collective-permute-start | bytes 731144 | tf_op jit(solution)/shard_map/ppermute | solution.py:160
  73.0 3.5 %collective-permute-start.12 = (bf16[136,896]{1,0:T(8,128)(2,1)S(1)}, bf16[136,896]{1,0:T(8,128)(2,1)}, u32[]{:S(2)}, u32[]{:S(2)}) collective-permute-start(bf16[136,896]{1,0:T(8,128)(2,1)S(1)} %collective-permute-done.10.refs_9_), channel_id=1, source_target_pairs={{0,16},{8,24},{16,32},{24,40},{32,48},{40,56},{48,64},{56,72},{64,... | collective-permute-start | bytes 731144 | tf_op jit(solution)/shard_map/ppermute | solution.py:156
  76.5 1.9 %collective-permute-start.7 = (bf16[136,896]{1,0:T(8,128)(2,1)S(1)}, bf16[136,896]{1,0:T(8,128)(2,1)}, u32[]{:S(2)}, u32[]{:S(2)}) collective-permute-start(bf16[136,896]{1,0:T(8,128)(2,1)S(1)} %collective-permute-done.5.refs_4_), channel_id=1, source_target_pairs={{0,16},{8,24},{16,32},{24,40},{32,48},{40,56},{48,64},{56,72},{64,... | collective-permute-start | bytes 731144 | tf_op jit(solution)/shard_map/ppermute | solution.py:156
  78.5 5.1 %collective-permute-start.15 = (bf16[136,896]{1,0:T(8,128)(2,1)S(1)}, bf16[136,896]{1,0:T(8,128)(2,1)}, u32[]{:S(2)}, u32[]{:S(2)}) collective-permute-start(bf16[136,896]{1,0:T(8,128)(2,1)S(1)} %collective-permute-done.13.refs_12_), channel_id=1, source_target_pairs={{0,112},{8,120},{16,0},{24,8},{32,16},{40,24},{48,32},{56,40},{64,... | collective-permute-start | bytes 731144 | tf_op jit(solution)/shard_map/ppermute | solution.py:160
  84.3 2.3 %collective-permute-start.8 = (bf16[136,896]{1,0:T(8,128)(2,1)}, bf16[136,896]{1,0:T(8,128)(2,1)}, u32[]{:S(2)}, u32[]{:S(2)}) collective-permute-start(bf16[136,896]{1,0:T(8,128)(2,1)} %collective-permute-done.6.refs_5_), channel_id=1, source_target_pairs={{0,112},{8,120},{16,0},{24,8},{32,16},{40,24},{48,32},{56,40},{64,... | collective-permute-start | bytes 731144 | tf_op jit(solution)/shard_map/ppermute | solution.py:160
  86.7 3.5 %collective-permute-start.14 = (bf16[136,896]{1,0:T(8,128)(2,1)}, bf16[136,896]{1,0:T(8,128)(2,1)}, u32[]{:S(2)}, u32[]{:S(2)}) collective-permute-start(bf16[136,896]{1,0:T(8,128)(2,1)} %collective-permute-done.12.refs_11_), channel_id=1, source_target_pairs={{0,16},{8,24},{16,32},{24,40},{32,48},{40,56},{48,64},{56,72},{64,... | collective-permute-start | bytes 731144 | tf_op jit(solution)/shard_map/ppermute | solution.py:156
  92.1 5.1 %collective-permute-start.16 = (bf16[136,896]{1,0:T(8,128)(2,1)}, bf16[136,896]{1,0:T(8,128)(2,1)}, u32[]{:S(2)}, u32[]{:S(2)}) collective-permute-start(bf16[136,896]{1,0:T(8,128)(2,1)} %collective-permute-done.15.refs_14_), channel_id=1, source_target_pairs={{0,112},{8,120},{16,0},{24,8},{32,16},{40,24},{48,32},{56,40},{64,... | collective-permute-start | bytes 731144 | tf_op jit(solution)/shard_map/ppermute | solution.py:160
  98.4 2.6 %collective-permute-done.9.refs_8_ = bf16[136,896]{1,0:T(8,128)(2,1)} collective-permute-done((bf16[136,896]{1,0:T(8,128)(2,1)}, bf16[136,896]{1,0:T(8,128)(2,1)}, u32[]{:S(2)}, u32[]{:S(2)}) %collective-permute-start.9) | collective-permute-done | bytes 243744 | tf_op jit(solution)/shard_map/ppermute | solution.py:156
  102.8 2.9 %shard_map.121 = (bf16[1280,896]{1,0:T(8,128)(2,1)S(1)}, f32[8,1280]{1,0:T(8,128)S(1)}) custom-call(s32[17]{0:T(128)S(1)} %copy-done.3, bf16[136,896]{1,0:T(8,128)(2,1)S(1)} %pad_maximum_fusion.1.refs_0_, bf16[136,896]{1,0:T(8,128)(2,1)S(1)} %collective-permute-done.4.refs_1_, bf16[136,896]{1,0:T(8,128)(2,1)S(1)} %collective-permute-done.2.refs_2_, ...), custom_call_target="tpu_custom_call" | custom-call | flops 587202560 | bytes 8388608 | tf_op jit(solution)/shard_map/pallas_call | solution.py:180
  106.4 4.2 %fusion = bf16[1024,1280]{1,0:T(8,128)(2,1)} fusion(bf16[1280,896]{1,0:T(8,128)(2,1)S(1)} %get-tuple-element.18, bf16[1,1,1024,896]{3,2,1,0:T(8,128)(2,1)S(1)} %copy-done), kind=kOutput, calls=%fused_computation.2 | convolution fusion | flops 2350120960 | bytes 6750208 | tf_op jit(solution)/shard_map/dot_general | solution.py:198
  110.6 3.3 %multiply_reduce_fusion = f32[1280]{0:T(1024)S(1)} fusion(bf16[1024,1280]{1,0:T(8,128)(2,1)} %all-gather.2.cloned.1.call-done, bf16[1024,1280]{1,0:T(8,128)(2,1)} %fusion), kind=kLoop, calls=%fused_computation | loop fusion | flops 5241600 | bytes 5248000 | tf_op jit(solution)/shard_map/reduce_sum | solution.py:204
  114.1 19.4 %psum.7 = f32[16,1,80]{2,0,1:T(8,128)} all-reduce(f32[16,1,80]{2,0,1:T(8,128)S(1)} %all_to_all.7), channel_id=1, replica_groups=mesh['section'=8,'expert'=16,'dp'=8] {'dp'}, use_global_device_ids=true, to_apply=%region_2.3 | all-reduce | flops 1280 | bytes 10240 | tf_op jit(solution)/shard_map/psum | solution.py:203
  133.5 6.5 %all-to-all-start = ((f32[16,1,80]{2,1,0:T(1,128)}), f32[16,1,80]{2,1,0:T(1,128)S(1)}, u32[]{:S(2)}, u32[]{:S(2)}) async-start(f32[16,1,80]{2,1,0:T(1,128)} %bitcast.37), calls=%async_computation.1 | async-start | bytes 16384 | tf_op jit(solution)/shard_map/all_to_all | solution.py:207
  140.7 11.5 %all-to-all-done = f32[16,1,80]{2,1,0:T(1,128)S(1)} async-done(((f32[16,1,80]{2,1,0:T(1,128)}), f32[16,1,80]{2,1,0:T(1,128)S(1)}, u32[]{:S(2)}, u32[]{:S(2)}) %all-to-all-start) | async-done | bytes 5152 | tf_op jit(solution)/shard_map/all_to_all | solution.py:207
  154.6 4.5 %reduce-scatter.2.cloned.1.call-done = bf16[128,1280]{1,0:T(8,128)(2,1)} async-done(((bf16[1024,1280]{1,0:T(8,128)(2,1)}), bf16[128,1280]{1,0:T(8,128)(2,1)}) %reduce-scatter.2.cloned.1.call-update) | async-done | bytes 327696 | tf_op jit(solution)/shard_map/reduce_scatter | solution.py:202
  (44 shorter events, 21.1 us)
Async XLA Ops:
  7.2 99.2 %copy-start = (bf16[1,1,1024,896]{3,2,1,0:T(8,128)(2,1)S(1)}, bf16[1,1,1024,896]{3,2,1,0:T(8,128)(2,1)}, u32[]{:S(2)}) copy-start(bf16[1,1,1024,896]{3,2,1,0:T(8,128)(2,1)} %param.15) | copy-start | bytes 5505028
  7.2 103.4 %all-gather.2.cloned.1.call-start = ((), (), s32[]{:S(2)}) async-start(), calls=%async_computation.3 | async-start | bytes 2949120 | tf_op jit(solution)/shard_map/all_gather | solution.py:146
  7.2 7.7 %collective-permute-start = (bf16[64,896]{1,0:T(8,128)(2,1)}, bf16[64,896]{1,0:T(8,128)(2,1)S(1)}, u32[]{:S(2)}, u32[]{:S(2)}) collective-permute-start(bf16[64,896]{1,0:T(8,128)(2,1)} %bitcast.63), channel_id=1, source_target_pairs={{0,896},{8,904},{16,912},{24,920},{32,928},{40,936},{48,944},{56,9... | collective-permute-start | bytes 344072 | tf_op jit(solution)/shard_map/ppermute | solution.py:131
  9.3 6.3 %collective-permute-start.1 = (bf16[64,896]{1,0:T(8,128)(2,1)}, bf16[64,896]{1,0:T(8,128)(2,1)S(1)}, u32[]{:S(2)}, u32[]{:S(2)}) collective-permute-start(bf16[64,896]{1,0:T(8,128)(2,1)} %bitcast.64), channel_id=1, source_target_pairs={{0,128},{8,136},{16,144},{24,152},{32,160},{40,168},{48,176},{56,1... | collective-permute-start | bytes 344072 | tf_op jit(solution)/shard_map/ppermute | solution.py:131
  16.4 142.7 %reduce-scatter.2.cloned.1.call-start = ((), (), s32[]{:S(2)}) async-start(), calls=%async_computation.2 | async-start | bytes 2949120 | tf_op jit(solution)/shard_map/reduce_scatter | solution.py:202
  16.4 25.1 %collective-permute-start.2 = (bf16[136,896]{1,0:T(8,128)(2,1)S(1)}, bf16[136,896]{1,0:T(8,128)(2,1)S(1)}, u32[]{:S(2)}, u32[]{:S(2)}) collective-permute-start(bf16[136,896]{1,0:T(8,128)(2,1)S(1)} %pad_maximum_fusion.1.refs_0_), channel_id=1, source_target_pairs={{0,16},{8,24},{16,32},{24,40},{32,48},{40,56},{48,64},{56,72},{64,... | collective-permute-start | bytes 731144 | tf_op jit(solution)/shard_map/ppermute | solution.py:156
  22.8 20.3 %collective-permute-start.3 = (bf16[136,896]{1,0:T(8,128)(2,1)S(1)}, bf16[136,896]{1,0:T(8,128)(2,1)S(1)}, u32[]{:S(2)}, u32[]{:S(2)}) collective-permute-start(bf16[136,896]{1,0:T(8,128)(2,1)S(1)} %pad_maximum_fusion.1.refs_0_), channel_id=1, source_target_pairs={{0,112},{8,120},{16,0},{24,8},{32,16},{40,24},{48,32},{56,40},{64,... | collective-permute-start | bytes 731144 | tf_op jit(solution)/shard_map/ppermute | solution.py:160
  36.8 19.6 %collective-permute-start.4 = (bf16[136,896]{1,0:T(8,128)(2,1)S(1)}, bf16[136,896]{1,0:T(8,128)(2,1)S(1)}, u32[]{:S(2)}, u32[]{:S(2)}) collective-permute-start(bf16[136,896]{1,0:T(8,128)(2,1)S(1)} %pad_maximum_fusion.1.refs_0_), channel_id=1, source_target_pairs={{0,8},{8,0},{16,24},{24,16},{32,40},{40,32},{48,56},{56,48},{64,72... | collective-permute-start | bytes 731144 | tf_op jit(solution)/shard_map/ppermute | solution.py:131
  56.4 9.6 %collective-permute-start.11 = (bf16[136,896]{1,0:T(8,128)(2,1)S(1)}, bf16[136,896]{1,0:T(8,128)(2,1)S(1)}, u32[]{:S(2)}, u32[]{:S(2)}) collective-permute-start(bf16[136,896]{1,0:T(8,128)(2,1)S(1)} %collective-permute-done.4.refs_1_), channel_id=1, source_target_pairs={{0,112},{8,120},{16,0},{24,8},{32,16},{40,24},{48,32},{56,40},{64,... | collective-permute-start | bytes 731144 | tf_op jit(solution)/shard_map/ppermute | solution.py:160
  60.0 12.9 %collective-permute-start.10 = (bf16[136,896]{1,0:T(8,128)(2,1)S(1)}, bf16[136,896]{1,0:T(8,128)(2,1)S(1)}, u32[]{:S(2)}, u32[]{:S(2)}) collective-permute-start(bf16[136,896]{1,0:T(8,128)(2,1)S(1)} %collective-permute-done.4.refs_1_), channel_id=1, source_target_pairs={{0,16},{8,24},{16,32},{24,40},{32,48},{40,56},{48,64},{56,72},{64,... | collective-permute-start | bytes 731144 | tf_op jit(solution)/shard_map/ppermute | solution.py:156
  62.2 14.3 %collective-permute-start.5 = (bf16[136,896]{1,0:T(8,128)(2,1)S(1)}, bf16[136,896]{1,0:T(8,128)(2,1)S(1)}, u32[]{:S(2)}, u32[]{:S(2)}) collective-permute-start(bf16[136,896]{1,0:T(8,128)(2,1)S(1)} %collective-permute-done.2.refs_2_), channel_id=1, source_target_pairs={{0,16},{8,24},{16,32},{24,40},{32,48},{40,56},{48,64},{56,72},{64,... | collective-permute-start | bytes 731144 | tf_op jit(solution)/shard_map/ppermute | solution.py:156
  66.0 12.5 %collective-permute-start.13 = (bf16[136,896]{1,0:T(8,128)(2,1)S(1)}, bf16[136,896]{1,0:T(8,128)(2,1)S(1)}, u32[]{:S(2)}, u32[]{:S(2)}) collective-permute-start(bf16[136,896]{1,0:T(8,128)(2,1)S(1)} %collective-permute-done.11.refs_10_), channel_id=1, source_target_pairs={{0,112},{8,120},{16,0},{24,8},{32,16},{40,24},{48,32},{56,40},{64,... | collective-permute-start | bytes 731144 | tf_op jit(solution)/shard_map/ppermute | solution.py:160
  70.7 13.7 %collective-permute-start.6 = (bf16[136,896]{1,0:T(8,128)(2,1)S(1)}, bf16[136,896]{1,0:T(8,128)(2,1)}, u32[]{:S(2)}, u32[]{:S(2)}) collective-permute-start(bf16[136,896]{1,0:T(8,128)(2,1)S(1)} %collective-permute-done.3.refs_3_), channel_id=1, source_target_pairs={{0,112},{8,120},{16,0},{24,8},{32,16},{40,24},{48,32},{56,40},{64,... | collective-permute-start | bytes 731144 | tf_op jit(solution)/shard_map/ppermute | solution.py:160
  73.0 13.7 %collective-permute-start.12 = (bf16[136,896]{1,0:T(8,128)(2,1)S(1)}, bf16[136,896]{1,0:T(8,128)(2,1)}, u32[]{:S(2)}, u32[]{:S(2)}) collective-permute-start(bf16[136,896]{1,0:T(8,128)(2,1)S(1)} %collective-permute-done.10.refs_9_), channel_id=1, source_target_pairs={{0,16},{8,24},{16,32},{24,40},{32,48},{40,56},{48,64},{56,72},{64,... | collective-permute-start | bytes 731144 | tf_op jit(solution)/shard_map/ppermute | solution.py:156
  76.5 13.7 %collective-permute-start.7 = (bf16[136,896]{1,0:T(8,128)(2,1)S(1)}, bf16[136,896]{1,0:T(8,128)(2,1)}, u32[]{:S(2)}, u32[]{:S(2)}) collective-permute-start(bf16[136,896]{1,0:T(8,128)(2,1)S(1)} %collective-permute-done.5.refs_4_), channel_id=1, source_target_pairs={{0,16},{8,24},{16,32},{24,40},{32,48},{40,56},{48,64},{56,72},{64,... | collective-permute-start | bytes 731144 | tf_op jit(solution)/shard_map/ppermute | solution.py:156
  78.5 13.7 %collective-permute-start.15 = (bf16[136,896]{1,0:T(8,128)(2,1)S(1)}, bf16[136,896]{1,0:T(8,128)(2,1)}, u32[]{:S(2)}, u32[]{:S(2)}) collective-permute-start(bf16[136,896]{1,0:T(8,128)(2,1)S(1)} %collective-permute-done.13.refs_12_), channel_id=1, source_target_pairs={{0,112},{8,120},{16,0},{24,8},{32,16},{40,24},{48,32},{56,40},{64,... | collective-permute-start | bytes 731144 | tf_op jit(solution)/shard_map/ppermute | solution.py:160
  83.6 0.7 copy-start.1
  84.3 13.8 %collective-permute-start.8 = (bf16[136,896]{1,0:T(8,128)(2,1)}, bf16[136,896]{1,0:T(8,128)(2,1)}, u32[]{:S(2)}, u32[]{:S(2)}) collective-permute-start(bf16[136,896]{1,0:T(8,128)(2,1)} %collective-permute-done.6.refs_5_), channel_id=1, source_target_pairs={{0,112},{8,120},{16,0},{24,8},{32,16},{40,24},{48,32},{56,40},{64,... | collective-permute-start | bytes 731144 | tf_op jit(solution)/shard_map/ppermute | solution.py:160
  86.7 11.7 %collective-permute-start.14 = (bf16[136,896]{1,0:T(8,128)(2,1)}, bf16[136,896]{1,0:T(8,128)(2,1)}, u32[]{:S(2)}, u32[]{:S(2)}) collective-permute-start(bf16[136,896]{1,0:T(8,128)(2,1)} %collective-permute-done.12.refs_11_), channel_id=1, source_target_pairs={{0,16},{8,24},{16,32},{24,40},{32,48},{40,56},{48,64},{56,72},{64,... | collective-permute-start | bytes 731144 | tf_op jit(solution)/shard_map/ppermute | solution.py:156
  90.2 10.8 %collective-permute-start.9 = (bf16[136,896]{1,0:T(8,128)(2,1)}, bf16[136,896]{1,0:T(8,128)(2,1)}, u32[]{:S(2)}, u32[]{:S(2)}) collective-permute-start(bf16[136,896]{1,0:T(8,128)(2,1)} %collective-permute-done.7.refs_6_), channel_id=1, source_target_pairs={{0,16},{8,24},{16,32},{24,40},{32,48},{40,56},{48,64},{56,72},{64,... | collective-permute-start | bytes 731144 | tf_op jit(solution)/shard_map/ppermute | solution.py:156
  92.1 9.1 %collective-permute-start.16 = (bf16[136,896]{1,0:T(8,128)(2,1)}, bf16[136,896]{1,0:T(8,128)(2,1)}, u32[]{:S(2)}, u32[]{:S(2)}) collective-permute-start(bf16[136,896]{1,0:T(8,128)(2,1)} %collective-permute-done.15.refs_14_), channel_id=1, source_target_pairs={{0,112},{8,120},{16,0},{24,8},{32,16},{40,24},{48,32},{56,40},{64,... | collective-permute-start | bytes 731144 | tf_op jit(solution)/shard_map/ppermute | solution.py:160
  101.3 0.9 copy-start.2
  102.2 0.6 copy-start.3
  133.5 18.8 %all-to-all-start = ((f32[16,1,80]{2,1,0:T(1,128)}), f32[16,1,80]{2,1,0:T(1,128)S(1)}, u32[]{:S(2)}, u32[]{:S(2)}) async-start(f32[16,1,80]{2,1,0:T(1,128)} %bitcast.37), calls=%async_computation.1 | async-start | bytes 16384 | tf_op jit(solution)/shard_map/all_to_all | solution.py:207
  (2 other events, 1.2 us)
Sparse Core Ops, SparseCore 0:
  16.5 60.6 all-gather.1
  110.7 48.2 reduce-scatter.1

commit v6 on v2

--- a/solution.py
+++ b/solution.py
@@ -77,7 +77,7 @@
             gcol[m, at, :] = col[m * cap : (m + 1) * cap]
     first = (lax.broadcasted_iota(jnp.int32, (8, gcol.shape[2]), 1) == 0).astype(f32).astype(bf16)
     for m in range(2):
-        rows16[m] = rows[m].astype(bf16)
+        rows16[m * slots : (m + 1) * slots, :] = rows[m].astype(bf16)
         gate_ref[:, m * slots : (m + 1) * slots] = lax.dot_general(
             first, gcol[m].astype(bf16), NT, preferred_element_type=f32
         )
@@ -86,14 +86,11 @@
     for i, at in enumerate(parts):
         for copy in fetched[i]:
             copy.wait()
-        w = w_ref[at, :]
-        for m in range(2):
-            cols = slice(m * slots, (m + 1) * slots)
-            part = lax.dot_general(w, rows16[m], NT, preferred_element_type=f32).astype(bf16)
-            part_ref[at, cols] = part
-            prod = part.astype(f32) * saved_ref[at, cols].astype(f32)
-            total = jnp.sum(prod.reshape(-1, 8, slots), axis=0)
-            slot_ref[:, cols] = total if i == 0 else slot_ref[:, cols] + total
+        part = lax.dot_general(w_ref[at, :], rows16[...], NT, preferred_element_type=f32).astype(bf16)
+        part_ref[at, :] = part
+        prod = part.astype(f32) * saved_ref[at, :].astype(f32)
+        total = jnp.sum(prod.reshape(-1, 8, 2 * slots), axis=0)
+        slot_ref[...] = total if i == 0 else slot_ref[...] + total
         copy = pltpu.make_async_copy(part_ref.at[at], part_hbm.at[at], part_sem.at[i])
         copy.start()
         sent.append(copy)
@@ -200,11 +197,16 @@
         if t == 1:
             own_rise, own_fall, far = lax.optimization_barrier((own_rise, own_fall, far))
             msgs[1:] = far, own_rise, own_fall
-    step(own_rise, None, column, half)
-    far_rise = far_fall = far
+        if t <= 2:
+            far_fall = hop(own_fall, 0, 1)
+            msgs.append(far_fall)
+            index.append((level + t) % depth * 2 + 1 - column)
+    step(None, own_fall, column, half)
+    far_rise = far
     for t in range(1, half):
-        far_rise, far_fall = step(far_rise, far_fall, 1 - column, t)
-    step(None, far_fall, 1 - column, half)
+        far_rise, _ = step(far_rise, None, 1 - column, t)
+    for t in range(3, half + 1):
+        _, far_fall = step(None, far_fall, 1 - column, t)
     info = jnp.stack([me] + index).astype(jnp.int32)
 
     tiles = max(1, ff // 256)
@@ -220,7 +222,7 @@
         ],
         scratch_shapes=[
             pltpu.VMEM((2, slots, width), f32),
-            pltpu.VMEM((2, slots, width), bf16),
+            pltpu.VMEM((2 * slots, width), bf16),
             pltpu.VMEM((2, slots, 128), f32),
             pltpu.VMEM((blocks * META, top * tok), f32),
             pltpu.VMEM((ff, width), bf16),

time: 160 us -> 169 us (1.056)
  waiting for transfers between devices: 34.5 us -> 38.9 us
  starting transfers between devices: 74.2 us -> 78.2 us
    ppermute x3 -> x5, starting transfers between devices: 10.1 us -> 21.4 us  [hop(): return lax.ppermute(array, ('section', 'expert'), pairs)]
    ppermute x7 -> x6, starting transfers between devices: 17.2 us -> 11.8 us  [step(): rise = lax.ppermute(rise, 'expert', up)]
    ppermute x7 -> x6, waiting for transfers between devices: 5.94 us -> 11 us  [step(): fall = lax.ppermute(fall, 'expert', down)]
    ppermute x7 -> x6, starting transfers between devices: 40.7 us -> 38.5 us  [step(): fall = lax.ppermute(fall, 'expert', down)]
    ppermute x7 -> x6, waiting for transfers between devices: 9 us -> 7.72 us  [step(): rise = lax.ppermute(rise, 'expert', up)]
  transfers between devices with their start and end apart: 20 -> 20, of which waited for: 8 -> 9; matrix products, arithmetic and copies ran while one was open for 1% -> 1% of each run, Pallas kernels for 2% -> 2%
where the time goes in v6:
time: 169 us; the launch traced here: 168 us
  starting transfers between devices  78.2 us (46%)
  waiting for transfers between devices  38.9 us (23%)
  blocking collectives  19.3 us (11%)
  between operations  14.4 us (9%)
  Pallas kernels  11.7 us (7%)
  other arithmetic  4.3 us (3%)
    ppermute x6, starting transfers between devices, step(): fall = lax.ppermute(fall, 'expert', down)  38.5 us
    ppermute x5, starting transfers between devices, hop(): return lax.ppermute(array, ('section', 'expert'), pairs)  21.4 us
    psum x1, blocking collectives, shards(): slot_grad = lax.psum(jnp.sum(slot_part, axis=0), 'dp')  19.3 us
    all_to_all x1, waiting for transfers between devices, shards(): lax.all_to_all(home, 'expert', split_axis=0, concat_axis=0, tiled=True)  12.3 us
    ppermute x6, starting transfers between devices, step(): rise = lax.ppermute(rise, 'expert', up)  11.8 us
    ppermute x6, waiting for transfers between devices, step(): fall = lax.ppermute(fall, 'expert', down)  11 us
    pallas_call x1, Pallas kernels, shards(): pl.pallas_call(functools.partial(expert_kernel, blocks, tok, top, cap), i...  8.52 us
    ppermute x6, waiting for transfers between devices, step(): rise = lax.ppermute(rise, 'expert', up)  7.72 us
  transfers between devices with their start and end apart: 20, of which 9 were waited for; matrix products, arithmetic and copies ran while one was open for 1% of the time, Pallas kernels for 2%

profile of v6, /device:TPU:6, one launch (start us, length us, event | category | flops | bytes accessed | tf_op | source)
XLA Modules:
  0.0 167.7 jit_solution(6873657655166033860)
XLA Ops:
  9.1 2.4 %collective-permute-start.1 = (bf16[64,896]{1,0:T(8,128)(2,1)}, bf16[64,896]{1,0:T(8,128)(2,1)S(1)}, u32[]{:S(2)}, u32[]{:S(2)}) collective-permute-start(bf16[64,896]{1,0:T(8,128)(2,1)} %bitcast.60), channel_id=1, source_target_pairs={{0,128},{8,136},{16,144},{24,152},{32,160},{40,168},{48,176},{56,1... | collective-permute-start | bytes 344072 | tf_op jit(solution)/shard_map/ppermute | solution.py:159
  16.3 5.8 %collective-permute-start.4 = (bf16[136,896]{1,0:T(8,128)(2,1)S(1)}, bf16[136,896]{1,0:T(8,128)(2,1)S(1)}, u32[]{:S(2)}, u32[]{:S(2)}) collective-permute-start(bf16[136,896]{1,0:T(8,128)(2,1)S(1)} %pad_maximum_fusion.1.refs_0_), channel_id=1, source_target_pairs={{0,8},{8,0},{16,24},{24,16},{32,40},{40,32},{48,56},{56,48},{64,72... | collective-permute-start | bytes 731144 | tf_op jit(solution)/shard_map/ppermute | solution.py:159
  22.1 17.3 %collective-permute-start.3 = (bf16[136,896]{1,0:T(8,128)(2,1)S(1)}, bf16[136,896]{1,0:T(8,128)(2,1)S(1)}, u32[]{:S(2)}, u32[]{:S(2)}) collective-permute-start(bf16[136,896]{1,0:T(8,128)(2,1)S(1)} %pad_maximum_fusion.1.refs_0_), channel_id=1, source_target_pairs={{0,112},{8,120},{16,0},{24,8},{32,16},{40,24},{48,32},{56,40},{64,... | collective-permute-start | bytes 731144 | tf_op jit(solution)/shard_map/ppermute | solution.py:188
  39.4 1.9 %collective-permute-start.2 = (bf16[136,896]{1,0:T(8,128)(2,1)S(1)}, bf16[136,896]{1,0:T(8,128)(2,1)S(1)}, u32[]{:S(2)}, u32[]{:S(2)}) collective-permute-start(bf16[136,896]{1,0:T(8,128)(2,1)S(1)} %pad_maximum_fusion.1.refs_0_), channel_id=1, source_target_pairs={{0,16},{8,24},{16,32},{24,40},{32,48},{40,56},{48,64},{56,72},{64,... | collective-permute-start | bytes 731144 | tf_op jit(solution)/shard_map/ppermute | solution.py:184
  41.3 4.2 %collective-permute-done.3.refs_3_ = bf16[136,896]{1,0:T(8,128)(2,1)S(1)} collective-permute-done((bf16[136,896]{1,0:T(8,128)(2,1)S(1)}, bf16[136,896]{1,0:T(8,128)(2,1)S(1)}, u32[]{:S(2)}, u32[]{:S(2)}) %collective-permute-start.3) | collective-permute-done | bytes 243744 | tf_op jit(solution)/shard_map/ppermute | solution.py:188
  45.5 5.3 %collective-permute-done.2.refs_2_ = bf16[136,896]{1,0:T(8,128)(2,1)S(1)} collective-permute-done((bf16[136,896]{1,0:T(8,128)(2,1)S(1)}, bf16[136,896]{1,0:T(8,128)(2,1)S(1)}, u32[]{:S(2)}, u32[]{:S(2)}) %collective-permute-start.2) | collective-permute-done | bytes 243744 | tf_op jit(solution)/shard_map/ppermute | solution.py:184
  50.8 3.6 %collective-permute-start.7 = (bf16[136,896]{1,0:T(8,128)(2,1)S(1)}, bf16[136,896]{1,0:T(8,128)(2,1)S(1)}, u32[]{:S(2)}, u32[]{:S(2)}) collective-permute-start(bf16[136,896]{1,0:T(8,128)(2,1)S(1)} %collective-permute-done.3.refs_3_), channel_id=1, source_target_pairs={{0,112},{8,120},{16,0},{24,8},{32,16},{40,24},{48,32},{56,40},{64,... | collective-permute-start | bytes 731144 | tf_op jit(solution)/shard_map/ppermute | solution.py:188
  54.5 2.2 %collective-permute-start.12 = (bf16[136,896]{1,0:T(8,128)(2,1)S(1)}, bf16[136,896]{1,0:T(8,128)(2,1)S(1)}, u32[]{:S(2)}, u32[]{:S(2)}) collective-permute-start(bf16[136,896]{1,0:T(8,128)(2,1)S(1)} %collective-permute-done.4.refs_1_), channel_id=1, source_target_pairs={{0,16},{8,24},{16,32},{24,40},{32,48},{40,56},{48,64},{56,72},{64,... | collective-permute-start | bytes 731144 | tf_op jit(solution)/shard_map/ppermute | solution.py:184
  56.7 3.7 %collective-permute-done.7.refs_6_ = bf16[136,896]{1,0:T(8,128)(2,1)S(1)} collective-permute-done((bf16[136,896]{1,0:T(8,128)(2,1)S(1)}, bf16[136,896]{1,0:T(8,128)(2,1)S(1)}, u32[]{:S(2)}, u32[]{:S(2)}) %collective-permute-start.7) | collective-permute-done | bytes 243744 | tf_op jit(solution)/shard_map/ppermute | solution.py:188
  60.4 5.0 %collective-permute-start.8 = (bf16[136,896]{1,0:T(8,128)(2,1)S(1)}, bf16[136,896]{1,0:T(8,128)(2,1)S(1)}, u32[]{:S(2)}, u32[]{:S(2)}) collective-permute-start(bf16[136,896]{1,0:T(8,128)(2,1)S(1)} %collective-permute-done.7.refs_6_), channel_id=1, source_target_pairs={{0,8},{8,0},{16,24},{24,16},{32,40},{40,32},{48,56},{56,48},{64,72... | collective-permute-start | bytes 731144 | tf_op jit(solution)/shard_map/ppermute | solution.py:159
  65.4 1.9 %collective-permute-start.6 = (bf16[136,896]{1,0:T(8,128)(2,1)S(1)}, bf16[136,896]{1,0:T(8,128)(2,1)S(1)}, u32[]{:S(2)}, u32[]{:S(2)}) collective-permute-start(bf16[136,896]{1,0:T(8,128)(2,1)S(1)} %collective-permute-done.2.refs_2_), channel_id=1, source_target_pairs={{0,16},{8,24},{16,32},{24,40},{32,48},{40,56},{48,64},{56,72},{64,... | collective-permute-start | bytes 731144 | tf_op jit(solution)/shard_map/ppermute | solution.py:184
  69.3 5.1 %collective-permute-start.10 = (bf16[136,896]{1,0:T(8,128)(2,1)S(1)}, bf16[136,896]{1,0:T(8,128)(2,1)S(1)}, u32[]{:S(2)}, u32[]{:S(2)}) collective-permute-start(bf16[136,896]{1,0:T(8,128)(2,1)S(1)} %collective-permute-done.7.refs_6_), channel_id=1, source_target_pairs={{0,112},{8,120},{16,0},{24,8},{32,16},{40,24},{48,32},{56,40},{64,... | collective-permute-start | bytes 731144 | tf_op jit(solution)/shard_map/ppermute | solution.py:188
  75.1 3.3 %collective-permute-start.15 = (bf16[136,896]{1,0:T(8,128)(2,1)S(1)}, bf16[136,896]{1,0:T(8,128)(2,1)S(1)}, u32[]{:S(2)}, u32[]{:S(2)}) collective-permute-start(bf16[136,896]{1,0:T(8,128)(2,1)S(1)} %collective-permute-done.8.refs_7_), channel_id=1, source_target_pairs={{0,112},{8,120},{16,0},{24,8},{32,16},{40,24},{48,32},{56,40},{64,... | collective-permute-start | bytes 731144 | tf_op jit(solution)/shard_map/ppermute | solution.py:188
  78.4 6.2 %collective-permute-start.5 = (bf16[136,896]{1,0:T(8,128)(2,1)S(1)}, bf16[136,896]{1,0:T(8,128)(2,1)S(1)}, u32[]{:S(2)}, u32[]{:S(2)}) collective-permute-start(bf16[136,896]{1,0:T(8,128)(2,1)S(1)} %collective-permute-done.3.refs_3_), channel_id=1, source_target_pairs={{0,8},{8,0},{16,24},{24,16},{32,40},{40,32},{48,56},{56,48},{64,72... | collective-permute-start | bytes 731144 | tf_op jit(solution)/shard_map/ppermute | solution.py:159
  86.6 1.9 %collective-permute-start.14 = (bf16[136,896]{1,0:T(8,128)(2,1)S(1)}, bf16[136,896]{1,0:T(8,128)(2,1)S(1)}, u32[]{:S(2)}, u32[]{:S(2)}) collective-permute-start(bf16[136,896]{1,0:T(8,128)(2,1)S(1)} %collective-permute-done.13.refs_12_), channel_id=1, source_target_pairs={{0,16},{8,24},{16,32},{24,40},{32,48},{40,56},{48,64},{56,72},{64,... | collective-permute-start | bytes 731144 | tf_op jit(solution)/shard_map/ppermute | solution.py:184
  88.5 5.1 %collective-permute-start.11 = (bf16[136,896]{1,0:T(8,128)(2,1)S(1)}, bf16[136,896]{1,0:T(8,128)(2,1)}, u32[]{:S(2)}, u32[]{:S(2)}) collective-permute-start(bf16[136,896]{1,0:T(8,128)(2,1)S(1)} %collective-permute-done.10.refs_9_), channel_id=1, source_target_pairs={{0,112},{8,120},{16,0},{24,8},{32,16},{40,24},{48,32},{56,40},{64,... | collective-permute-start | bytes 731144 | tf_op jit(solution)/shard_map/ppermute | solution.py:188
  93.7 3.9 %collective-permute-start.16 = (bf16[136,896]{1,0:T(8,128)(2,1)S(1)}, bf16[136,896]{1,0:T(8,128)(2,1)}, u32[]{:S(2)}, u32[]{:S(2)}) collective-permute-start(bf16[136,896]{1,0:T(8,128)(2,1)S(1)} %collective-permute-done.15.refs_14_), channel_id=1, source_target_pairs={{0,112},{8,120},{16,0},{24,8},{32,16},{40,24},{48,32},{56,40},{64,... | collective-permute-start | bytes 731144 | tf_op jit(solution)/shard_map/ppermute | solution.py:188
  97.9 2.4 %collective-permute-done.14.refs_13_ = bf16[136,896]{1,0:T(8,128)(2,1)S(1)} collective-permute-done((bf16[136,896]{1,0:T(8,128)(2,1)S(1)}, bf16[136,896]{1,0:T(8,128)(2,1)S(1)}, u32[]{:S(2)}, u32[]{:S(2)}) %collective-permute-start.14) | collective-permute-done | bytes 243744 | tf_op jit(solution)/shard_map/ppermute | solution.py:184
  100.3 3.1 %collective-permute-done.16.refs_15_ = bf16[136,896]{1,0:T(8,128)(2,1)} collective-permute-done((bf16[136,896]{1,0:T(8,128)(2,1)S(1)}, bf16[136,896]{1,0:T(8,128)(2,1)}, u32[]{:S(2)}, u32[]{:S(2)}) %collective-permute-start.16) | collective-permute-done | bytes 243744 | tf_op jit(solution)/shard_map/ppermute | solution.py:188
  103.4 8.5 %shard_map.121 = (bf16[1024,1280]{1,0:T(8,128)(2,1)}, f32[8,1280]{1,0:T(8,128)S(1)}, f32[8,1280]{1,0:T(8,128)S(1)}) custom-call(s32[17]{0:T(128)S(1)} %stack.68.info, bf16[136,896]{1,0:T(8,128)(2,1)S(1)} %pad_maximum_fusion.1.refs_0_, bf16[136,896]{1,0:T(8,128)(2,1)S(1)} %collective-permute-done.4.refs_1_, ...), custom_call_target="tpu_custom_call" | custom-call | flops 2348810240 | bytes 16777216 | tf_op jit(solution)/shard_map/pallas_call | solution.py:214
  112.2 19.3 %psum.7 = f32[16,1,80]{2,0,1:T(8,128)} all-reduce(f32[16,1,80]{2,0,1:T(8,128)S(1)} %all_to_all.7), channel_id=1, replica_groups=mesh['section'=8,'expert'=16,'dp'=8] {'dp'}, use_global_device_ids=true, to_apply=%region_2.3 | all-reduce | flops 1280 | bytes 10240 | tf_op jit(solution)/shard_map/psum | solution.py:242
  131.5 6.4 %all-to-all-start = ((f32[16,1,80]{2,1,0:T(1,128)}), f32[16,1,80]{2,1,0:T(1,128)S(1)}, u32[]{:S(2)}, u32[]{:S(2)}) async-start(f32[16,1,80]{2,1,0:T(1,128)} %bitcast.36), calls=%async_computation.1 | async-start | bytes 16384 | tf_op jit(solution)/shard_map/all_to_all | solution.py:244
  137.9 12.3 %all-to-all-done = f32[16,1,80]{2,1,0:T(1,128)S(1)} async-done(((f32[16,1,80]{2,1,0:T(1,128)}), f32[16,1,80]{2,1,0:T(1,128)S(1)}, u32[]{:S(2)}, u32[]{:S(2)}) %all-to-all-start) | async-done | bytes 5152 | tf_op jit(solution)/shard_map/all_to_all | solution.py:244
  152.5 6.5 %reduce-scatter.2.cloned.1.call-done = bf16[128,1280]{1,0:T(8,128)(2,1)} async-done(((bf16[1024,1280]{1,0:T(8,128)(2,1)}), bf16[128,1280]{1,0:T(8,128)(2,1)}) %reduce-scatter.2.cloned.1.call-update) | async-done | bytes 327696 | tf_op jit(solution)/shard_map/reduce_scatter | solution.py:241
  (33 shorter events, 15.6 us)
Async XLA Ops:
  7.2 96.2 %all-gather.2.cloned.1.call-start = ((), (), s32[]{:S(2)}) async-start(), calls=%async_computation.2 | async-start | bytes 2949120 | tf_op jit(solution)/shard_map/all_gather | solution.py:174
  7.2 7.6 %collective-permute-start = (bf16[64,896]{1,0:T(8,128)(2,1)}, bf16[64,896]{1,0:T(8,128)(2,1)S(1)}, u32[]{:S(2)}, u32[]{:S(2)}) collective-permute-start(bf16[64,896]{1,0:T(8,128)(2,1)} %bitcast.59), channel_id=1, source_target_pairs={{0,896},{8,904},{16,912},{24,920},{32,928},{40,936},{48,944},{56,9... | collective-permute-start | bytes 344072 | tf_op jit(solution)/shard_map/ppermute | solution.py:159
  9.1 6.3 %collective-permute-start.1 = (bf16[64,896]{1,0:T(8,128)(2,1)}, bf16[64,896]{1,0:T(8,128)(2,1)S(1)}, u32[]{:S(2)}, u32[]{:S(2)}) collective-permute-start(bf16[64,896]{1,0:T(8,128)(2,1)} %bitcast.60), channel_id=1, source_target_pairs={{0,128},{8,136},{16,144},{24,152},{32,160},{40,168},{48,176},{56,1... | collective-permute-start | bytes 344072 | tf_op jit(solution)/shard_map/ppermute | solution.py:159
  16.2 142.8 %reduce-scatter.2.cloned.1.call-start = ((), (), s32[]{:S(2)}) async-start(), calls=%async_computation.3 | async-start | bytes 2949120 | tf_op jit(solution)/shard_map/reduce_scatter | solution.py:241
  16.3 25.1 %collective-permute-start.4 = (bf16[136,896]{1,0:T(8,128)(2,1)S(1)}, bf16[136,896]{1,0:T(8,128)(2,1)S(1)}, u32[]{:S(2)}, u32[]{:S(2)}) collective-permute-start(bf16[136,896]{1,0:T(8,128)(2,1)S(1)} %pad_maximum_fusion.1.refs_0_), channel_id=1, source_target_pairs={{0,8},{8,0},{16,24},{24,16},{32,40},{40,32},{48,56},{56,48},{64,72... | collective-permute-start | bytes 731144 | tf_op jit(solution)/shard_map/ppermute | solution.py:159
  22.1 23.4 %collective-permute-start.3 = (bf16[136,896]{1,0:T(8,128)(2,1)S(1)}, bf16[136,896]{1,0:T(8,128)(2,1)S(1)}, u32[]{:S(2)}, u32[]{:S(2)}) collective-permute-start(bf16[136,896]{1,0:T(8,128)(2,1)S(1)} %pad_maximum_fusion.1.refs_0_), channel_id=1, source_target_pairs={{0,112},{8,120},{16,0},{24,8},{32,16},{40,24},{48,32},{56,40},{64,... | collective-permute-start | bytes 731144 | tf_op jit(solution)/shard_map/ppermute | solution.py:188
  39.4 11.4 %collective-permute-start.2 = (bf16[136,896]{1,0:T(8,128)(2,1)S(1)}, bf16[136,896]{1,0:T(8,128)(2,1)S(1)}, u32[]{:S(2)}, u32[]{:S(2)}) collective-permute-start(bf16[136,896]{1,0:T(8,128)(2,1)S(1)} %pad_maximum_fusion.1.refs_0_), channel_id=1, source_target_pairs={{0,16},{8,24},{16,32},{24,40},{32,48},{40,56},{48,64},{56,72},{64,... | collective-permute-start | bytes 731144 | tf_op jit(solution)/shard_map/ppermute | solution.py:184
  50.8 9.5 %collective-permute-start.7 = (bf16[136,896]{1,0:T(8,128)(2,1)S(1)}, bf16[136,896]{1,0:T(8,128)(2,1)S(1)}, u32[]{:S(2)}, u32[]{:S(2)}) collective-permute-start(bf16[136,896]{1,0:T(8,128)(2,1)S(1)} %collective-permute-done.3.refs_3_), channel_id=1, source_target_pairs={{0,112},{8,120},{16,0},{24,8},{32,16},{40,24},{48,32},{56,40},{64,... | collective-permute-start | bytes 731144 | tf_op jit(solution)/shard_map/ppermute | solution.py:188
  54.5 12.8 %collective-permute-start.12 = (bf16[136,896]{1,0:T(8,128)(2,1)S(1)}, bf16[136,896]{1,0:T(8,128)(2,1)S(1)}, u32[]{:S(2)}, u32[]{:S(2)}) collective-permute-start(bf16[136,896]{1,0:T(8,128)(2,1)S(1)} %collective-permute-done.4.refs_1_), channel_id=1, source_target_pairs={{0,16},{8,24},{16,32},{24,40},{32,48},{40,56},{48,64},{56,72},{64,... | collective-permute-start | bytes 731144 | tf_op jit(solution)/shard_map/ppermute | solution.py:184
  60.4 14.7 %collective-permute-start.8 = (bf16[136,896]{1,0:T(8,128)(2,1)S(1)}, bf16[136,896]{1,0:T(8,128)(2,1)S(1)}, u32[]{:S(2)}, u32[]{:S(2)}) collective-permute-start(bf16[136,896]{1,0:T(8,128)(2,1)S(1)} %collective-permute-done.7.refs_6_), channel_id=1, source_target_pairs={{0,8},{8,0},{16,24},{24,16},{32,40},{40,32},{48,56},{56,48},{64,72... | collective-permute-start | bytes 731144 | tf_op jit(solution)/shard_map/ppermute | solution.py:159
  65.4 19.3 %collective-permute-start.6 = (bf16[136,896]{1,0:T(8,128)(2,1)S(1)}, bf16[136,896]{1,0:T(8,128)(2,1)S(1)}, u32[]{:S(2)}, u32[]{:S(2)}) collective-permute-start(bf16[136,896]{1,0:T(8,128)(2,1)S(1)} %collective-permute-done.2.refs_2_), channel_id=1, source_target_pairs={{0,16},{8,24},{16,32},{24,40},{32,48},{40,56},{48,64},{56,72},{64,... | collective-permute-start | bytes 731144 | tf_op jit(solution)/shard_map/ppermute | solution.py:184
  67.3 19.3 %collective-permute-start.13 = (bf16[136,896]{1,0:T(8,128)(2,1)S(1)}, bf16[136,896]{1,0:T(8,128)(2,1)S(1)}, u32[]{:S(2)}, u32[]{:S(2)}) collective-permute-start(bf16[136,896]{1,0:T(8,128)(2,1)S(1)} %collective-permute-done.12.refs_11_), channel_id=1, source_target_pairs={{0,16},{8,24},{16,32},{24,40},{32,48},{40,56},{48,64},{56,72},{64,... | collective-permute-start | bytes 731144 | tf_op jit(solution)/shard_map/ppermute | solution.py:184
  69.3 19.3 %collective-permute-start.10 = (bf16[136,896]{1,0:T(8,128)(2,1)S(1)}, bf16[136,896]{1,0:T(8,128)(2,1)S(1)}, u32[]{:S(2)}, u32[]{:S(2)}) collective-permute-start(bf16[136,896]{1,0:T(8,128)(2,1)S(1)} %collective-permute-done.7.refs_6_), channel_id=1, source_target_pairs={{0,112},{8,120},{16,0},{24,8},{32,16},{40,24},{48,32},{56,40},{64,... | collective-permute-start | bytes 731144 | tf_op jit(solution)/shard_map/ppermute | solution.py:188
  75.1 18.6 %collective-permute-start.15 = (bf16[136,896]{1,0:T(8,128)(2,1)S(1)}, bf16[136,896]{1,0:T(8,128)(2,1)S(1)}, u32[]{:S(2)}, u32[]{:S(2)}) collective-permute-start(bf16[136,896]{1,0:T(8,128)(2,1)S(1)} %collective-permute-done.8.refs_7_), channel_id=1, source_target_pairs={{0,112},{8,120},{16,0},{24,8},{32,16},{40,24},{48,32},{56,40},{64,... | collective-permute-start | bytes 731144 | tf_op jit(solution)/shard_map/ppermute | solution.py:188
  78.4 19.5 %collective-permute-start.5 = (bf16[136,896]{1,0:T(8,128)(2,1)S(1)}, bf16[136,896]{1,0:T(8,128)(2,1)S(1)}, u32[]{:S(2)}, u32[]{:S(2)}) collective-permute-start(bf16[136,896]{1,0:T(8,128)(2,1)S(1)} %collective-permute-done.3.refs_3_), channel_id=1, source_target_pairs={{0,8},{8,0},{16,24},{24,16},{32,40},{40,32},{48,56},{56,48},{64,72... | collective-permute-start | bytes 731144 | tf_op jit(solution)/shard_map/ppermute | solution.py:159
  84.7 13.2 %collective-permute-start.9 = (bf16[136,896]{1,0:T(8,128)(2,1)S(1)}, bf16[136,896]{1,0:T(8,128)(2,1)S(1)}, u32[]{:S(2)}, u32[]{:S(2)}) collective-permute-start(bf16[136,896]{1,0:T(8,128)(2,1)S(1)} %collective-permute-done.6.refs_5_), channel_id=1, source_target_pairs={{0,16},{8,24},{16,32},{24,40},{32,48},{40,56},{48,64},{56,72},{64,... | collective-permute-start | bytes 731144 | tf_op jit(solution)/shard_map/ppermute | solution.py:184
  86.6 13.7 %collective-permute-start.14 = (bf16[136,896]{1,0:T(8,128)(2,1)S(1)}, bf16[136,896]{1,0:T(8,128)(2,1)S(1)}, u32[]{:S(2)}, u32[]{:S(2)}) collective-permute-start(bf16[136,896]{1,0:T(8,128)(2,1)S(1)} %collective-permute-done.13.refs_12_), channel_id=1, source_target_pairs={{0,16},{8,24},{16,32},{24,40},{32,48},{40,56},{48,64},{56,72},{64,... | collective-permute-start | bytes 731144 | tf_op jit(solution)/shard_map/ppermute | solution.py:184
  88.5 11.7 %collective-permute-start.11 = (bf16[136,896]{1,0:T(8,128)(2,1)S(1)}, bf16[136,896]{1,0:T(8,128)(2,1)}, u32[]{:S(2)}, u32[]{:S(2)}) collective-permute-start(bf16[136,896]{1,0:T(8,128)(2,1)S(1)} %collective-permute-done.10.refs_9_), channel_id=1, source_target_pairs={{0,112},{8,120},{16,0},{24,8},{32,16},{40,24},{48,32},{56,40},{64,... | collective-permute-start | bytes 731144 | tf_op jit(solution)/shard_map/ppermute | solution.py:188
  93.7 9.7 %collective-permute-start.16 = (bf16[136,896]{1,0:T(8,128)(2,1)S(1)}, bf16[136,896]{1,0:T(8,128)(2,1)}, u32[]{:S(2)}, u32[]{:S(2)}) collective-permute-start(bf16[136,896]{1,0:T(8,128)(2,1)S(1)} %collective-permute-done.15.refs_14_), channel_id=1, source_target_pairs={{0,112},{8,120},{16,0},{24,8},{32,16},{40,24},{48,32},{56,40},{64,... | collective-permute-start | bytes 731144 | tf_op jit(solution)/shard_map/ppermute | solution.py:188
  131.5 18.8 %all-to-all-start = ((f32[16,1,80]{2,1,0:T(1,128)}), f32[16,1,80]{2,1,0:T(1,128)S(1)}, u32[]{:S(2)}, u32[]{:S(2)}) async-start(f32[16,1,80]{2,1,0:T(1,128)} %bitcast.36), calls=%async_computation.1 | async-start | bytes 16384 | tf_op jit(solution)/shard_map/all_to_all | solution.py:244
  150.2 0.6 copy-start
Sparse Core Ops, SparseCore 0:
  16.3 60.6 all-gather.1
  112.1 46.9 reduce-scatter.1
